TPU v7x, 128 devices: a whole 4x4x4 slice. The times are simulated.
128 devices in a mesh: tm: 8 (over x, core), chan: 16 (over z, y).
Axes of the slice: x: 4, y: 4, z: 4, core: 2. Of those that a mesh axis runs over, the one named last changes fastest.
Arguments:
- raw_data: float32 [1024, 5120], P('chan', 'tm'), may hold values from -400 to 400
- whiten_taps: float32 [1024, 16], P('chan'), may hold values from -0.6 to 0.6
- band_taps: bfloat16 [113], replicated, may hold values from -0.5 to 0.5
- templates: bfloat16 [512, 512], P('tm'), may hold values from -5 to 5
- channel_mask: int32 [512, 1024], P('tm', 'chan'), may hold values 0 or 1
- moveouts: int32 [1024], P('chan'), may hold values from 0 to 511, as said below
Outputs:
- stacked: float32 [4096, 512], P('chan', 'tm')
Inputs may be any that keep to these rules, and one draw needn't show every extreme that they name: `moveouts`: a channel's moveout; 0 on some channel and 511 on some channel.
All inputs are finite; a program needn't handle non-finite values. No bound on the sum of `channel_mask` on one device may be relied on, other than what follows from the above.
Results may differ from a plain program's by a relative error of at most 0.0041.
Values may be sent and summed in bfloat16 or wider, within the bound.
No kernel may reach another device: no remote copies, remote signals or barrier semaphores. Data moves between devices by JAX's collectives and lax.ppermute only.
A program may use at most 128 MiB of HBM per device.

v0:
```python
import math

import jax
import jax.numpy as jnp
from jax import lax
from jax.sharding import PartitionSpec as P

SPAN = 512
OUT_DEV = 256


EPSILON = 1e-06


def shifted(value, axis, steps):
    count = lax.axis_size(axis)
    initial, last = (max(0, -steps), min(count, count - steps))
    return lax.ppermute(value, axis, [(source, source + steps) for source in range(initial, last)])


def band_matrix(band_taps, block_time):
    tap_count = band_taps.shape[0]
    source = jnp.arange(block_time + tap_count - 1, dtype=jnp.int32)[:, None]
    target = jnp.arange(block_time, dtype=jnp.int32)[None, :]
    offset = target - source + (tap_count - 1)
    matrix = jnp.zeros((block_time + tap_count - 1, block_time), band_taps.dtype)
    for tap_index in range(tap_count):
        matrix = jnp.where(offset == tap_index, band_taps[tap_index], matrix)
    return matrix


def filter_block(extended, coeffs, matrix):
    tap_count = coeffs.shape[1]
    span_len = extended.shape[-1] - tap_count
    expand = (coeffs.shape[0],) + (1,) * (extended.ndim - 1)
    whitened = extended[..., tap_count:]
    for lag_step in range(1, tap_count + 1):
        earlier_cut = extended[..., tap_count - lag_step : tap_count - lag_step + span_len]
        whitened = whitened - coeffs[:, lag_step - 1].reshape(expand) * earlier_cut
    whitened = whitened.astype(jnp.bfloat16)
    passed = jnp.einsum("...r,rt->...t", whitened, matrix, preferred_element_type=jnp.float32)
    return passed.astype(jnp.bfloat16)


def shift_traces(traces, moveouts, aligned_len):
    channels = traces.shape[0]
    current = traces
    for bit_index in range(max(SPAN - 1, 1).bit_length()):
        step_len = 1 << bit_index
        moved = jnp.concatenate(
            [current[:, step_len:], jnp.zeros((channels, step_len), current.dtype)], axis=1
        )
        chosen = jnp.bitwise_and(jnp.right_shift(moveouts, bit_index), 1) == 1
        current = jnp.where(chosen[:, None], moved, current)
    return current[:, :aligned_len]


def inverse_energy(aligned, tmpl_len, block_len):
    squares = jnp.square(aligned.astype(jnp.float32))
    channels, full_len = squares.shape
    blocks = squares.reshape(channels, full_len // block_len, block_len)
    block_sums = jnp.sum(blocks, axis=2)
    upper = (jnp.arange(block_len)[:, None] < jnp.arange(block_len)[None, :]).astype(jnp.float32)
    prefix = jnp.einsum("cnb,bj->cnj", blocks, upper, precision=lax.Precision.HIGHEST)
    lag_blocks = full_len // block_len - tmpl_len // block_len
    energy = prefix[:, tmpl_len // block_len :] - prefix[:, :lag_blocks]
    for offset in range(tmpl_len // block_len):
        energy = energy + block_sums[:, offset : offset + lag_blocks, None]
    inverse = lax.rsqrt(energy / tmpl_len + EPSILON)
    return inverse.reshape(channels, lag_blocks * block_len)


def template_matrix(templates, block_len):
    tmpl_count, tmpl_len = templates.shape
    zero_rows = jnp.zeros((block_len, tmpl_count), templates.dtype)
    padded = jnp.concatenate([zero_rows, templates.T, zero_rows], axis=0)
    columns = [
        padded[block_len - target : block_len - target + tmpl_len + block_len]
        for target in range(block_len)
    ]
    toeplitz = jnp.stack(columns, axis=1)
    return toeplitz.reshape(tmpl_len + block_len, block_len * tmpl_count)


def stack_rows(
    aligned, data_scale, mask_float, toeplitz, template_scale, block_len, tmpl_len, row_count
):
    channels = aligned.shape[0]
    tmpl_count = template_scale.shape[0]
    group_size = channels // math.gcd(channels, 8)
    lag_blocks = row_count // block_len
    segment = lax.slice_in_dim(aligned, 0, row_count + tmpl_len, axis=1)
    pieces = segment.reshape(channels, lag_blocks + tmpl_len // block_len, block_len)
    windows = jnp.concatenate(
        [pieces[:, offset : offset + lag_blocks] for offset in range(tmpl_len // block_len + 1)],
        axis=2,
    )
    scales = lax.slice_in_dim(data_scale, 0, row_count, axis=1).reshape(
        channels, lag_blocks, block_len, 1
    )

    def add_group(group_index, running):
        first_row = group_index * group_size
        group_rows = lax.dynamic_slice_in_dim(windows, first_row, group_size, 0)
        products = jnp.einsum(
            "gps,sq->gpq", group_rows, toeplitz, preferred_element_type=jnp.float32
        )
        products = products.reshape(group_size, lag_blocks, block_len, tmpl_count)
        group_mask = lax.dynamic_slice_in_dim(mask_float, first_row, group_size, 0)
        factor = (
            lax.dynamic_slice_in_dim(scales, first_row, group_size, 0)
            * group_mask[:, None, None, :]
        )
        return running + jnp.sum(products * factor, axis=0)

    running = lax.fori_loop(
        0,
        channels // group_size,
        add_group,
        jnp.zeros((lag_blocks, block_len, tmpl_count), jnp.float32),
    )
    return running.reshape(row_count, tmpl_count) * template_scale[None, :]


def shards(raw_data, whiten_taps, band_taps, templates, channel_mask, moveouts):
    chan_ways = lax.axis_size("chan")
    channels, block_time = raw_data.shape
    halo_len = whiten_taps.shape[1] + band_taps.shape[0] - 1
    tmpl_count, tmpl_len = templates.shape
    out_rows = OUT_DEV
    lag_total = out_rows * chan_ways
    matrix = band_matrix(band_taps, block_time)
    earlier = shifted(raw_data[:, block_time - halo_len :], "tm", 1)
    filtered = filter_block(jnp.concatenate([earlier, raw_data], axis=1), whiten_taps, matrix)
    traces = lax.all_gather(filtered, "tm", axis=1, tiled=True)
    aligned_len = lag_total + tmpl_len
    aligned = shift_traces(traces, moveouts, aligned_len)
    block_len = math.gcd(math.gcd(tmpl_len, out_rows), 64)
    tmpl_float = templates.astype(jnp.float32)
    template_scale = 1.0 / (
        tmpl_len * jnp.sqrt(jnp.mean(tmpl_float * tmpl_float, axis=1) + EPSILON)
    )
    toeplitz = template_matrix(templates, block_len)
    data_scale = inverse_energy(aligned, tmpl_len, block_len)
    mask_float = channel_mask.T.astype(jnp.float32)
    return lax.psum_scatter(
        stack_rows(
            aligned,
            data_scale,
            mask_float,
            toeplitz,
            template_scale,
            block_len,
            tmpl_len,
            out_rows * lax.axis_size("chan"),
        ),
        "chan",
        scatter_dimension=0,
        tiled=True,
    )


def solution(mesh):
    in_specs = (P("chan", "tm"), P("chan", None), P(), P("tm", None), P("tm", "chan"), P("chan"))
    out_specs = P("chan", "tm")
    return jax.shard_map(shards, mesh=mesh, in_specs=in_specs, out_specs=out_specs, check_vma=False)
```

profile of v0, /device:TPU:0, one launch (start us, length us, event | category | flops | bytes accessed | tf_op | source)
XLA Modules:
  0.0 548.1 jit_solution(3293527875311218050)
XLA Ops:
  8.6 2.1 fusion.607
  10.7 2.1 fusion.606
  12.8 2.1 fusion.608
  14.8 2.1 fusion.609
  16.9 2.1 fusion.610
  28.3 2.3 copy-done.2
  32.7 7.7 %copy.14 = bf16[576,4096]{1,0:T(8,128)(2,1)} copy(bf16[576,4096]{0,1:T(8,128)(2,1)} %bitcast.422) | data formatting | bytes 9437184
  40.4 76.2 %convolution_convert_fusion = bf16[64,640]{1,0:T(8,128)(2,1)S(1)} fusion(bf16[]{:T(256)} %bitcast.128, bf16[]{:T(256)} %bitcast.127, bf16[]{:T(256)} %bitcast.126, bf16[]{:T(256)} %bitcast.125, bf16[]{:T(256)} %bitcast.124, bf16[]{:T(256)} %bitcast.123, bf16[]{:T(256)} %bitcast.122, bf16[]{:T(256)} %bitcast.121, bf16[]{:T(256)} %bitcast.120, ...), kind=kOutput, calls=%fused_computation.248 | convolution fusion | flops 172964864 | bytes 3432674 | tf_op jit(solution)/shard_map/...r,rt->...t/dot_general | solution.py:41
  116.6 14.8 %all_gather.3 = bf16[64,5120]{1,0:T(8,128)(2,1)S(1)} all-gather(bf16[64,640]{1,0:T(8,128)(2,1)S(1)} %convolution_convert_fusion), channel_id=1, replica_groups=mesh['tm'=8,'chan'=16] {'tm'}, dimensions={1}, use_global_device_ids=true | all-gather | bytes 737280 | tf_op jit(solution)/shard_map/all_gather | solution.py:135
  136.6 4.6 fusion.488
  143.2 3.9 fusion.604
  147.1 2.6 fusion.14
  149.7 11.5 %concatenate.49 = bf16[64,64,576]{2,1,0:T(8,128)(2,1)} concatenate(bf16[64,64,64]{2,1,0:T(8,128)(2,1)} %get-tuple-element.170, bf16[64,64,64]{2,1,0:T(8,128)(2,1)} %get-tuple-element.169, bf16[64,64,64]{2,1,0:T(8,128)(2,1)} %get-tuple-element.168, bf16[64,64,64]{2,1,0:T(8,128)(2,1)} %get-tuple-element.167, bf16[64,64,64]{2,1,0:T(8,128)(2,1)} %get-tuple-element.166, ...), dimensions={2} | concatenate | bytes 9437184 | tf_op jit(solution)/shard_map/concatenate | solution.py:94
  161.2 301.9 %while.14 = (s32[]{:T(128)}, f32[64,64,64]{2,1,0:T(8,128)}, bf16[64,64,576]{2,1,0:T(8,128)(2,1)}, bf16[576,4096]{1,0:T(8,128)(2,1)}, f32[64,64,64,1]{1,2,0,3:T(8...) while((s32[]{:T(128)}, f32[64,64,64]{2,1,0:T(8,128)}, ...), condition=%wide.region_3.4_spmd.clone, body=%wide.region_1.3_spmd.clone.sunk | while | flops 2422472704 | bytes 46405800 | solution.py:116
  162.3 8.4 %mul.441 = f32[8,64,64,64]{3,2,1,0:T(8,128)} broadcast(f32[8,64,64]{2,1,0:T(8,128)S(1)} %bitcast.421), dimensions={0,1,2} | broadcast | bytes 8519680 | tf_op jit(solution)/shard_map/while/body/eval_jaxpr/mul | solution.py:111
  170.7 14.7 %mul.442 = f32[8,64,4096]{2,1,0:T(8,128)} reshape(f32[8,64,64,64]{3,2,1,0:T(8,128)} %mul.441) | data formatting | bytes 16777216 | tf_op jit(solution)/shard_map/while/body/eval_jaxpr/mul | solution.py:111
  186.3 8.6 %multiply_reduce_fusion.3 = f32[64,4096]{1,0:T(8,128)S(1)} fusion(f32[8,64,4096]{2,1,0:T(8,128)} %mul.442, bf16[576,4096]{1,0:T(8,128)(2,1)} %get-tuple-element.377, f32[8,4096]{1,0:T(8,128)S(1)} %mul.444, bf16[64,64,576]{2,1,0:T(8,128)(2,1)} %get-tuple-element.376, s32[]{:T(128)S(6)} %select_n.13393), kind=kOutput, calls=%fused_computation.clone.1 | convolution fusion | flops 2421948416 | bytes 14942212 | tf_op jit(solution)/shard_map/while/body/eval_jaxpr/gps,sq->gpq/dot_general | solution.py:105
  195.7 1.8 select_add_fusion.2
  198.6 8.4 %mul.441 = f32[8,64,64,64]{3,2,1,0:T(8,128)} broadcast(f32[8,64,64]{2,1,0:T(8,128)S(1)} %bitcast.421), dimensions={0,1,2} | broadcast | bytes 8519680 | tf_op jit(solution)/shard_map/while/body/eval_jaxpr/mul | solution.py:111
  207.0 14.7 %mul.442 = f32[8,64,4096]{2,1,0:T(8,128)} reshape(f32[8,64,64,64]{3,2,1,0:T(8,128)} %mul.441) | data formatting | bytes 16777216 | tf_op jit(solution)/shard_map/while/body/eval_jaxpr/mul | solution.py:111
  222.6 8.6 %multiply_reduce_fusion.3 = f32[64,4096]{1,0:T(8,128)S(1)} fusion(f32[8,64,4096]{2,1,0:T(8,128)} %mul.442, bf16[576,4096]{1,0:T(8,128)(2,1)} %get-tuple-element.377, f32[8,4096]{1,0:T(8,128)S(1)} %mul.444, bf16[64,64,576]{2,1,0:T(8,128)(2,1)} %get-tuple-element.376, s32[]{:T(128)S(6)} %select_n.13393), kind=kOutput, calls=%fused_computation.clone.1 | convolution fusion | flops 2421948416 | bytes 14942212 | tf_op jit(solution)/shard_map/while/body/eval_jaxpr/gps,sq->gpq/dot_general | solution.py:105
  232.1 3.4 select_add_fusion.2
  236.6 8.4 %mul.441 = f32[8,64,64,64]{3,2,1,0:T(8,128)} broadcast(f32[8,64,64]{2,1,0:T(8,128)S(1)} %bitcast.421), dimensions={0,1,2} | broadcast | bytes 8519680 | tf_op jit(solution)/shard_map/while/body/eval_jaxpr/mul | solution.py:111
  245.0 14.7 %mul.442 = f32[8,64,4096]{2,1,0:T(8,128)} reshape(f32[8,64,64,64]{3,2,1,0:T(8,128)} %mul.441) | data formatting | bytes 16777216 | tf_op jit(solution)/shard_map/while/body/eval_jaxpr/mul | solution.py:111
  260.6 8.6 %multiply_reduce_fusion.3 = f32[64,4096]{1,0:T(8,128)S(1)} fusion(f32[8,64,4096]{2,1,0:T(8,128)} %mul.442, bf16[576,4096]{1,0:T(8,128)(2,1)} %get-tuple-element.377, f32[8,4096]{1,0:T(8,128)S(1)} %mul.444, bf16[64,64,576]{2,1,0:T(8,128)(2,1)} %get-tuple-element.376, s32[]{:T(128)S(6)} %select_n.13393), kind=kOutput, calls=%fused_computation.clone.1 | convolution fusion | flops 2421948416 | bytes 14942212 | tf_op jit(solution)/shard_map/while/body/eval_jaxpr/gps,sq->gpq/dot_general | solution.py:105
  270.0 3.4 select_add_fusion.2
  274.5 8.4 %mul.441 = f32[8,64,64,64]{3,2,1,0:T(8,128)} broadcast(f32[8,64,64]{2,1,0:T(8,128)S(1)} %bitcast.421), dimensions={0,1,2} | broadcast | bytes 8519680 | tf_op jit(solution)/shard_map/while/body/eval_jaxpr/mul | solution.py:111
  282.9 14.7 %mul.442 = f32[8,64,4096]{2,1,0:T(8,128)} reshape(f32[8,64,64,64]{3,2,1,0:T(8,128)} %mul.441) | data formatting | bytes 16777216 | tf_op jit(solution)/shard_map/while/body/eval_jaxpr/mul | solution.py:111
  298.5 8.6 %multiply_reduce_fusion.3 = f32[64,4096]{1,0:T(8,128)S(1)} fusion(f32[8,64,4096]{2,1,0:T(8,128)} %mul.442, bf16[576,4096]{1,0:T(8,128)(2,1)} %get-tuple-element.377, f32[8,4096]{1,0:T(8,128)S(1)} %mul.444, bf16[64,64,576]{2,1,0:T(8,128)(2,1)} %get-tuple-element.376, s32[]{:T(128)S(6)} %select_n.13393), kind=kOutput, calls=%fused_computation.clone.1 | convolution fusion | flops 2421948416 | bytes 14942212 | tf_op jit(solution)/shard_map/while/body/eval_jaxpr/gps,sq->gpq/dot_general | solution.py:105
  308.0 3.4 select_add_fusion.2
  312.4 8.4 %mul.441 = f32[8,64,64,64]{3,2,1,0:T(8,128)} broadcast(f32[8,64,64]{2,1,0:T(8,128)S(1)} %bitcast.421), dimensions={0,1,2} | broadcast | bytes 8519680 | tf_op jit(solution)/shard_map/while/body/eval_jaxpr/mul | solution.py:111
  320.8 14.7 %mul.442 = f32[8,64,4096]{2,1,0:T(8,128)} reshape(f32[8,64,64,64]{3,2,1,0:T(8,128)} %mul.441) | data formatting | bytes 16777216 | tf_op jit(solution)/shard_map/while/body/eval_jaxpr/mul | solution.py:111
  336.4 8.6 %multiply_reduce_fusion.3 = f32[64,4096]{1,0:T(8,128)S(1)} fusion(f32[8,64,4096]{2,1,0:T(8,128)} %mul.442, bf16[576,4096]{1,0:T(8,128)(2,1)} %get-tuple-element.377, f32[8,4096]{1,0:T(8,128)S(1)} %mul.444, bf16[64,64,576]{2,1,0:T(8,128)(2,1)} %get-tuple-element.376, s32[]{:T(128)S(6)} %select_n.13393), kind=kOutput, calls=%fused_computation.clone.1 | convolution fusion | flops 2421948416 | bytes 14942212 | tf_op jit(solution)/shard_map/while/body/eval_jaxpr/gps,sq->gpq/dot_general | solution.py:105
  345.9 3.4 select_add_fusion.2
  350.4 8.4 %mul.441 = f32[8,64,64,64]{3,2,1,0:T(8,128)} broadcast(f32[8,64,64]{2,1,0:T(8,128)S(1)} %bitcast.421), dimensions={0,1,2} | broadcast | bytes 8519680 | tf_op jit(solution)/shard_map/while/body/eval_jaxpr/mul | solution.py:111
  358.8 14.7 %mul.442 = f32[8,64,4096]{2,1,0:T(8,128)} reshape(f32[8,64,64,64]{3,2,1,0:T(8,128)} %mul.441) | data formatting | bytes 16777216 | tf_op jit(solution)/shard_map/while/body/eval_jaxpr/mul | solution.py:111
  374.4 8.6 %multiply_reduce_fusion.3 = f32[64,4096]{1,0:T(8,128)S(1)} fusion(f32[8,64,4096]{2,1,0:T(8,128)} %mul.442, bf16[576,4096]{1,0:T(8,128)(2,1)} %get-tuple-element.377, f32[8,4096]{1,0:T(8,128)S(1)} %mul.444, bf16[64,64,576]{2,1,0:T(8,128)(2,1)} %get-tuple-element.376, s32[]{:T(128)S(6)} %select_n.13393), kind=kOutput, calls=%fused_computation.clone.1 | convolution fusion | flops 2421948416 | bytes 14942212 | tf_op jit(solution)/shard_map/while/body/eval_jaxpr/gps,sq->gpq/dot_general | solution.py:105
  383.8 3.4 select_add_fusion.2
  388.3 8.4 %mul.441 = f32[8,64,64,64]{3,2,1,0:T(8,128)} broadcast(f32[8,64,64]{2,1,0:T(8,128)S(1)} %bitcast.421), dimensions={0,1,2} | broadcast | bytes 8519680 | tf_op jit(solution)/shard_map/while/body/eval_jaxpr/mul | solution.py:111
  396.7 14.7 %mul.442 = f32[8,64,4096]{2,1,0:T(8,128)} reshape(f32[8,64,64,64]{3,2,1,0:T(8,128)} %mul.441) | data formatting | bytes 16777216 | tf_op jit(solution)/shard_map/while/body/eval_jaxpr/mul | solution.py:111
  412.3 8.6 %multiply_reduce_fusion.3 = f32[64,4096]{1,0:T(8,128)S(1)} fusion(f32[8,64,4096]{2,1,0:T(8,128)} %mul.442, bf16[576,4096]{1,0:T(8,128)(2,1)} %get-tuple-element.377, f32[8,4096]{1,0:T(8,128)S(1)} %mul.444, bf16[64,64,576]{2,1,0:T(8,128)(2,1)} %get-tuple-element.376, s32[]{:T(128)S(6)} %select_n.13393), kind=kOutput, calls=%fused_computation.clone.1 | convolution fusion | flops 2421948416 | bytes 14942212 | tf_op jit(solution)/shard_map/while/body/eval_jaxpr/gps,sq->gpq/dot_general | solution.py:105
  421.7 3.4 select_add_fusion.2
  426.2 8.4 %mul.441 = f32[8,64,64,64]{3,2,1,0:T(8,128)} broadcast(f32[8,64,64]{2,1,0:T(8,128)S(1)} %bitcast.421), dimensions={0,1,2} | broadcast | bytes 8519680 | tf_op jit(solution)/shard_map/while/body/eval_jaxpr/mul | solution.py:111
  434.6 14.7 %mul.442 = f32[8,64,4096]{2,1,0:T(8,128)} reshape(f32[8,64,64,64]{3,2,1,0:T(8,128)} %mul.441) | data formatting | bytes 16777216 | tf_op jit(solution)/shard_map/while/body/eval_jaxpr/mul | solution.py:111
  450.2 8.6 %multiply_reduce_fusion.3 = f32[64,4096]{1,0:T(8,128)S(1)} fusion(f32[8,64,4096]{2,1,0:T(8,128)} %mul.442, bf16[576,4096]{1,0:T(8,128)(2,1)} %get-tuple-element.377, f32[8,4096]{1,0:T(8,128)S(1)} %mul.444, bf16[64,64,576]{2,1,0:T(8,128)(2,1)} %get-tuple-element.376, s32[]{:T(128)S(6)} %select_n.13393), kind=kOutput, calls=%fused_computation.clone.1 | convolution fusion | flops 2421948416 | bytes 14942212 | tf_op jit(solution)/shard_map/while/body/eval_jaxpr/gps,sq->gpq/dot_general | solution.py:105
  459.7 3.4 select_add_fusion.2
  463.0 2.2 copy.18
  466.4 74.8 %reduce-scatter.2.cloned.1.call-done = f32[256,64]{0,1:T(8,128)} async-done(((f32[4096,64]{0,1:T(8,128)}), f32[256,64]{0,1:T(8,128)}) %reduce-scatter.2.cloned.1.call-update) | async-done | bytes 65552 | tf_op jit(solution)/shard_map/reduce_scatter | solution.py:146
  (171 shorter events, 43.1 us)
Async XLA Ops:
  6.5 534.7 %reduce-scatter.2.cloned.1.call-start = ((), (), s32[]{:S(2)}) async-start(), calls=%async_computation.1 | async-start | bytes 1114112 | tf_op jit(solution)/shard_map/reduce_scatter | solution.py:146
  7.3 33.1 %collective-permute-start = (f32[64,128]{1,0:T(8,128)S(1)}, f32[64,128]{1,0:T(8,128)S(1)}, u32[]{:S(2)}, u32[]{:S(2)}) collective-permute-start(f32[64,128]{1,0:T(8,128)S(1)} %slice.719), channel_id=1, source_target_pairs={{0,16},{16,32},{32,48},{48,64},{64,80},{80,96},{96,112},{1,17},{17... | collective-permute-start | bytes 98312 | tf_op jit(solution)/shard_map/ppermute | solution.py:18
  20.8 9.8 %copy-start.7 = (f32[64,16]{0,1:T(8,128)S(1)}, f32[64,16]{0,1:T(8,128)}, u32[]{:S(2)}) copy-start(f32[64,16]{0,1:T(8,128)} %param.9) | copy-start | bytes 12292
  20.8 9.8 %copy-start.9 = (s32[64]{0:T(128)S(1)}, s32[64]{0:T(128)}, u32[]{:S(2)}) copy-start(s32[64]{0:T(128)} %param.13) | copy-start | bytes 772
  20.8 9.8 %copy-start.6 = (s32[64,64]{1,0:T(8,128)S(1)}, s32[64,64]{1,0:T(8,128)}, u32[]{:S(2)}) copy-start(s32[64,64]{1,0:T(8,128)} %param.12) | copy-start | bytes 49156
  21.8 10.1 %copy-start.1 = (bf16[113]{0:T(256)(128)(2,1)S(1)}, bf16[113]{0:T(256)(128)(2,1)}, u32[]{:S(2)}) copy-start(bf16[113]{0:T(256)(128)(2,1)} %param.10) | copy-start | bytes 682
  28.1 12.3 %copy-start.5 = (f32[64,640]{1,0:T(8,128)S(1)}, f32[64,640]{1,0:T(8,128)}, u32[]{:S(2)}) copy-start(f32[64,640]{1,0:T(8,128)} %param.8) | copy-start | bytes 491524
  28.3 2.3 copy-start.2
  136.6 5.9 %copy-start.4 = (bf16[64,4608]{1,0:T(8,128)(2,1)S(1)}, bf16[64,4608]{1,0:T(8,128)(2,1)}, u32[]{:S(2)}) copy-start(bf16[64,4608]{1,0:T(8,128)(2,1)} %get-tuple-element.161) | copy-start | bytes 1769476
  143.2 4.0 copy-start
  147.1 2.6 copy-start.3
  161.2 304.1 %copy-start.8 = (f32[64]{0:T(128)S(1)}, f32[64]{0:T(128)}, u32[]{:S(2)}) copy-start(f32[64]{0:T(128)} %multiply_divide_fusion) | copy-start | bytes 772
Sparse Core Ops, SparseCore 0:
  466.5 74.6 reduce-scatter.1
where the time goes:
time: 553 us; the launch traced here: 548 us
  local copies, waits for them, and re-layouts  257 us (46%)
  matrix products  150 us (27%)
  waiting for transfers between devices  74.9 us (14%)
  other arithmetic  36.1 us (7%)
  blocking collectives  14.8 us (3%)
  between operations  14.2 us (3%)
    mul x32, local copies, waits for them, and re-layouts, add_group(): lax.dynamic_slice_in_dim(scales, first_row, group_size, 0)  186 us
    dot_general x1, matrix products, filter_block(): jnp.einsum('...r,rt->...t', whitened, matrix, preferred_element_type=jnp....  76.2 us
    reduce_scatter x1, waiting for transfers between devices, shards(): lax.psum_scatter(stack_rows(aligned, data_scale, mask_float, toeplitz, te...  74.8 us
    dot_general x8, matrix products, add_group(): jnp.einsum('gps,sq->gpq', group_rows, toeplitz, preferred_element_type=jn...  68.9 us
    add x8, other arithmetic, add_group(): return running + jnp.sum(products * factor, axis=0)  25.3 us
    unnamed x86, local copies, waits for them, and re-layouts  16.8 us
    all_gather x1, blocking collectives, shards(): traces = lax.all_gather(filtered, 'tm', axis=1, tiled=True)  14.8 us
    concatenate x1, local copies, waits for them, and re-layouts, stack_rows(): jnp.concatenate([pieces[:, offset:offset + lag_blocks] for offset in rang...  11.5 us
  transfers between devices with their start and end apart: 2, of which 1 were waited for; matrix products, arithmetic and copies ran while one was open for 5% of the time, Pallas kernels for 0%

commit v1 on v0

v1 whole, which is shorter than its diff:
```python
import functools

import jax
import jax.numpy as jnp
from jax import lax
from jax.experimental import pallas as pl
from jax.experimental.pallas import tpu as pltpu
from jax.sharding import PartitionSpec as P

EPSILON = 1e-06
PH = 8
HALO = 128
VMEM = pl.BlockSpec(memory_space=pltpu.VMEM)
SMEM = pl.BlockSpec(memory_space=pltpu.SMEM)
BF = jnp.bfloat16
F32 = jnp.float32


def lane_iota(shape):
    return lax.broadcasted_iota(jnp.int32, shape, len(shape) - 1)


def row_iota(shape):
    return lax.broadcasted_iota(jnp.int32, shape, 0)


def whiten_kernel(raw_ref, halo_ref, taps_ref, out_ref):
    ext = jnp.concatenate([halo_ref[...], raw_ref[...]], axis=1)
    acc = raw_ref[...]
    for m in range(1, taps_ref.shape[1] + 1):
        acc = acc - taps_ref[:, m - 1 : m] * pltpu.roll(ext, m, 1)[:, HALO:]
    out_ref[...] = acc.astype(BF)


def shift_left(pieces, amount, lane):
    moved = [pltpu.roll(p, jnp.where(amount == 0, 0, 128 - amount), 1) for p in pieces]
    keep = lane < 128 - amount
    return [
        jnp.where(keep, moved[i], moved[(i + 1) % len(pieces)]) for i in range(len(pieces))
    ]


def shift_static(pieces, amount, lane):
    if amount == 0:
        return pieces
    moved = [pltpu.roll(p, 128 - amount, 1) for p in pieces]
    keep = lane < 128 - amount
    return [
        jnp.where(keep, moved[i], moved[(i + 1) % len(pieces)]) for i in range(len(pieces))
    ]


def band_setup(band_ref, b_ref):
    x = lane_iota((8, 128))
    s = row_iota((8, 128))
    residue = jnp.bitwise_and(8 - s, 7)
    band = jnp.broadcast_to(band_ref[...].astype(F32), (8, 128))
    left = jnp.where(jnp.bitwise_and(x, 7) == residue, band, 0.0).astype(BF)
    rx = row_iota((128, 128))
    rn = lane_iota((128, 128))
    right = (jnp.right_shift(rx + 16, 3) == rn).astype(F32).astype(BF)
    table = jnp.dot(left, right, preferred_element_type=F32)
    lane16 = lane_iota((16, 128))
    for v in range(PH):
        z = pltpu.roll(table, v, 0) if v else table
        z0 = pltpu.roll(z, 126, 1)
        z1 = pltpu.roll(z, 127, 1)
        upper = s <= v
        g = jnp.concatenate([jnp.where(upper, z0, z1), jnp.where(upper, z1, z)], axis=0)
        for pair in range(72):
            at = 2 * pair - 16
            turned = pltpu.roll(g, at % 128, 1) if at else g
            inside = (lane16 >= at) & (lane16 < at + 16)
            b_ref[16 * pair : 16 * pair + 16, 128 * v : 128 * v + 128] = jnp.where(
                inside, turned, 0.0
            ).astype(BF)


def stack_kernel(
    moveouts_ref, w_ref_in, band_ref, tmpl_ref, mask_ref, tail_ref, out_ref,
    b_ref, wide, f8, w_ref, h0, h1, q_ref, acc,
):
    channels = mask_ref.shape[1]
    count, length = tmpl_ref.shape
    rows = 512
    groups = rows // 128
    lane = lane_iota((8, 128))
    sub = row_iota((8, 128))

    tmpl = tmpl_ref[...]
    for t in range(PH):
        if t == 0:
            w_ref[0:count, :] = tmpl
        else:
            turned = pltpu.roll(tmpl.astype(F32), t, 1)
            w_ref[t * count : (t + 1) * count, :] = jnp.where(
                lane_iota((count, length)) >= t, turned, 0.0
            ).astype(BF)

    band_setup(band_ref, b_ref)
    tiles = w_ref_in.shape[1] // 1024
    for m in range(tiles):
        at = 64 * m
        if m == 0:
            wide[0:64, 0:HALO] = jnp.zeros((64, HALO), BF)
            wide[0:64, HALO:] = w_ref_in[:, 0:1024]
        else:
            wide[at : at + 64, :] = w_ref_in[:, 1024 * m - HALO : 1024 * m + 1024]
    for v in range(0, PH, 2):
        passed = jnp.dot(
            wide[...], b_ref[:, 128 * v : 128 * v + 256], preferred_element_type=F32
        ).astype(BF).astype(F32)
        for m in range(tiles):
            for e in range(2):
                f8[:, v + e, 128 * m : 128 * m + 128] = passed[
                    64 * m : 64 * m + 64, 128 * e : 128 * e + 128
                ]

    def prepare(c):
        move = moveouts_ref[c]
        move1 = jnp.right_shift(move, 3)
        move0 = jnp.bitwise_and(move, 7)
        whole = f8[c]
        x = [whole[:, 128 * i : 128 * i + 128] for i in range(5)]
        y = shift_left(x, move1, lane)
        y2 = shift_left(x, move1 + 1, lane)
        turn = jnp.bitwise_and(8 - move0, 7)
        near = sub < 8 - move0
        a = [jnp.where(near, pltpu.roll(p, turn, 0), pltpu.roll(q, turn, 0)) for p, q in zip(y, y2)]
        nxt = shift_static(a, 1, lane)
        a16 = jnp.concatenate(
            [jnp.concatenate([p, q], axis=0) for p, q in zip(a, nxt)], axis=1
        ).astype(BF)
        total = [p * p for p in a]
        for k in range(6):
            total = [p + q for p, q in zip(total, shift_static(total, 1 << k, lane))]
        after = shift_static(total, 1, lane)
        scales = []
        for i in range(groups):
            suffix = total[i]
            prefix = jnp.where(sub >= 1, pltpu.roll(after[i], 1, 0), 0.0)
            for k in (1, 2, 4):
                suffix = suffix + jnp.where(sub < 8 - k, pltpu.roll(suffix, 8 - k, 0), 0.0)
                prefix = prefix + jnp.where(sub >= k, pltpu.roll(prefix, k, 0), 0.0)
            scales.append(lax.rsqrt((suffix + prefix) / length + EPSILON))
        late = [pltpu.roll(p, 64, 1) for p in a]
        tail = [jnp.where(lane < 64, late[i], late[i + 1]) for i in range(groups)]
        return a16, scales, tail

    def build(a16, h_ref):
        for u in range(32):
            turned = pltpu.roll(a16, 640 - 2 * u, 1) if u else a16
            h_ref[16 * u : 16 * u + 16, :] = turned[:, :rows]

    def add_channel(h_ref, scales, c):
        mask = pltpu.roll(mask_ref[...], jnp.where(c == 0, 0, channels - c), 1)[:, 0:1]
        mask = jnp.broadcast_to(mask, (count, 128))
        for nt in range(2):
            r = jnp.dot(w_ref[...], h_ref[:, 256 * nt : 256 * nt + 256], preferred_element_type=F32)
            for t in range(PH):
                for g in range(2):
                    factor = mask * scales[2 * nt + g][t : t + 1, :]
                    at = (slice(count * t, count * t + count), slice(256 * nt + 128 * g, 256 * nt + 128 * g + 128))
                    acc[at] = acc[at] + r[count * t : count * t + count, 128 * g : 128 * g + 128] * factor

    acc[...] = jnp.zeros_like(acc)

    def pair(i, carry):
        c = 2 * i
        a16_0, s0, t0 = prepare(c)
        build(a16_0, h0)
        a16_1, s1, t1 = prepare(c + 1)
        build(a16_1, h1)
        add_channel(h0, s0, c)
        add_channel(h1, s1, c + 1)
        at = pl.multiple_of(16 * i, 16)
        for t in range(1, PH):
            q_ref[t - 1, pl.ds(at, 16), :] = jnp.concatenate(
                [
                    jnp.concatenate([t0[g] * s0[g][t : t + 1, :], t1[g] * s1[g][t : t + 1, :]], axis=0)
                    for g in range(groups)
                ],
                axis=1,
            ).astype(BF)
        return carry

    lax.fori_loop(0, channels // 2, pair, 0)

    wide_tmpl = tmpl.astype(F32)
    power = jnp.mean(wide_tmpl * wide_tmpl, axis=1, keepdims=True)
    gain = 1.0 / (length * jnp.sqrt(power + EPSILON))
    for t in range(PH):
        block = acc[count * t : count * t + count, :]
        if t:
            block = block + jnp.dot(tail_ref[t - 1], q_ref[t - 1], preferred_element_type=F32)
        block = block * gain
        out_ref[:, count * t : count * t + count] = block.T.astype(BF)


def shards(raw_data, whiten_taps, band_taps, templates, channel_mask, moveouts):
    channels, block_time = raw_data.shape
    count, length = templates.shape
    tm = lax.axis_size("tm")
    chan = lax.axis_size("chan")
    halo = lax.ppermute(
        raw_data[:, block_time - HALO :], "tm", [(q, q + 1) for q in range(tm - 1)]
    )
    white = pl.pallas_call(
        whiten_kernel,
        out_shape=jax.ShapeDtypeStruct((channels, block_time), BF),
        in_specs=[VMEM] * 3,
        out_specs=VMEM,
    )(raw_data, halo, whiten_taps)
    white = lax.all_gather(white, "tm", axis=1, tiled=True)

    mask = channel_mask.astype(BF)
    spread = jnp.repeat(mask, PH, axis=1)
    tails = []
    for t in range(1, PH):
        last = jnp.pad(templates[:, length - t :], ((0, 0), (0, PH - t)))
        tails.append(jnp.tile(last, (1, channels)) * spread)
    tails = jnp.stack(tails)
    band = jnp.pad(band_taps, (0, 128 - band_taps.shape[0])).reshape(1, 128)

    partial = pl.pallas_call(
        stack_kernel,
        out_shape=jax.ShapeDtypeStruct((512, PH * count), BF),
        in_specs=[SMEM] + [VMEM] * 5,
        out_specs=VMEM,
        scratch_shapes=[
            pltpu.VMEM((1152, 1024), BF),
            pltpu.VMEM((320, 1152), BF),
            pltpu.VMEM((64, 8, 640), F32),
            pltpu.VMEM((512, 512), BF),
            pltpu.VMEM((512, 512), BF),
            pltpu.VMEM((512, 512), BF),
            pltpu.VMEM((7, 512, 512), BF),
            pltpu.VMEM((512, 512), F32),
        ],
        compiler_params=pltpu.CompilerParams(vmem_limit_bytes=40 * 2**20),
    )(moveouts, white, band, templates, channel_mask.astype(F32), tails)
    parts = lax.all_to_all(partial, "chan", 0, 0, tiled=True)
    total = jnp.sum(parts.reshape(chan, 512 // chan, PH * count).astype(F32), axis=0)
    return total.reshape(512 // chan * PH, count)


def solution(mesh):
    in_specs = (P("chan", "tm"), P("chan", None), P(), P("tm", None), P("tm", "chan"), P("chan"))
    out_specs = P("chan", "tm")
    return jax.shard_map(shards, mesh=mesh, in_specs=in_specs, out_specs=out_specs, check_vma=False)
```

time: 553 us -> 102 us (0.18)
  local copies, waits for them, and re-layouts: 257 us -> 6.88 us
  matrix products: 150 us -> 0 us
  waiting for transfers between devices: 74.9 us -> 0.01 us
  Pallas kernels: 0 us -> 58.7 us
  other arithmetic: 36.1 us -> 0.16 us
  blocking collectives: 14.8 us -> 34.7 us
  between operations: 14.2 us -> 0.21 us
    mul x33 -> x7, local copies, waits for them, and re-layouts: 186 us -> 0.68 us  [shards(): tails.append(jnp.tile(last, (1, channels)) * spread)]
    dot_general x10 -> x0, matrix products: 150 us -> none  [the longest x1 76.2 us: filter_block(): jnp.einsum('...r,rt->...t', whitened, matrix, preferred_element_type=jnp....]
    reduce_scatter x1 -> x0, waiting for transfers between devices: 74.8 us -> none  [shards(): lax.psum_scatter(stack_rows(aligned, data_scale, mask_float, toeplitz, te...]
    pallas_call x0 -> x2, Pallas kernels: none -> 58.7 us  [the longest x1 56 us: shards(): pl.pallas_call(stack_kernel, out_shape=jax.ShapeDtypeStruct((512, PH * co...]
    add x8 -> x0, other arithmetic: 25.3 us -> none  [add_group(): return running + jnp.sum(products * factor, axis=0)]
    all_to_all x0 -> x1, blocking collectives: none -> 19.9 us  [shards(): parts = lax.all_to_all(partial, 'chan', 0, 0, tiled=True)]
    slice x18 -> x8, local copies, waits for them, and re-layouts: 17.7 us -> 1.33 us  [the longest x1 0.79 us: shards(): raw_data[:, block_time - HALO:]]
    dynamic_slice x24 -> x0, local copies, waits for them, and re-layouts: 14.3 us -> none  [the longest x16 8.77 us: add_group(): lax.dynamic_slice_in_dim(scales, first_row, group_size, 0)]
  transfers between devices with their start and end apart: 2 -> 1, of which waited for: 1 -> 0; matrix products, arithmetic and copies ran while one was open for 5% -> 3% of each run, Pallas kernels for 0% -> 0%
where the time goes in v1:
time: 102 us
  Pallas kernels  58.7 us (58%)
  blocking collectives  34.7 us (34%)
  local copies, waits for them, and re-layouts  6.88 us (7%)
  starting transfers between devices  1.28 us (1%)
    pallas_call x1, Pallas kernels, shards(): pl.pallas_call(stack_kernel, out_shape=jax.ShapeDtypeStruct((512, PH * co...  56 us
    all_to_all x1, blocking collectives, shards(): parts = lax.all_to_all(partial, 'chan', 0, 0, tiled=True)  19.9 us
    all_gather x1, blocking collectives, shards(): white = lax.all_gather(white, 'tm', axis=1, tiled=True)  14.8 us
    unnamed x26, local copies, waits for them, and re-layouts  3.91 us
    pallas_call x1, Pallas kernels, shards(): pl.pallas_call(whiten_kernel, out_shape=jax.ShapeDtypeStruct((channels, b...  2.74 us
  transfers between devices with their start and end apart: 1, of which 0 were waited for; matrix products, arithmetic and copies ran while one was open for 3% of the time, Pallas kernels for 0%

profile of v1, /device:TPU:0, one launch (start us, length us, event | category | flops | bytes accessed | tf_op | source)
XLA Modules:
  0.0 101.9 jit_solution(17916902138444581995)
XLA Ops:
  0.0 0.0 copy-start
  0.0 0.8 slice.24
  0.8 1.3 %collective-permute-start = (f32[64,128]{1,0:T(8,128)S(1)}, f32[64,128]{1,0:T(8,128)S(1)}, u32[]{:S(2)}, u32[]{:S(2)}) collective-permute-start(f32[64,128]{1,0:T(8,128)S(1)} %slice.24), channel_id=1, source_target_pairs={{0,16},{16,32},{32,48},{48,64},{64,80},{80,96},{96,112},{1,17},{17... | collective-permute-start | bytes 98312 | tf_op jit(solution)/shard_map/ppermute | solution.py:205
  2.1 0.0 copy-done
  2.1 0.1 slice.29
  2.2 0.1 slice.30
  2.2 0.1 slice.31
  2.3 0.1 slice.27
  2.4 0.1 slice.28
  2.5 0.0 copy-start.3
  2.5 0.1 slice.25
  2.6 0.1 slice.26
  2.6 0.6 copy-done.3
  3.2 0.1 copy.10
  3.3 0.1 copy.29
  3.4 0.1 copy.30
  3.6 0.1 copy.31
  3.7 0.1 copy.27
  3.8 0.1 copy.28
  3.9 0.1 copy.25
  4.0 0.1 copy.26
  4.1 0.1 multiply_bitcast_fusion
  4.2 0.1 copy.17
  4.3 0.1 copy.18
  4.4 0.1 copy.19
  4.5 0.1 copy.20
  4.6 0.1 copy.21
  4.7 0.1 copy.22
  4.8 0.1 copy.23
  5.0 0.0 copy-start.5
  5.0 0.0 copy-start.4
  5.0 0.6 copy-done.5
  5.6 0.1 copy-done.4
  5.7 0.7 copy.8.taps_ref
  6.4 0.0 collective-permute-done.halo_ref
  6.4 0.0 copy-start.2
  6.4 0.6 copy-done.2
  7.0 2.7 %shard_map.64 = bf16[64,640]{1,0:T(8,128)(2,1)} custom-call(f32[64,640]{1,0:T(8,128)} %raw_ref.1, f32[64,128]{1,0:T(8,128)} %copy-done.2, f32[64,16]{1,0:T(8,128)} %copy.8.taps_ref), custom_call_target="tpu_custom_call" | custom-call | tf_op jit(solution)/shard_map/pallas_call | solution.py:208
  9.7 14.8 %all_gather.3.w_ref_in = bf16[64,5120]{1,0:T(8,128)(2,1)S(1)} all-gather(bf16[64,640]{1,0:T(8,128)(2,1)} %shard_map.64), channel_id=1, replica_groups=mesh['tm'=8,'chan'=16] {'tm'}, dimensions={1}, use_global_device_ids=true | all-gather | bytes 737280 | tf_op jit(solution)/shard_map/all_gather | solution.py:214
  24.5 0.0 copy-start.1
  24.5 0.7 copy-done.1
  25.2 56.0 %shard_map.65 = bf16[512,512]{1,0:T(8,128)(2,1)S(1)} custom-call(s32[64]{0:T(128)S(1)} %copy-done.1, bf16[64,5120]{1,0:T(8,128)(2,1)S(1)} %all_gather.3.w_ref_in, bf16[1,128]{1,0:T(2,128)(2,1)S(1)} %pad_bitcast_fusion.band_ref, bf16[64,512]{1,0:T(8,128)(2,1)S(1)} %copy-done, f32[64,64]{1,0:T(8,128)S(1)} %get-tuple-element.6.mask_ref, ...), custom_call_target="tpu_custom_call" | custom-call | tf_op jit(solution)/shard_map/pallas_call | solution.py:225
  81.2 19.9 %all_to_all.9 = bf16[16,32,512]{2,1,0:T(8,128)(2,1)S(1)} all-to-all(bf16[16,32,512]{2,1,0:T(8,128)(2,1)S(1)} %bitcast.17), channel_id=1, replica_groups=mesh['tm'=8,'chan'=16] {'chan'}, dimensions={0} | all-to-all | bytes 1048576 | tf_op jit(solution)/shard_map/all_to_all | solution.py:242
  101.1 0.1 convert_reduce_fusion
  101.1 0.1 reshape.180
  101.2 0.7 copy.24
  (16 shorter events, 0.1 us)
Async XLA Ops:
  0.0 2.1 %copy-start = (bf16[64,512]{1,0:T(8,128)(2,1)S(1)}, bf16[64,512]{1,0:T(8,128)(2,1)}, u32[]{:S(2)}) copy-start(bf16[64,512]{1,0:T(8,128)(2,1)} %tmpl_ref.1) | copy-start | bytes 196612
  0.8 5.6 %collective-permute-start = (f32[64,128]{1,0:T(8,128)S(1)}, f32[64,128]{1,0:T(8,128)S(1)}, u32[]{:S(2)}, u32[]{:S(2)}) collective-permute-start(f32[64,128]{1,0:T(8,128)S(1)} %slice.24), channel_id=1, source_target_pairs={{0,16},{16,32},{32,48},{48,64},{64,80},{80,96},{96,112},{1,17},{17... | collective-permute-start | bytes 98312 | tf_op jit(solution)/shard_map/ppermute | solution.py:205
  2.5 0.8 copy-start.3
  5.0 0.7 copy-start.5
  5.0 0.7 copy-start.4
  6.4 0.6 copy-start.2
  24.5 0.7 copy-start.1

commit v2 on v1

v2 whole, which is shorter than its diff:
```python
import functools

import jax
import jax.numpy as jnp
from jax import lax
from jax.experimental import pallas as pl
from jax.experimental.pallas import tpu as pltpu
from jax.sharding import PartitionSpec as P

EPSILON = 1e-06
GROUP = 8
UNROLL = 4
FIRST = (1, 4, 5)
SECOND = (2, 8, 10)
PH = 8
HALO = 128
VMEM = pl.BlockSpec(memory_space=pltpu.VMEM)
SMEM = pl.BlockSpec(memory_space=pltpu.SMEM)
BF = jnp.bfloat16
F32 = jnp.float32


def lane_iota(shape):
    return lax.broadcasted_iota(jnp.int32, shape, len(shape) - 1)


def row_iota(shape):
    return lax.broadcasted_iota(jnp.int32, shape, 0)


def whiten_kernel(raw_ref, halo_ref, taps_ref, out_ref):
    taps = taps_ref[...].T
    for at in range(0, raw_ref.shape[0], 16):
        halves = []
        for row in (at, at + 8):
            rows = slice(row, row + 8)
            ext = jnp.concatenate([halo_ref[rows, :], raw_ref[rows, :]], axis=1)
            acc = raw_ref[rows, :]
            for m in range(1, taps.shape[1] + 1):
                acc = acc - taps[rows, m - 1 : m] * pltpu.roll(ext, m, 1)[:, HALO:]
            halves.append(acc)
        out_ref[at : at + 16, :] = jnp.concatenate(halves, axis=0).astype(BF)


def shift_left(pieces, amount, lane):
    moved = [pltpu.roll(p, jnp.where(amount == 0, 0, 128 - amount), 1) for p in pieces]
    keep = lane < 128 - amount
    return [
        jnp.where(keep, moved[i], moved[(i + 1) % len(pieces)]) for i in range(len(pieces))
    ]


def shift_static(pieces, amount, lane):
    if amount == 0:
        return pieces
    moved = [pltpu.roll(p, 128 - amount, 1) for p in pieces]
    keep = lane < 128 - amount
    return [
        jnp.where(keep, moved[i], moved[(i + 1) % len(pieces)]) for i in range(len(pieces))
    ]


def band_setup(band_ref, b_ref):
    x = lane_iota((8, 128))
    s = row_iota((8, 128))
    residue = jnp.bitwise_and(8 - s, 7)
    band = jnp.broadcast_to(band_ref[...].astype(F32), (8, 128))
    left = jnp.where(jnp.bitwise_and(x, 7) == residue, band, 0.0).astype(BF)
    rx = row_iota((128, 128))
    rn = lane_iota((128, 128))
    right = (jnp.right_shift(rx + 16, 3) == rn).astype(F32).astype(BF)
    table = jnp.dot(left, right, preferred_element_type=F32)
    lane16 = lane_iota((16, 128))
    for v in range(PH):
        z = pltpu.roll(table, v, 0) if v else table
        z0 = pltpu.roll(z, 126, 1)
        z1 = pltpu.roll(z, 127, 1)
        upper = s <= v
        g = jnp.concatenate([jnp.where(upper, z0, z1), jnp.where(upper, z1, z)], axis=0)
        for pair in range(72):
            at = 2 * pair - 16
            turned = pltpu.roll(g, at % 128, 1) if at else g
            inside = (lane16 >= at) & (lane16 < at + 16)
            b_ref[16 * pair : 16 * pair + 16, 128 * v : 128 * v + 128] = jnp.where(
                inside, turned, 0.0
            ).astype(BF)


def setup_kernel(band_ref, tmpl_ref, b_ref, w_ref):
    count, length = tmpl_ref.shape
    wide_tmpl = tmpl_ref[...].astype(F32)
    w_ref[0:count, :] = tmpl_ref[...]
    for t in range(1, PH):
        w_ref[t * count : (t + 1) * count, :] = jnp.where(
            lane_iota((count, length)) >= t, pltpu.roll(wide_tmpl, t, 1), 0.0
        ).astype(BF)
    band_setup(band_ref, b_ref)


def spread_masks(tmpl_ref, mask_ref, ones_ref, tail_ref, m_ref):
    count, length = tmpl_ref.shape
    channels = mask_ref.shape[1]
    ri = row_iota((640, 640))
    ci = lane_iota((640, 640))
    ones_ref[...] = ((ri >= ci) & (ri < ci + 64)).astype(F32).astype(BF)
    mask = mask_ref[...].astype(F32).astype(BF)
    wide = 128 * 8
    for block in range(channels // 8):
        pick = row_iota((channels, wide)) == 8 * block + jnp.right_shift(lane_iota((channels, wide)), 7)
        spread = jnp.dot(mask, pick.astype(F32).astype(BF), preferred_element_type=F32).astype(BF)
        for k in range(8):
            m_ref[8 * block + k] = spread[:, 128 * k : 128 * k + 128]
    lanes = channels * PH
    repeat = row_iota((channels, lanes)) == jnp.right_shift(lane_iota((channels, lanes)), 3)
    spread = jnp.dot(mask, repeat.astype(F32).astype(BF), preferred_element_type=F32)
    v = jnp.bitwise_and(lane_iota((128, lanes)), PH - 1)
    j = row_iota((128, lanes))
    for t in range(1, PH):
        pick = (j == 128 - t + v) & (v < t)
        last = jnp.dot(
            tmpl_ref[:, length - 128 :], pick.astype(F32).astype(BF), preferred_element_type=F32
        )
        tail_ref[t - 1] = (last * spread).astype(BF)


def stack_kernel(place_ref, moveouts_ref, *refs):
    blocks = refs[:8]
    (tmpl_ref, mask_ref, b_ref, w_ref, keep_ref, *send_refs) = refs[8:16]
    (white, wide, f8, ones_ref, tail_ref, m_ref, h0, h1, a_ref, s_ref, q_ref, acc,
     high_ref, low_ref, tail_rows, sums, turned) = refs[16:]
    channels, _, rows = s_ref.shape
    count, length = tmpl_ref.shape
    groups = rows // 128
    lane = lane_iota((8, 128))
    sub = row_iota((8, 128))
    spread_masks(tmpl_ref, mask_ref, ones_ref, tail_ref, m_ref)

    me = place_ref[0]
    block_time = blocks[0].shape[1]
    white[:, 0:HALO] = jnp.zeros((64, HALO), BF)
    for k in range(8):
        chip = jnp.bitwise_and(jnp.right_shift(me, 1) + (k & 3), 3)
        core = jnp.bitwise_xor(jnp.bitwise_and(me, 1), k >> 2)
        at = pl.multiple_of(HALO + block_time * (2 * chip + core), 128)
        white[:, pl.ds(at, block_time)] = blocks[k][...]

    tiles = 5
    for m in range(tiles):
        wide[64 * m : 64 * m + 64, :] = white[:, 1024 * m : 1024 * m + 1024 + HALO]
    for v in range(0, PH, 2):
        passed = jnp.dot(
            wide[...], b_ref[:, 128 * v : 128 * v + 256], preferred_element_type=F32
        ).astype(BF).astype(F32)
        for m in range(tiles):
            for e in range(2):
                f8[:, v + e, 128 * m : 128 * m + 128] = passed[
                    64 * m : 64 * m + 64, 128 * e : 128 * e + 128
                ]

    def align(c):
        move = moveouts_ref[c]
        move1 = jnp.right_shift(move, 3)
        move0 = jnp.bitwise_and(move, 7)
        turn = jnp.bitwise_and(8 - move0, 7)
        near = sub < 8 - move0
        whole = f8[c]
        x = [pltpu.roll(whole[:, 128 * i : 128 * i + 128], turn, 0) for i in range(5)]
        y0 = shift_left(x, move1, lane)
        y1 = shift_static(y0, 1, lane)
        y2 = shift_static(y1, 1, lane)
        a = [jnp.where(near, p, q) for p, q in zip(y0, y1)]
        nxt = [jnp.where(near, p, q) for p, q in zip(y1, y2)]
        a_ref[c] = jnp.concatenate(
            [jnp.concatenate([p, q], axis=0) for p, q in zip(a, nxt)], axis=1
        ).astype(BF)
        return jnp.concatenate(a, axis=1)

    def first(i, carry):
        for e in range(0, GROUP, 2):
            c = GROUP * i + e
            both = jnp.concatenate([align(c), align(c + 1)], axis=0)
            square = both * both
            high = square.astype(BF)
            at = pl.ds(pl.multiple_of(8 * c, 16), 16)
            high_ref[at, :] = high
            low_ref[at, :] = (square - high.astype(F32)).astype(BF)
            tail_rows[at, :] = pltpu.roll(both.astype(BF), 640 - 64, 1)[:, :rows]
        return carry

    lax.fori_loop(0, channels // GROUP, first, 0)

    for half in range(2):
        at = slice(256 * half, 256 * half + 256)
        sums[at, :] = jnp.dot(
            high_ref[at, :], ones_ref[...], preferred_element_type=F32
        ) + jnp.dot(low_ref[at, :], ones_ref[...], preferred_element_type=F32)

    def second(i, carry):
        for e in range(0, GROUP, 2):
            pair_scales = []
            for k in range(2):
                c = GROUP * i + e + k
                whole = sums[pl.ds(pl.multiple_of(8 * c, 8), 8), :]
                total = [whole[:, 128 * g : 128 * g + 128] for g in range(5)]
                after = shift_static(total, 1, lane)
                scales = []
                for g in range(groups):
                    suffix = total[g]
                    prefix = jnp.where(sub >= 1, pltpu.roll(after[g], 1, 0), 0.0)
                    for step in (1, 2, 4):
                        suffix = suffix + jnp.where(sub < 8 - step, pltpu.roll(suffix, 8 - step, 0), 0.0)
                        prefix = prefix + jnp.where(sub >= step, pltpu.roll(prefix, step, 0), 0.0)
                    scales.append(lax.rsqrt((suffix + prefix) / length + EPSILON))
                scales = jnp.concatenate(scales, axis=1)
                s_ref[c] = scales
                pair_scales.append(scales)
            at = pl.ds(pl.multiple_of(8 * (GROUP * i + e), 16), 16)
            tail = tail_rows[at, :].astype(F32)
            for t in range(1, PH):
                q_ref[t - 1, at, :] = jnp.concatenate(
                    [tail[8 * k : 8 * k + 8] * pair_scales[k][t : t + 1, :] for k in range(2)], axis=0
                ).astype(BF)
        return carry

    lax.fori_loop(0, channels // GROUP, second, 0)
    keep = lane_iota((16, 128))

    def build(c, h_ref):
        x = a_ref[c]
        for u in range(32):
            for g in range(groups):
                p, q = x[:, 128 * g : 128 * g + 128], x[:, 128 * g + 128 : 128 * g + 256]
                if u:
                    p = pltpu.roll(jnp.where(keep >= 2 * u, p, q), 128 - 2 * u, 1)
                h_ref[16 * u : 16 * u + 16, 128 * g : 128 * g + 128] = p

    def add_channel(h_ref, c):
        mask = m_ref[c].astype(F32)
        for nt in range(2):
            lanes = slice(256 * nt, 256 * nt + 256)
            for half in range(2):
                r = jnp.dot(
                    w_ref[256 * half : 256 * half + 256, :], h_ref[:, lanes], preferred_element_type=F32
                )
                for t in range(4):
                    for g in range(2):
                        col = slice(256 * nt + 128 * g, 256 * nt + 128 * g + 128)
                        row = 4 * half + t
                        at = (slice(count * row, count * row + count), col)
                        part = r[count * t : count * t + count, 128 * g : 128 * g + 128]
                        acc[at] = acc[at] + part * (mask * s_ref[c, row : row + 1, col])

    acc[...] = jnp.zeros_like(acc)
    build(0, h0)

    def several(i, carry):
        for k in range(0, UNROLL, 2):
            c = UNROLL * i + k
            build(c + 1, h1)
            add_channel(h0, c)
            build(jnp.minimum(c + 2, channels - 1), h0)
            add_channel(h1, c + 1)
        return carry

    lax.fori_loop(0, channels // UNROLL, several, 0)

    wide_tmpl = tmpl_ref[...].astype(F32)
    power = jnp.mean(wide_tmpl * wide_tmpl, axis=1, keepdims=True)
    gain = 1.0 / (length * jnp.sqrt(power + EPSILON))
    for t in range(PH):
        at = slice(count * t, count * t + count)
        block = acc[at, :]
        if t:
            block = block + jnp.dot(tail_ref[t - 1], q_ref[t - 1], preferred_element_type=F32)
        turned[:, at] = (block * gain).T
    home = place_ref[1]
    for first_flip, ref in zip((0,) + FIRST, (keep_ref, *send_refs)):
        for p, second_flip in enumerate((0,) + SECOND):
            owner = jnp.bitwise_xor(home, first_flip ^ second_flip)
            part = turned[pl.ds(pl.multiple_of(32 * owner, 32), 32), :]
            ref[32 * p : 32 * p + 32, :] = part.astype(ref.dtype)


def gather_time(white):
    own = [white]
    for d in (1, 2, 3):
        own.append(lax.ppermute(white, "tm", [((q + 2 * d) % 8, q) for q in range(8)]))
    other = [lax.ppermute(p, "tm", [(q ^ 1, q) for q in range(8)]) for p in own]
    return own + other


def swap(value, flip):
    return lax.ppermute(value, "chan", [(i, i ^ flip) for i in range(lax.axis_size("chan"))])


def reduce_lags(kept, sent):
    total = kept
    for part, flip in zip([swap(p, f) for p, f in zip(sent, FIRST)], FIRST):
        total = total + part.astype(F32)
    narrow = total.astype(BF)
    rows = total.shape[0] // 4
    total = total[:rows]
    for k, flip in enumerate(SECOND):
        total = total + swap(narrow[rows * k + rows : rows * k + 2 * rows], flip).astype(F32)
    return total


def shards(raw_data, whiten_taps, band_taps, templates, channel_mask, moveouts):
    channels, block_time = raw_data.shape
    count, length = templates.shape
    tm = lax.axis_size("tm")
    halo = lax.ppermute(
        raw_data[:, block_time - HALO :], "tm", [(q, q + 1) for q in range(tm - 1)]
    )
    band = jnp.pad(band_taps, (0, 128 - band_taps.shape[0])).reshape(1, 128)
    b, w = pl.pallas_call(
        setup_kernel,
        out_shape=[
            jax.ShapeDtypeStruct((1152, 1024), BF),
            jax.ShapeDtypeStruct((512, 512), BF),
        ],
        in_specs=[VMEM] * 2,
        out_specs=[VMEM] * 2,
        cost_estimate=pl.CostEstimate(flops=2**31, bytes_accessed=2**22, transcendentals=0),
        compiler_params=pltpu.CompilerParams(vmem_limit_bytes=8 * 2**20),
    )(band, templates)
    white = pl.pallas_call(
        whiten_kernel,
        out_shape=jax.ShapeDtypeStruct((channels, block_time), BF),
        in_specs=[VMEM] * 3,
        out_specs=VMEM,
    )(raw_data, halo, whiten_taps.T)
    blocks = gather_time(white)
    place = jnp.stack([lax.axis_index("tm"), lax.axis_index("chan")]).astype(jnp.int32)
    kept, *sent = pl.pallas_call(
        stack_kernel,
        out_shape=[jax.ShapeDtypeStruct((128, PH * count), F32)]
        + [jax.ShapeDtypeStruct((128, PH * count), BF)] * 3,
        in_specs=[SMEM] * 2 + [VMEM] * 12,
        out_specs=[VMEM] * 4,
        scratch_shapes=[
            pltpu.VMEM((64, HALO + 5120), BF),
            pltpu.VMEM((320, 1152), BF),
            pltpu.VMEM((64, 8, 640), F32),
            pltpu.VMEM((640, 640), BF),
            pltpu.VMEM((7, 64, 512), BF),
            pltpu.VMEM((64, 64, 128), BF),
            pltpu.VMEM((512, 512), BF),
            pltpu.VMEM((512, 512), BF),
            pltpu.VMEM((64, 16, 640), BF),
            pltpu.VMEM((64, 8, 512), F32),
            pltpu.VMEM((7, 512, 512), BF),
            pltpu.VMEM((512, 512), F32),
            pltpu.VMEM((512, 640), BF),
            pltpu.VMEM((512, 640), BF),
            pltpu.VMEM((512, 512), BF),
            pltpu.VMEM((512, 640), F32),
            pltpu.VMEM((512, 512), F32),
        ],
        cost_estimate=pl.CostEstimate(flops=2**34, bytes_accessed=2**23, transcendentals=0),
        compiler_params=pltpu.CompilerParams(vmem_limit_bytes=30 * 2**20),
    )(place, moveouts, *blocks, templates, channel_mask, b, w)
    return reduce_lags(kept, sent).reshape(256, count)


def solution(mesh):
    in_specs = (P("chan", "tm"), P("chan", None), P(), P("tm", None), P("tm", "chan"), P("chan"))
    out_specs = P("chan", "tm")
    return jax.shard_map(shards, mesh=mesh, in_specs=in_specs, out_specs=out_specs, check_vma=False)
```

time: 102 us -> 74.8 us (0.73)
  blocking collectives: 34.7 us -> 0 us
  Pallas kernels: 58.7 us -> 36 us
  starting transfers between devices: 1.28 us -> 21.2 us
  waiting for transfers between devices: 0.01 us -> 13.3 us
  local copies, waits for them, and re-layouts: 6.88 us -> 3.7 us
    pallas_call x1 -> x2, Pallas kernels: 56 us -> 33.2 us  [the longest x1 31.8 us: shards(): pl.pallas_call(stack_kernel, out_shape=[jax.ShapeDtypeStruct((128, PH * c...]
    ppermute x0 -> x13, starting transfers between devices: none -> 20 us  [the longest x6 10.3 us: swap(): lax.ppermute(value, 'chan', [(i, i ^ flip) for i in range(lax.axis_size('...]
    all_to_all x1 -> x0, blocking collectives: 19.9 us -> none  [shards(): parts = lax.all_to_all(partial, 'chan', 0, 0, tiled=True)]
    all_gather x1 -> x0, blocking collectives: 14.8 us -> none  [shards(): white = lax.all_gather(white, 'tm', axis=1, tiled=True)]
    ppermute x0 -> x13, waiting for transfers between devices: none -> 13.1 us  [the longest x6 11.7 us: swap(): lax.ppermute(value, 'chan', [(i, i ^ flip) for i in range(lax.axis_size('...]
    unnamed x26 -> x12, local copies, waits for them, and re-layouts: 3.91 us -> 1.47 us
  transfers between devices with their start and end apart: 1 -> 14, of which waited for: 0 -> 10; matrix products, arithmetic and copies ran while one was open for 3% -> 1% of each run, Pallas kernels for 0% -> 2%
where the time goes in v2:
time: 74.8 us; the launch traced here: 74.5 us
  Pallas kernels  36 us (48%)
  starting transfers between devices  21.2 us (28%)
  waiting for transfers between devices  13.3 us (18%)
  local copies, waits for them, and re-layouts  3.7 us (5%)
    pallas_call x1, Pallas kernels, shards(): pl.pallas_call(stack_kernel, out_shape=[jax.ShapeDtypeStruct((128, PH * c...  31.8 us
    ppermute x6, waiting for transfers between devices, swap(): lax.ppermute(value, 'chan', [(i, i ^ flip) for i in range(lax.axis_size('...  11.7 us
    ppermute x6, starting transfers between devices, swap(): lax.ppermute(value, 'chan', [(i, i ^ flip) for i in range(lax.axis_size('...  10.3 us
    ppermute x3, starting transfers between devices, gather_time(): lax.ppermute(white, 'tm', [((q + 2 * d) % 8, q) for q in range(8)])  8.83 us
    pallas_call x1, Pallas kernels, shards(): pl.pallas_call(whiten_kernel, out_shape=jax.ShapeDtypeStruct((channels, b...  2.85 us
  transfers between devices with their start and end apart: 14, of which 10 were waited for; matrix products, arithmetic and copies ran while one was open for 1% of the time, Pallas kernels for 2%

profile of v2, /device:TPU:0, one launch (start us, length us, event | category | flops | bytes accessed | tf_op | source)
XLA Modules:
  0.0 74.5 jit_solution(1273362473060350903)
XLA Ops:
  0.0 0.8 %slice.15 = f32[64,128]{1,0:T(8,128)S(1)} slice(f32[64,640]{1,0:T(8,128)} %raw_ref.1), slice={[0:64], [512:640]} | slice | bytes 65536 | tf_op jit(solution)/shard_map/slice | solution.py:313
  0.8 1.3 %collective-permute-start = (f32[64,128]{1,0:T(8,128)S(1)}, f32[64,128]{1,0:T(8,128)S(1)}, u32[]{:S(2)}, u32[]{:S(2)}) collective-permute-start(f32[64,128]{1,0:T(8,128)S(1)} %slice.15), channel_id=1, source_target_pairs={{0,16},{16,32},{32,48},{48,64},{64,80},{80,96},{96,112},{1,17},{17... | collective-permute-start | bytes 98312 | tf_op jit(solution)/shard_map/ppermute | solution.py:312
  2.0 0.7 pad_bitcast_fusion.band_ref
  2.7 0.2 collective-permute-done.halo_ref
  2.9 0.0 copy-start.5
  2.9 0.6 copy-done.5
  3.5 0.0 copy-start.2
  3.5 0.0 copy-start.3
  3.5 0.0 copy-start.4
  3.5 2.9 %shard_map.64.refs_0_ = bf16[64,640]{1,0:T(8,128)(2,1)} custom-call(f32[64,640]{1,0:T(8,128)} %raw_ref.1, f32[64,128]{1,0:T(8,128)} %copy-done.5, f32[16,64]{1,0:T(8,128)} %bitcast.5), custom_call_target="tpu_custom_call" | custom-call | tf_op jit(solution)/shard_map/pallas_call | solution.py:327
  6.4 0.0 copy-start
  6.4 4.7 %collective-permute-start.3 = (bf16[64,640]{1,0:T(8,128)(2,1)}, bf16[64,640]{1,0:T(8,128)(2,1)S(1)}, u32[]{:S(2)}, u32[]{:S(2)}) collective-permute-start(bf16[64,640]{1,0:T(8,128)(2,1)} %shard_map.64.refs_0_), channel_id=1, source_target_pairs={{96,0},{112,16},{0,32},{16,48},{32,64},{48,80},{64,96},{80,112},{9... | collective-permute-start | bytes 245768 | tf_op jit(solution)/shard_map/ppermute | solution.py:287
  11.0 2.7 %collective-permute-start.2 = (bf16[64,640]{1,0:T(8,128)(2,1)}, bf16[64,640]{1,0:T(8,128)(2,1)S(1)}, u32[]{:S(2)}, u32[]{:S(2)}) collective-permute-start(bf16[64,640]{1,0:T(8,128)(2,1)} %shard_map.64.refs_0_), channel_id=1, source_target_pairs={{64,0},{80,16},{96,32},{112,48},{0,64},{16,80},{32,96},{48,112},{6... | collective-permute-start | bytes 245768 | tf_op jit(solution)/shard_map/ppermute | solution.py:287
  13.8 1.4 %collective-permute-start.1 = (bf16[64,640]{1,0:T(8,128)(2,1)}, bf16[64,640]{1,0:T(8,128)(2,1)S(1)}, u32[]{:S(2)}, u32[]{:S(2)}) collective-permute-start(bf16[64,640]{1,0:T(8,128)(2,1)} %shard_map.64.refs_0_), channel_id=1, source_target_pairs={{32,0},{48,16},{64,32},{80,48},{96,64},{112,80},{0,96},{16,112},{3... | collective-permute-start | bytes 245768 | tf_op jit(solution)/shard_map/ppermute | solution.py:287
  15.2 0.8 %copy-done.1 = bf16[64,512]{1,0:T(8,128)(2,1)S(1)} copy-done((bf16[64,512]{1,0:T(8,128)(2,1)S(1)}, bf16[64,512]{1,0:T(8,128)(2,1)}, u32[]{:S(2)}) %copy-start.1) | copy-done | bytes 65560
  16.0 1.4 %shard_map.65 = (bf16[1152,1024]{1,0:T(8,128)(2,1)S(1)}, bf16[512,512]{1,0:T(8,128)(2,1)S(1)}) custom-call(bf16[1,128]{1,0:T(2,128)(2,1)S(1)} %pad_bitcast_fusion.band_ref, bf16[64,512]{1,0:T(8,128)(2,1)S(1)} %copy-done.1), custom_call_target="tpu_custom_call" | custom-call | flops 2147483648 | bytes 4194304 | tf_op jit(solution)/shard_map/pallas_call | solution.py:316
  17.4 0.0 copy-done
  17.4 0.1 collective-permute-start.4
  17.5 0.0 collective-permute-done.3.refs_3_
  17.5 0.5 collective-permute-start.7
  18.0 0.0 collective-permute-done.2.refs_2_
  18.0 0.1 collective-permute-start.6
  18.1 0.3 collective-permute-done.1.refs_1_
  18.4 0.1 collective-permute-start.5
  18.6 0.1 pad_add_fusion.place_ref
  18.6 0.2 collective-permute-done.4.refs_4_
  18.8 0.2 collective-permute-done.7.refs_7_
  19.0 0.4 collective-permute-done.6.refs_6_
  19.3 0.4 collective-permute-done.5.refs_5_
  19.7 0.0 copy-done.2
  19.7 0.0 copy-done.3
  19.7 0.0 copy-done.4
  19.7 31.8 %shard_map.66 = (f32[128,512]{1,0:T(8,128)S(1)}, bf16[128,512]{1,0:T(8,128)(2,1)S(1)}, bf16[128,512]{1,0:T(8,128)(2,1)S(1)}, bf16[128,512]{1,0:T(8,128)(2,1)S(1)}) custom-call(s32[2]{0:T(128)S(1)} %pad_add_fusion.place_ref, s32[64]{0:T(128)S(1)} %copy-done.4, bf16[64,640]{1,0:T(8,128)(2,1)S(1)} %copy-done, ...), custom_call_target="tpu_custom_call" | custom-call | flops 17179869184 | bytes 8388608 | tf_op jit(solution)/shard_map/pallas_call | solution.py:335
  51.5 1.7 %collective-permute-start.8 = (bf16[128,512]{1,0:T(8,128)(2,1)S(1)}, bf16[128,512]{1,0:T(8,128)(2,1)S(1)}, u32[]{:S(2)}, u32[]{:S(2)}) collective-permute-start(bf16[128,512]{1,0:T(8,128)(2,1)S(1)} %get-tuple-element.14), channel_id=1, source_target_pairs={{0,1},{1,0},{2,3},{3,2},{4,5},{5,4},{6,7},{7,6},{8,9},{9,8},{10,11... | collective-permute-start | bytes 393224 | tf_op jit(solution)/shard_map/ppermute | solution.py:293
  53.2 1.9 %collective-permute-start.9 = (bf16[128,512]{1,0:T(8,128)(2,1)S(1)}, bf16[128,512]{1,0:T(8,128)(2,1)S(1)}, u32[]{:S(2)}, u32[]{:S(2)}) collective-permute-start(bf16[128,512]{1,0:T(8,128)(2,1)S(1)} %get-tuple-element.15), channel_id=1, source_target_pairs={{0,4},{1,5},{2,6},{3,7},{4,0},{5,1},{6,2},{7,3},{8,12},{9,13},{10,... | collective-permute-start | bytes 393224 | tf_op jit(solution)/shard_map/ppermute | solution.py:293
  55.1 0.0 collective-permute-start.10
  55.1 2.1 %collective-permute-done.8 = bf16[128,512]{1,0:T(8,128)(2,1)S(1)} collective-permute-done((bf16[128,512]{1,0:T(8,128)(2,1)S(1)}, bf16[128,512]{1,0:T(8,128)(2,1)S(1)}, u32[]{:S(2)}, u32[]{:S(2)}) %collective-permute-start.8) | collective-permute-done | bytes 131104 | tf_op jit(solution)/shard_map/ppermute | solution.py:293
  57.2 4.2 %collective-permute-done.9 = bf16[128,512]{1,0:T(8,128)(2,1)S(1)} collective-permute-done((bf16[128,512]{1,0:T(8,128)(2,1)S(1)}, bf16[128,512]{1,0:T(8,128)(2,1)S(1)}, u32[]{:S(2)}, u32[]{:S(2)}) %collective-permute-start.9) | collective-permute-done | bytes 131104 | tf_op jit(solution)/shard_map/ppermute | solution.py:293
  61.4 0.0 collective-permute-done.10
  61.4 0.1 fusion.2
  61.5 3.2 %collective-permute-start.11 = (bf16[32,512]{1,0:T(8,128)(2,1)S(1)}, bf16[32,512]{1,0:T(8,128)(2,1)S(1)}, u32[]{:S(2)}, u32[]{:S(2)}) collective-permute-start(bf16[32,512]{1,0:T(8,128)(2,1)S(1)} %get-tuple-element.19), channel_id=1, source_target_pairs={{0,2},{1,3},{2,0},{3,1},{4,6},{5,7},{6,4},{7,5},{8,10},{9,11},{10,... | collective-permute-start | bytes 98312 | tf_op jit(solution)/shard_map/ppermute | solution.py:293
  64.7 3.6 %collective-permute-start.13 = (bf16[32,512]{1,0:T(8,128)(2,1)S(1)}, bf16[32,512]{1,0:T(8,128)(2,1)S(1)}, u32[]{:S(2)}, u32[]{:S(2)}) collective-permute-start(bf16[32,512]{1,0:T(8,128)(2,1)S(1)} %get-tuple-element.20), channel_id=1, source_target_pairs={{0,10},{1,11},{2,8},{3,9},{4,14},{5,15},{6,12},{7,13},{8,2},{9,3},... | collective-permute-start | bytes 98312 | tf_op jit(solution)/shard_map/ppermute | solution.py:293
  68.3 0.0 collective-permute-start.12
  68.3 0.0 collective-permute-done.11
  68.3 4.2 %collective-permute-done.13 = bf16[32,512]{1,0:T(8,128)(2,1)S(1)} collective-permute-done((bf16[32,512]{1,0:T(8,128)(2,1)S(1)}, bf16[32,512]{1,0:T(8,128)(2,1)S(1)}, u32[]{:S(2)}, u32[]{:S(2)}) %collective-permute-start.13) | collective-permute-done | bytes 32800 | tf_op jit(solution)/shard_map/ppermute | solution.py:293
  72.5 1.2 %collective-permute-done.12 = bf16[32,512]{1,0:T(8,128)(2,1)S(1)} collective-permute-done((bf16[32,512]{1,0:T(8,128)(2,1)S(1)}, bf16[32,512]{1,0:T(8,128)(2,1)S(1)}, u32[]{:S(2)}, u32[]{:S(2)}) %collective-permute-start.12) | collective-permute-done | bytes 32800 | tf_op jit(solution)/shard_map/ppermute | solution.py:293
  73.7 0.1 reshape.7
  73.8 0.7 copy.8
  (3 shorter events, 0.0 us)
Async XLA Ops:
  0.8 2.1 %collective-permute-start = (f32[64,128]{1,0:T(8,128)S(1)}, f32[64,128]{1,0:T(8,128)S(1)}, u32[]{:S(2)}, u32[]{:S(2)}) collective-permute-start(f32[64,128]{1,0:T(8,128)S(1)} %slice.15), channel_id=1, source_target_pairs={{0,16},{16,32},{32,48},{48,64},{64,80},{80,96},{96,112},{1,17},{17... | collective-permute-start | bytes 98312 | tf_op jit(solution)/shard_map/ppermute | solution.py:312
  2.9 0.6 copy-start.5
  3.5 16.2 %copy-start.2 = (bf16[64,512]{1,0:T(8,128)(2,1)S(1)}, bf16[64,512]{1,0:T(8,128)(2,1)}, u32[]{:S(2)}) copy-start(bf16[64,512]{1,0:T(8,128)(2,1)} %refs_8_.1) | copy-start | bytes 196612
  3.5 16.2 %copy-start.3 = (s32[64,64]{1,0:T(8,128)S(1)}, s32[64,64]{1,0:T(8,128)}, u32[]{:S(2)}) copy-start(s32[64,64]{1,0:T(8,128)} %refs_9_.1) | copy-start | bytes 49156
  3.5 16.2 %copy-start.4 = (s32[64]{0:T(128)S(1)}, s32[64]{0:T(128)}, u32[]{:S(2)}) copy-start(s32[64]{0:T(128)} %moveouts_ref.1) | copy-start | bytes 772
  6.4 11.1 %copy-start = (bf16[64,640]{1,0:T(8,128)(2,1)S(1)}, bf16[64,640]{1,0:T(8,128)(2,1)}, u32[]{:S(2)}) copy-start(bf16[64,640]{1,0:T(8,128)(2,1)} %shard_map.64.refs_0_) | copy-start | bytes 245764
  6.4 11.2 %collective-permute-start.3 = (bf16[64,640]{1,0:T(8,128)(2,1)}, bf16[64,640]{1,0:T(8,128)(2,1)S(1)}, u32[]{:S(2)}, u32[]{:S(2)}) collective-permute-start(bf16[64,640]{1,0:T(8,128)(2,1)} %shard_map.64.refs_0_), channel_id=1, source_target_pairs={{96,0},{112,16},{0,32},{16,48},{32,64},{48,80},{64,96},{80,112},{9... | collective-permute-start | bytes 245768 | tf_op jit(solution)/shard_map/ppermute | solution.py:287
  11.0 7.0 %collective-permute-start.2 = (bf16[64,640]{1,0:T(8,128)(2,1)}, bf16[64,640]{1,0:T(8,128)(2,1)S(1)}, u32[]{:S(2)}, u32[]{:S(2)}) collective-permute-start(bf16[64,640]{1,0:T(8,128)(2,1)} %shard_map.64.refs_0_), channel_id=1, source_target_pairs={{64,0},{80,16},{96,32},{112,48},{0,64},{16,80},{32,96},{48,112},{6... | collective-permute-start | bytes 245768 | tf_op jit(solution)/shard_map/ppermute | solution.py:287
  13.8 4.7 %collective-permute-start.1 = (bf16[64,640]{1,0:T(8,128)(2,1)}, bf16[64,640]{1,0:T(8,128)(2,1)S(1)}, u32[]{:S(2)}, u32[]{:S(2)}) collective-permute-start(bf16[64,640]{1,0:T(8,128)(2,1)} %shard_map.64.refs_0_), channel_id=1, source_target_pairs={{32,0},{48,16},{64,32},{80,48},{96,64},{112,80},{0,96},{16,112},{3... | collective-permute-start | bytes 245768 | tf_op jit(solution)/shard_map/ppermute | solution.py:287
  15.2 0.8 %copy-start.1 = (bf16[64,512]{1,0:T(8,128)(2,1)S(1)}, bf16[64,512]{1,0:T(8,128)(2,1)}, u32[]{:S(2)}) copy-start(bf16[64,512]{1,0:T(8,128)(2,1)} %refs_8_.1) | copy-start | bytes 196612
  17.4 1.4 %collective-permute-start.4 = (bf16[64,640]{1,0:T(8,128)(2,1)S(1)}, bf16[64,640]{1,0:T(8,128)(2,1)S(1)}, u32[]{:S(2)}, u32[]{:S(2)}) collective-permute-start(bf16[64,640]{1,0:T(8,128)(2,1)S(1)} %copy-done), channel_id=1, source_target_pairs={{16,0},{0,16},{48,32},{32,48},{80,64},{64,80},{112,96},{96,112},{1... | collective-permute-start | bytes 245768 | tf_op jit(solution)/shard_map/ppermute | solution.py:288
  17.5 1.4 %collective-permute-start.7 = (bf16[64,640]{1,0:T(8,128)(2,1)S(1)}, bf16[64,640]{1,0:T(8,128)(2,1)S(1)}, u32[]{:S(2)}, u32[]{:S(2)}) collective-permute-start(bf16[64,640]{1,0:T(8,128)(2,1)S(1)} %collective-permute-done.3.refs_3_), channel_id=1, source_target_pairs={{16,0},{0,16},{48,32},{32,48},{80,64},{64,80},{112,96},{96,112},{1... | collective-permute-start | bytes 245768 | tf_op jit(solution)/shard_map/ppermute | solution.py:288
  18.0 1.3 %collective-permute-start.6 = (bf16[64,640]{1,0:T(8,128)(2,1)S(1)}, bf16[64,640]{1,0:T(8,128)(2,1)S(1)}, u32[]{:S(2)}, u32[]{:S(2)}) collective-permute-start(bf16[64,640]{1,0:T(8,128)(2,1)S(1)} %collective-permute-done.2.refs_2_), channel_id=1, source_target_pairs={{16,0},{0,16},{48,32},{32,48},{80,64},{64,80},{112,96},{96,112},{1... | collective-permute-start | bytes 245768 | tf_op jit(solution)/shard_map/ppermute | solution.py:288
  18.4 1.3 %collective-permute-start.5 = (bf16[64,640]{1,0:T(8,128)(2,1)S(1)}, bf16[64,640]{1,0:T(8,128)(2,1)S(1)}, u32[]{:S(2)}, u32[]{:S(2)}) collective-permute-start(bf16[64,640]{1,0:T(8,128)(2,1)S(1)} %collective-permute-done.1.refs_1_), channel_id=1, source_target_pairs={{16,0},{0,16},{48,32},{32,48},{80,64},{64,80},{112,96},{96,112},{1... | collective-permute-start | bytes 245768 | tf_op jit(solution)/shard_map/ppermute | solution.py:288
  51.5 5.7 %collective-permute-start.8 = (bf16[128,512]{1,0:T(8,128)(2,1)S(1)}, bf16[128,512]{1,0:T(8,128)(2,1)S(1)}, u32[]{:S(2)}, u32[]{:S(2)}) collective-permute-start(bf16[128,512]{1,0:T(8,128)(2,1)S(1)} %get-tuple-element.14), channel_id=1, source_target_pairs={{0,1},{1,0},{2,3},{3,2},{4,5},{5,4},{6,7},{7,6},{8,9},{9,8},{10,11... | collective-permute-start | bytes 393224 | tf_op jit(solution)/shard_map/ppermute | solution.py:293
  53.2 8.2 %collective-permute-start.9 = (bf16[128,512]{1,0:T(8,128)(2,1)S(1)}, bf16[128,512]{1,0:T(8,128)(2,1)S(1)}, u32[]{:S(2)}, u32[]{:S(2)}) collective-permute-start(bf16[128,512]{1,0:T(8,128)(2,1)S(1)} %get-tuple-element.15), channel_id=1, source_target_pairs={{0,4},{1,5},{2,6},{3,7},{4,0},{5,1},{6,2},{7,3},{8,12},{9,13},{10,... | collective-permute-start | bytes 393224 | tf_op jit(solution)/shard_map/ppermute | solution.py:293
  55.1 6.3 %collective-permute-start.10 = (bf16[128,512]{1,0:T(8,128)(2,1)S(1)}, bf16[128,512]{1,0:T(8,128)(2,1)S(1)}, u32[]{:S(2)}, u32[]{:S(2)}) collective-permute-start(bf16[128,512]{1,0:T(8,128)(2,1)S(1)} %get-tuple-element.16), channel_id=1, source_target_pairs={{0,5},{1,4},{2,7},{3,6},{4,1},{5,0},{6,3},{7,2},{8,13},{9,12},{10,... | collective-permute-start | bytes 393224 | tf_op jit(solution)/shard_map/ppermute | solution.py:293
  61.5 6.8 %collective-permute-start.11 = (bf16[32,512]{1,0:T(8,128)(2,1)S(1)}, bf16[32,512]{1,0:T(8,128)(2,1)S(1)}, u32[]{:S(2)}, u32[]{:S(2)}) collective-permute-start(bf16[32,512]{1,0:T(8,128)(2,1)S(1)} %get-tuple-element.19), channel_id=1, source_target_pairs={{0,2},{1,3},{2,0},{3,1},{4,6},{5,7},{6,4},{7,5},{8,10},{9,11},{10,... | collective-permute-start | bytes 98312 | tf_op jit(solution)/shard_map/ppermute | solution.py:293
  64.7 7.8 %collective-permute-start.13 = (bf16[32,512]{1,0:T(8,128)(2,1)S(1)}, bf16[32,512]{1,0:T(8,128)(2,1)S(1)}, u32[]{:S(2)}, u32[]{:S(2)}) collective-permute-start(bf16[32,512]{1,0:T(8,128)(2,1)S(1)} %get-tuple-element.20), channel_id=1, source_target_pairs={{0,10},{1,11},{2,8},{3,9},{4,14},{5,15},{6,12},{7,13},{8,2},{9,3},... | collective-permute-start | bytes 98312 | tf_op jit(solution)/shard_map/ppermute | solution.py:293
  68.3 5.4 %collective-permute-start.12 = (bf16[32,512]{1,0:T(8,128)(2,1)S(1)}, bf16[32,512]{1,0:T(8,128)(2,1)S(1)}, u32[]{:S(2)}, u32[]{:S(2)}) collective-permute-start(bf16[32,512]{1,0:T(8,128)(2,1)S(1)} %get-tuple-element.21), channel_id=1, source_target_pairs={{0,8},{1,9},{2,10},{3,11},{4,12},{5,13},{6,14},{7,15},{8,0},{9,1},... | collective-permute-start | bytes 98312 | tf_op jit(solution)/shard_map/ppermute | solution.py:293

commit v3 on v2

--- a/solution.py
+++ b/solution.py
@@ -10,8 +10,8 @@
 EPSILON = 1e-06
 GROUP = 8
 UNROLL = 4
-FIRST = (1, 4, 5)
-SECOND = (2, 8, 10)
+FIRST = (1, 3, 2)
+SECOND = (4, 12, 8)
 PH = 8
 HALO = 128
 VMEM = pl.BlockSpec(memory_space=pltpu.VMEM)
@@ -28,17 +28,30 @@
     return lax.broadcasted_iota(jnp.int32, shape, 0)
 
 
-def whiten_kernel(raw_ref, halo_ref, taps_ref, out_ref):
+def whiten_kernel(raw_ref, taps_ref, out_ref):
     taps = taps_ref[...].T
+    lane = lane_iota((8, 128))
+    width = raw_ref.shape[1]
     for at in range(0, raw_ref.shape[0], 16):
         halves = []
         for row in (at, at + 8):
             rows = slice(row, row + 8)
-            ext = jnp.concatenate([halo_ref[rows, :], raw_ref[rows, :]], axis=1)
-            acc = raw_ref[rows, :]
+            raw = [raw_ref[rows, k : k + 128] for k in range(0, width, 128)]
+            pieces = [jnp.zeros((8, 128), F32)] + raw
+            acc = raw
             for m in range(1, taps.shape[1] + 1):
-                acc = acc - taps[rows, m - 1 : m] * pltpu.roll(ext, m, 1)[:, HALO:]
-            halves.append(acc)
+                tap = taps[rows, m - 1 : m]
+                acc = [
+                    acc[i] - tap * pltpu.roll(jnp.where(lane < 128 - m, pieces[i + 1], pieces[i]), m, 1)
+                    for i in range(len(raw))
+                ]
+            edge = jnp.where(lane < 16, pltpu.roll(raw[-1], 16, 1), pltpu.roll(acc[0], 16, 1))
+            edge = jnp.where(lane < 32, edge, 0.0)
+            high = edge.astype(BF).astype(F32)
+            middle = (edge - high).astype(BF).astype(F32)
+            low = edge - high - middle
+            edge = high + pltpu.roll(middle, 32, 1) + pltpu.roll(low, 64, 1)
+            halves.append(jnp.concatenate(acc + [edge], axis=1))
         out_ref[at : at + 16, :] = jnp.concatenate(halves, axis=0).astype(BF)
 
 
@@ -64,7 +77,9 @@
     x = lane_iota((8, 128))
     s = row_iota((8, 128))
     residue = jnp.bitwise_and(8 - s, 7)
-    band = jnp.broadcast_to(band_ref[...].astype(F32), (8, 128))
+    taps = band_ref[...].astype(F32)
+    taps = jnp.concatenate([taps, jnp.zeros((1, 128 - taps.shape[1]), F32)], axis=1)
+    band = jnp.broadcast_to(taps, (8, 128))
     left = jnp.where(jnp.bitwise_and(x, 7) == residue, band, 0.0).astype(BF)
     rx = row_iota((128, 128))
     rn = lane_iota((128, 128))
@@ -100,8 +115,8 @@
 def spread_masks(tmpl_ref, mask_ref, ones_ref, tail_ref, m_ref):
     count, length = tmpl_ref.shape
     channels = mask_ref.shape[1]
-    ri = row_iota((640, 640))
-    ci = lane_iota((640, 640))
+    ri = row_iota((384, 256))
+    ci = lane_iota((384, 256))
     ones_ref[...] = ((ri >= ci) & (ri < ci + 64)).astype(F32).astype(BF)
     mask = mask_ref[...].astype(F32).astype(BF)
     wide = 128 * 8
@@ -125,9 +140,9 @@
 
 def stack_kernel(place_ref, moveouts_ref, *refs):
     blocks = refs[:8]
-    (tmpl_ref, mask_ref, b_ref, w_ref, keep_ref, *send_refs) = refs[8:16]
-    (white, wide, f8, ones_ref, tail_ref, m_ref, h0, h1, a_ref, s_ref, q_ref, acc,
-     high_ref, low_ref, tail_rows, sums, turned) = refs[16:]
+    (tmpl_ref, mask_ref, taps_ref, b_ref, w_ref, keep_ref, *send_refs) = refs[8:17]
+    (white, edges, wide, f8, ones_ref, tail_ref, m_ref, h0, h1, a_ref, s_ref, q_ref, acc,
+     high_ref, low_ref, tail_rows, sums, turned) = refs[17:]
     channels, _, rows = s_ref.shape
     count, length = tmpl_ref.shape
     groups = rows // 128
@@ -136,13 +151,44 @@
     spread_masks(tmpl_ref, mask_ref, ones_ref, tail_ref, m_ref)
 
     me = place_ref[0]
-    block_time = blocks[0].shape[1]
+    block_time = blocks[0].shape[1] - 128
     white[:, 0:HALO] = jnp.zeros((64, HALO), BF)
     for k in range(8):
         chip = jnp.bitwise_and(jnp.right_shift(me, 1) + (k & 3), 3)
         core = jnp.bitwise_xor(jnp.bitwise_and(me, 1), k >> 2)
-        at = pl.multiple_of(HALO + block_time * (2 * chip + core), 128)
-        white[:, pl.ds(at, block_time)] = blocks[k][...]
+        when = 2 * chip + core
+        at = pl.multiple_of(HALO + block_time * when, 128)
+        white[:, pl.ds(at, block_time)] = blocks[k][:, 0:block_time]
+        edge = blocks[k][:, block_time:].astype(F32)
+        edges[when] = edge + pltpu.roll(edge, 96, 1) + pltpu.roll(edge, 64, 1)
+
+    taps = taps_ref[...].T
+    for at in range(0, 64, 16):
+        fixed = []
+        for row in (at, at + 8):
+            rows16 = slice(row, row + 8)
+            both = []
+            for quad in range(2):
+                start = jnp.zeros((8, 128), F32)
+                before = jnp.zeros((8, 128), F32)
+                for k in range(4):
+                    when = 4 * quad + k
+                    own = edges[when, rows16, :]
+                    start = jnp.where((lane >= 32 * k + 16) & (lane < 32 * k + 32), pltpu.roll(own, 32 * k, 1) if k else own, start)
+                    if when:
+                        last = edges[when - 1, rows16, :]
+                        before = jnp.where((lane >= 32 * k) & (lane < 32 * k + 16), pltpu.roll(last, 32 * k, 1) if k else last, before)
+                for m in range(1, taps.shape[1] + 1):
+                    start = start - taps[rows16, m - 1 : m] * pltpu.roll(before, m, 1)
+                both.append(start)
+            fixed.append(both)
+        for when in range(1, 8):
+            quad, k = when >> 2, when & 3
+            first16 = jnp.concatenate([fixed[0][quad], fixed[1][quad]], axis=0)
+            first16 = pltpu.roll(first16, (112 - 32 * k) % 128, 1)
+            cols = slice(HALO + block_time * when, HALO + block_time * when + 128)
+            old = white[at : at + 16, cols].astype(F32)
+            white[at : at + 16, cols] = jnp.where(lane_iota((16, 128)) < 16, first16, old).astype(BF)
 
     tiles = 5
     for m in range(tiles):
@@ -190,10 +236,13 @@
     lax.fori_loop(0, channels // GROUP, first, 0)
 
     for half in range(2):
-        at = slice(256 * half, 256 * half + 256)
-        sums[at, :] = jnp.dot(
-            high_ref[at, :], ones_ref[...], preferred_element_type=F32
-        ) + jnp.dot(low_ref[at, :], ones_ref[...], preferred_element_type=F32)
+        at = slice(256 * half, 256 * half + 384)
+        sums[:, 256 * half : 256 * half + 256] = jnp.dot(
+            high_ref[:, at], ones_ref[...], preferred_element_type=F32
+        ) + jnp.dot(low_ref[:, at], ones_ref[...], preferred_element_type=F32)
+    last = high_ref[:, 512:640].astype(F32) + low_ref[:, 512:640].astype(F32)
+    last = jnp.sum(jnp.where(lane_iota((512, 128)) < 64, last, 0.0), axis=1, keepdims=True)
+    sums[:, 512:640] = jnp.broadcast_to(last, (512, 128))
 
     def second(i, carry):
         for e in range(0, GROUP, 2):
@@ -308,11 +357,13 @@
 def shards(raw_data, whiten_taps, band_taps, templates, channel_mask, moveouts):
     channels, block_time = raw_data.shape
     count, length = templates.shape
-    tm = lax.axis_size("tm")
-    halo = lax.ppermute(
-        raw_data[:, block_time - HALO :], "tm", [(q, q + 1) for q in range(tm - 1)]
-    )
-    band = jnp.pad(band_taps, (0, 128 - band_taps.shape[0])).reshape(1, 128)
+    white = pl.pallas_call(
+        whiten_kernel,
+        out_shape=jax.ShapeDtypeStruct((channels, block_time + 128), BF),
+        in_specs=[VMEM] * 2,
+        out_specs=VMEM,
+        compiler_params=pltpu.CompilerParams(vmem_limit_bytes=4 * 2**20),
+    )(raw_data, whiten_taps.T)
     b, w = pl.pallas_call(
         setup_kernel,
         out_shape=[
@@ -323,26 +374,21 @@
         out_specs=[VMEM] * 2,
         cost_estimate=pl.CostEstimate(flops=2**31, bytes_accessed=2**22, transcendentals=0),
         compiler_params=pltpu.CompilerParams(vmem_limit_bytes=8 * 2**20),
-    )(band, templates)
-    white = pl.pallas_call(
-        whiten_kernel,
-        out_shape=jax.ShapeDtypeStruct((channels, block_time), BF),
-        in_specs=[VMEM] * 3,
-        out_specs=VMEM,
-    )(raw_data, halo, whiten_taps.T)
+    )(band_taps.reshape(1, -1), templates)
     blocks = gather_time(white)
     place = jnp.stack([lax.axis_index("tm"), lax.axis_index("chan")]).astype(jnp.int32)
     kept, *sent = pl.pallas_call(
         stack_kernel,
         out_shape=[jax.ShapeDtypeStruct((128, PH * count), F32)]
         + [jax.ShapeDtypeStruct((128, PH * count), BF)] * 3,
-        in_specs=[SMEM] * 2 + [VMEM] * 12,
+        in_specs=[SMEM] * 2 + [VMEM] * 13,
         out_specs=[VMEM] * 4,
         scratch_shapes=[
             pltpu.VMEM((64, HALO + 5120), BF),
+            pltpu.VMEM((8, 64, 128), F32),
             pltpu.VMEM((320, 1152), BF),
             pltpu.VMEM((64, 8, 640), F32),
-            pltpu.VMEM((640, 640), BF),
+            pltpu.VMEM((384, 256), BF),
             pltpu.VMEM((7, 64, 512), BF),
             pltpu.VMEM((64, 64, 128), BF),
             pltpu.VMEM((512, 512), BF),
@@ -358,8 +404,8 @@
             pltpu.VMEM((512, 512), F32),
         ],
         cost_estimate=pl.CostEstimate(flops=2**34, bytes_accessed=2**23, transcendentals=0),
-        compiler_params=pltpu.CompilerParams(vmem_limit_bytes=30 * 2**20),
-    )(place, moveouts, *blocks, templates, channel_mask, b, w)
+        compiler_params=pltpu.CompilerParams(vmem_limit_bytes=26 * 2**20),
+    )(place, moveouts, *blocks, templates, channel_mask, whiten_taps.T, b, w)
     return reduce_lags(kept, sent).reshape(256, count)
 
 

time: 74.8 us -> 71.7 us (0.959)
  starting transfers between devices: 21.2 us -> 16.7 us
  Pallas kernels: 36 us -> 37.3 us
    ppermute x3, starting transfers between devices: 8.83 us -> 5.81 us  [gather_time(): lax.ppermute(white, 'tm', [((q + 2 * d) % 8, q) for q in range(8)])]
    pallas_call x1, Pallas kernels: 31.8 us -> 33.9 us  [shards(): pl.pallas_call(stack_kernel, out_shape=[jax.ShapeDtypeStruct((128, PH * c...]
    unnamed x12 -> x16, local copies, waits for them, and re-layouts: 1.47 us -> 3.12 us
    ppermute x1 -> x0, starting transfers between devices: 1.28 us -> none  [shards(): lax.ppermute(raw_data[:, block_time - HALO:], 'tm', [(q, q + 1) for q in...]
    pallas_call x1, Pallas kernels: 2.85 us -> 1.99 us  [shards(): pl.pallas_call(whiten_kernel, out_shape=jax.ShapeDtypeStruct((channels, b...]
    slice x1 -> x0, local copies, waits for them, and re-layouts: 0.76 us -> none  [shards(): raw_data[:, block_time - HALO:]]
  transfers between devices with their start and end apart: 14 -> 13, of which waited for: 10 -> 8; matrix products, arithmetic and copies ran while one was open for 1% -> 0% of each run, Pallas kernels for 2% -> 2%
where the time goes in v3:
time: 71.7 us; the launch traced here: 71.4 us
  Pallas kernels  37.3 us (52%)
  starting transfers between devices  16.7 us (23%)
  waiting for transfers between devices  13.4 us (19%)
  local copies, waits for them, and re-layouts  3.93 us (5%)
    pallas_call x1, Pallas kernels, shards(): pl.pallas_call(stack_kernel, out_shape=[jax.ShapeDtypeStruct((128, PH * c...  33.9 us
    ppermute x6, waiting for transfers between devices, swap(): lax.ppermute(value, 'chan', [(i, i ^ flip) for i in range(lax.axis_size('...  11.7 us
    ppermute x6, starting transfers between devices, swap(): lax.ppermute(value, 'chan', [(i, i ^ flip) for i in range(lax.axis_size('...  10.2 us
    ppermute x3, starting transfers between devices, gather_time(): lax.ppermute(white, 'tm', [((q + 2 * d) % 8, q) for q in range(8)])  5.81 us
    unnamed x16, local copies, waits for them, and re-layouts  3.12 us
    pallas_call x1, Pallas kernels, shards(): pl.pallas_call(whiten_kernel, out_shape=jax.ShapeDtypeStruct((channels, b...  1.99 us
  transfers between devices with their start and end apart: 13, of which 8 were waited for; matrix products, arithmetic and copies ran while one was open for 0% of the time, Pallas kernels for 2%

profile of v3, /device:TPU:0, one launch (start us, length us, event | category | flops | bytes accessed | tf_op | source)
XLA Modules:
  0.0 71.4 jit_solution(12473718400800603303)
XLA Ops:
  0.0 0.0 copy-start
  0.0 0.9 %copy-done = f32[64,640]{1,0:T(8,128)S(1)} copy-done((f32[64,640]{1,0:T(8,128)S(1)}, f32[64,640]{1,0:T(8,128)}, u32[]{:S(2)}) %copy-start) | copy-done | bytes 163864
  0.9 0.0 copy-start.1
  0.9 0.7 copy-done.1
  1.6 2.0 %shard_map.64.refs_0_ = bf16[64,768]{1,0:T(8,128)(2,1)S(1)} custom-call(f32[64,640]{1,0:T(8,128)S(1)} %copy-done, f32[16,64]{1,0:T(8,128)S(1)} %bitcast.4), custom_call_target="tpu_custom_call" | custom-call | tf_op jit(solution)/shard_map/pallas_call | solution.py:360
  3.6 0.1 collective-permute-start.3
  3.7 1.6 %collective-permute-start.2 = (bf16[64,768]{1,0:T(8,128)(2,1)S(1)}, bf16[64,768]{1,0:T(8,128)(2,1)S(1)}, u32[]{:S(2)}, u32[]{:S(2)}) collective-permute-start(bf16[64,768]{1,0:T(8,128)(2,1)S(1)} %shard_map.64.refs_0_), channel_id=1, source_target_pairs={{96,0},{112,16},{0,32},{16,48},{32,64},{48,80},{64,96},{80,112},{9... | collective-permute-start | bytes 294920 | tf_op jit(solution)/shard_map/ppermute | solution.py:336
  5.3 2.7 %collective-permute-start.1 = (bf16[64,768]{1,0:T(8,128)(2,1)S(1)}, bf16[64,768]{1,0:T(8,128)(2,1)S(1)}, u32[]{:S(2)}, u32[]{:S(2)}) collective-permute-start(bf16[64,768]{1,0:T(8,128)(2,1)S(1)} %shard_map.64.refs_0_), channel_id=1, source_target_pairs={{64,0},{80,16},{96,32},{112,48},{0,64},{16,80},{32,96},{48,112},{6... | collective-permute-start | bytes 294920 | tf_op jit(solution)/shard_map/ppermute | solution.py:336
  8.1 1.4 %collective-permute-start = (bf16[64,768]{1,0:T(8,128)(2,1)S(1)}, bf16[64,768]{1,0:T(8,128)(2,1)S(1)}, u32[]{:S(2)}, u32[]{:S(2)}) collective-permute-start(bf16[64,768]{1,0:T(8,128)(2,1)S(1)} %shard_map.64.refs_0_), channel_id=1, source_target_pairs={{32,0},{48,16},{64,32},{80,48},{96,64},{112,80},{0,96},{16,112},{3... | collective-permute-start | bytes 294920 | tf_op jit(solution)/shard_map/ppermute | solution.py:336
  9.5 0.0 copy-start.3
  9.5 0.8 %copy-done.3 = bf16[64,512]{1,0:T(8,128)(2,1)S(1)} copy-done((bf16[64,512]{1,0:T(8,128)(2,1)S(1)}, bf16[64,512]{1,0:T(8,128)(2,1)}, u32[]{:S(2)}) %copy-start.3) | copy-done | bytes 65560
  10.4 0.0 copy-start.6
  10.4 0.7 copy-done.6
  11.0 0.0 copy-start.2
  11.0 0.0 copy-start.4
  11.0 0.0 copy-start.5
  11.0 1.4 %shard_map.65 = (bf16[1152,1024]{1,0:T(8,128)(2,1)S(1)}, bf16[512,512]{1,0:T(8,128)(2,1)S(1)}) custom-call(bf16[1,113]{1,0:T(2,128)(2,1)S(1)} %bitcast.6, bf16[64,512]{1,0:T(8,128)(2,1)S(1)} %copy-done.3), custom_call_target="tpu_custom_call" | custom-call | flops 2147483648 | bytes 4194304 | tf_op jit(solution)/shard_map/pallas_call | solution.py:367
  12.4 0.0 collective-permute-done.2.refs_3_
  12.4 0.1 collective-permute-start.6
  12.5 0.8 %collective-permute-done.1.refs_2_ = bf16[64,768]{1,0:T(8,128)(2,1)S(1)} collective-permute-done((bf16[64,768]{1,0:T(8,128)(2,1)S(1)}, bf16[64,768]{1,0:T(8,128)(2,1)S(1)}, u32[]{:S(2)}, u32[]{:S(2)}) %collective-permute-start.1) | collective-permute-done | bytes 98336 | tf_op jit(solution)/shard_map/ppermute | solution.py:336
  13.3 0.0 collective-permute-start.5
  13.3 0.0 collective-permute-done.refs_1_
  13.3 0.5 collective-permute-start.4
  13.8 0.1 pad_add_fusion.place_ref
  13.9 0.0 collective-permute-done.3.refs_4_
  13.9 0.0 collective-permute-done.6.refs_7_
  13.9 0.7 collective-permute-done.5.refs_6_
  14.6 0.2 collective-permute-done.4.refs_5_
  14.8 0.0 copy-done.2
  14.8 0.0 copy-done.4
  14.8 0.0 copy-done.5
  14.8 0.0 copy-done.7
  14.8 33.9 %shard_map.66 = (f32[128,512]{1,0:T(8,128)S(1)}, bf16[128,512]{1,0:T(8,128)(2,1)S(1)}, bf16[128,512]{1,0:T(8,128)(2,1)S(1)}, bf16[128,512]{1,0:T(8,128)(2,1)S(1)}) custom-call(s32[2]{0:T(128)S(1)} %pad_add_fusion.place_ref, s32[64]{0:T(128)S(1)} %copy-done.7, bf16[64,768]{1,0:T(8,128)(2,1)S(1)} %shard_map.64.refs_0_, ...), custom_call_target="tpu_custom_call" | custom-call | flops 17179869184 | bytes 8388608 | tf_op jit(solution)/shard_map/pallas_call | solution.py:380
  48.7 1.7 %collective-permute-start.7 = (bf16[128,512]{1,0:T(8,128)(2,1)S(1)}, bf16[128,512]{1,0:T(8,128)(2,1)S(1)}, u32[]{:S(2)}, u32[]{:S(2)}) collective-permute-start(bf16[128,512]{1,0:T(8,128)(2,1)S(1)} %get-tuple-element.14), channel_id=1, source_target_pairs={{0,1},{1,0},{2,3},{3,2},{4,5},{5,4},{6,7},{7,6},{8,9},{9,8},{10,11... | collective-permute-start | bytes 393224 | tf_op jit(solution)/shard_map/ppermute | solution.py:342
  50.3 2.2 %collective-permute-start.8 = (bf16[128,512]{1,0:T(8,128)(2,1)S(1)}, bf16[128,512]{1,0:T(8,128)(2,1)S(1)}, u32[]{:S(2)}, u32[]{:S(2)}) collective-permute-start(bf16[128,512]{1,0:T(8,128)(2,1)S(1)} %get-tuple-element.15), channel_id=1, source_target_pairs={{0,3},{1,2},{2,1},{3,0},{4,7},{5,6},{6,5},{7,4},{8,11},{9,10},{10,... | collective-permute-start | bytes 393224 | tf_op jit(solution)/shard_map/ppermute | solution.py:342
  52.5 0.7 %collective-permute-start.9 = (bf16[128,512]{1,0:T(8,128)(2,1)S(1)}, bf16[128,512]{1,0:T(8,128)(2,1)S(1)}, u32[]{:S(2)}, u32[]{:S(2)}) collective-permute-start(bf16[128,512]{1,0:T(8,128)(2,1)S(1)} %get-tuple-element.16), channel_id=1, source_target_pairs={{0,2},{1,3},{2,0},{3,1},{4,6},{5,7},{6,4},{7,5},{8,10},{9,11},{10,... | collective-permute-start | bytes 393224 | tf_op jit(solution)/shard_map/ppermute | solution.py:342
  53.2 1.3 %collective-permute-done.7 = bf16[128,512]{1,0:T(8,128)(2,1)S(1)} collective-permute-done((bf16[128,512]{1,0:T(8,128)(2,1)S(1)}, bf16[128,512]{1,0:T(8,128)(2,1)S(1)}, u32[]{:S(2)}, u32[]{:S(2)}) %collective-permute-start.7) | collective-permute-done | bytes 131104 | tf_op jit(solution)/shard_map/ppermute | solution.py:342
  54.5 3.8 %collective-permute-done.8 = bf16[128,512]{1,0:T(8,128)(2,1)S(1)} collective-permute-done((bf16[128,512]{1,0:T(8,128)(2,1)S(1)}, bf16[128,512]{1,0:T(8,128)(2,1)S(1)}, u32[]{:S(2)}, u32[]{:S(2)}) %collective-permute-start.8) | collective-permute-done | bytes 131104 | tf_op jit(solution)/shard_map/ppermute | solution.py:342
  58.3 1.5 %collective-permute-done.9 = bf16[128,512]{1,0:T(8,128)(2,1)S(1)} collective-permute-done((bf16[128,512]{1,0:T(8,128)(2,1)S(1)}, bf16[128,512]{1,0:T(8,128)(2,1)S(1)}, u32[]{:S(2)}, u32[]{:S(2)}) %collective-permute-start.9) | collective-permute-done | bytes 131104 | tf_op jit(solution)/shard_map/ppermute | solution.py:342
  59.8 0.1 fusion.2
  59.9 2.0 %collective-permute-start.10 = (bf16[32,512]{1,0:T(8,128)(2,1)S(1)}, bf16[32,512]{1,0:T(8,128)(2,1)S(1)}, u32[]{:S(2)}, u32[]{:S(2)}) collective-permute-start(bf16[32,512]{1,0:T(8,128)(2,1)S(1)} %get-tuple-element.19), channel_id=1, source_target_pairs={{0,4},{1,5},{2,6},{3,7},{4,0},{5,1},{6,2},{7,3},{8,12},{9,13},{10,... | collective-permute-start | bytes 98312 | tf_op jit(solution)/shard_map/ppermute | solution.py:342
  61.9 3.6 %collective-permute-start.12 = (bf16[32,512]{1,0:T(8,128)(2,1)S(1)}, bf16[32,512]{1,0:T(8,128)(2,1)S(1)}, u32[]{:S(2)}, u32[]{:S(2)}) collective-permute-start(bf16[32,512]{1,0:T(8,128)(2,1)S(1)} %get-tuple-element.20), channel_id=1, source_target_pairs={{0,8},{1,9},{2,10},{3,11},{4,12},{5,13},{6,14},{7,15},{8,0},{9,1},... | collective-permute-start | bytes 98312 | tf_op jit(solution)/shard_map/ppermute | solution.py:342
  65.5 0.0 collective-permute-start.11
  65.5 0.0 collective-permute-done.10
  65.5 2.2 %collective-permute-done.12 = bf16[32,512]{1,0:T(8,128)(2,1)S(1)} collective-permute-done((bf16[32,512]{1,0:T(8,128)(2,1)S(1)}, bf16[32,512]{1,0:T(8,128)(2,1)S(1)}, u32[]{:S(2)}, u32[]{:S(2)}) %collective-permute-start.12) | collective-permute-done | bytes 32800 | tf_op jit(solution)/shard_map/ppermute | solution.py:342
  67.7 2.9 %collective-permute-done.11 = bf16[32,512]{1,0:T(8,128)(2,1)S(1)} collective-permute-done((bf16[32,512]{1,0:T(8,128)(2,1)S(1)}, bf16[32,512]{1,0:T(8,128)(2,1)S(1)}, u32[]{:S(2)}, u32[]{:S(2)}) %collective-permute-start.11) | collective-permute-done | bytes 32800 | tf_op jit(solution)/shard_map/ppermute | solution.py:342
  70.6 0.1 reshape.7
  70.7 0.7 copy.8
  (3 shorter events, 0.0 us)
Async XLA Ops:
  0.0 0.9 %copy-start = (f32[64,640]{1,0:T(8,128)S(1)}, f32[64,640]{1,0:T(8,128)}, u32[]{:S(2)}) copy-start(f32[64,640]{1,0:T(8,128)} %raw_ref.1) | copy-start | bytes 491524
  0.9 0.7 copy-start.1
  3.6 10.3 %collective-permute-start.3 = (bf16[64,768]{1,0:T(8,128)(2,1)S(1)}, bf16[64,768]{1,0:T(8,128)(2,1)S(1)}, u32[]{:S(2)}, u32[]{:S(2)}) collective-permute-start(bf16[64,768]{1,0:T(8,128)(2,1)S(1)} %shard_map.64.refs_0_), channel_id=1, source_target_pairs={{16,0},{0,16},{48,32},{32,48},{80,64},{64,80},{112,96},{96,112},{1... | collective-permute-start | bytes 294920 | tf_op jit(solution)/shard_map/ppermute | solution.py:337
  3.7 8.7 %collective-permute-start.2 = (bf16[64,768]{1,0:T(8,128)(2,1)S(1)}, bf16[64,768]{1,0:T(8,128)(2,1)S(1)}, u32[]{:S(2)}, u32[]{:S(2)}) collective-permute-start(bf16[64,768]{1,0:T(8,128)(2,1)S(1)} %shard_map.64.refs_0_), channel_id=1, source_target_pairs={{96,0},{112,16},{0,32},{16,48},{32,64},{48,80},{64,96},{80,112},{9... | collective-permute-start | bytes 294920 | tf_op jit(solution)/shard_map/ppermute | solution.py:336
  5.3 8.0 %collective-permute-start.1 = (bf16[64,768]{1,0:T(8,128)(2,1)S(1)}, bf16[64,768]{1,0:T(8,128)(2,1)S(1)}, u32[]{:S(2)}, u32[]{:S(2)}) collective-permute-start(bf16[64,768]{1,0:T(8,128)(2,1)S(1)} %shard_map.64.refs_0_), channel_id=1, source_target_pairs={{64,0},{80,16},{96,32},{112,48},{0,64},{16,80},{32,96},{48,112},{6... | collective-permute-start | bytes 294920 | tf_op jit(solution)/shard_map/ppermute | solution.py:336
  8.1 5.2 %collective-permute-start = (bf16[64,768]{1,0:T(8,128)(2,1)S(1)}, bf16[64,768]{1,0:T(8,128)(2,1)S(1)}, u32[]{:S(2)}, u32[]{:S(2)}) collective-permute-start(bf16[64,768]{1,0:T(8,128)(2,1)S(1)} %shard_map.64.refs_0_), channel_id=1, source_target_pairs={{32,0},{48,16},{64,32},{80,48},{96,64},{112,80},{0,96},{16,112},{3... | collective-permute-start | bytes 294920 | tf_op jit(solution)/shard_map/ppermute | solution.py:336
  9.5 0.8 %copy-start.3 = (bf16[64,512]{1,0:T(8,128)(2,1)S(1)}, bf16[64,512]{1,0:T(8,128)(2,1)}, u32[]{:S(2)}) copy-start(bf16[64,512]{1,0:T(8,128)(2,1)} %refs_8_.1) | copy-start | bytes 196612
  10.4 0.7 copy-start.6
  11.0 3.8 %copy-start.2 = (f32[64,16]{0,1:T(8,128)S(1)}, f32[64,16]{0,1:T(8,128)}, u32[]{:S(2)}) copy-start(f32[64,16]{0,1:T(8,128)} %param.7) | copy-start | bytes 12292
  11.0 3.8 %copy-start.4 = (bf16[64,512]{1,0:T(8,128)(2,1)S(1)}, bf16[64,512]{1,0:T(8,128)(2,1)}, u32[]{:S(2)}) copy-start(bf16[64,512]{1,0:T(8,128)(2,1)} %refs_8_.1) | copy-start | bytes 196612
  11.0 3.8 %copy-start.5 = (s32[64,64]{1,0:T(8,128)S(1)}, s32[64,64]{1,0:T(8,128)}, u32[]{:S(2)}) copy-start(s32[64,64]{1,0:T(8,128)} %refs_9_.1) | copy-start | bytes 49156
  11.0 3.8 %copy-start.7 = (s32[64]{0:T(128)S(1)}, s32[64]{0:T(128)}, u32[]{:S(2)}) copy-start(s32[64]{0:T(128)} %moveouts_ref.1) | copy-start | bytes 772
  12.4 1.5 %collective-permute-start.6 = (bf16[64,768]{1,0:T(8,128)(2,1)S(1)}, bf16[64,768]{1,0:T(8,128)(2,1)S(1)}, u32[]{:S(2)}, u32[]{:S(2)}) collective-permute-start(bf16[64,768]{1,0:T(8,128)(2,1)S(1)} %collective-permute-done.2.refs_3_), channel_id=1, source_target_pairs={{16,0},{0,16},{48,32},{32,48},{80,64},{64,80},{112,96},{96,112},{1... | collective-permute-start | bytes 294920 | tf_op jit(solution)/shard_map/ppermute | solution.py:337
  13.3 1.3 %collective-permute-start.5 = (bf16[64,768]{1,0:T(8,128)(2,1)S(1)}, bf16[64,768]{1,0:T(8,128)(2,1)S(1)}, u32[]{:S(2)}, u32[]{:S(2)}) collective-permute-start(bf16[64,768]{1,0:T(8,128)(2,1)S(1)} %collective-permute-done.1.refs_2_), channel_id=1, source_target_pairs={{16,0},{0,16},{48,32},{32,48},{80,64},{64,80},{112,96},{96,112},{1... | collective-permute-start | bytes 294920 | tf_op jit(solution)/shard_map/ppermute | solution.py:337
  13.3 1.5 %collective-permute-start.4 = (bf16[64,768]{1,0:T(8,128)(2,1)S(1)}, bf16[64,768]{1,0:T(8,128)(2,1)S(1)}, u32[]{:S(2)}, u32[]{:S(2)}) collective-permute-start(bf16[64,768]{1,0:T(8,128)(2,1)S(1)} %collective-permute-done.refs_1_), channel_id=1, source_target_pairs={{16,0},{0,16},{48,32},{32,48},{80,64},{64,80},{112,96},{96,112},{1... | collective-permute-start | bytes 294920 | tf_op jit(solution)/shard_map/ppermute | solution.py:337
  48.7 5.8 %collective-permute-start.7 = (bf16[128,512]{1,0:T(8,128)(2,1)S(1)}, bf16[128,512]{1,0:T(8,128)(2,1)S(1)}, u32[]{:S(2)}, u32[]{:S(2)}) collective-permute-start(bf16[128,512]{1,0:T(8,128)(2,1)S(1)} %get-tuple-element.14), channel_id=1, source_target_pairs={{0,1},{1,0},{2,3},{3,2},{4,5},{5,4},{6,7},{7,6},{8,9},{9,8},{10,11... | collective-permute-start | bytes 393224 | tf_op jit(solution)/shard_map/ppermute | solution.py:342
  50.3 8.0 %collective-permute-start.8 = (bf16[128,512]{1,0:T(8,128)(2,1)S(1)}, bf16[128,512]{1,0:T(8,128)(2,1)S(1)}, u32[]{:S(2)}, u32[]{:S(2)}) collective-permute-start(bf16[128,512]{1,0:T(8,128)(2,1)S(1)} %get-tuple-element.15), channel_id=1, source_target_pairs={{0,3},{1,2},{2,1},{3,0},{4,7},{5,6},{6,5},{7,4},{8,11},{9,10},{10,... | collective-permute-start | bytes 393224 | tf_op jit(solution)/shard_map/ppermute | solution.py:342
  52.5 7.3 %collective-permute-start.9 = (bf16[128,512]{1,0:T(8,128)(2,1)S(1)}, bf16[128,512]{1,0:T(8,128)(2,1)S(1)}, u32[]{:S(2)}, u32[]{:S(2)}) collective-permute-start(bf16[128,512]{1,0:T(8,128)(2,1)S(1)} %get-tuple-element.16), channel_id=1, source_target_pairs={{0,2},{1,3},{2,0},{3,1},{4,6},{5,7},{6,4},{7,5},{8,10},{9,11},{10,... | collective-permute-start | bytes 393224 | tf_op jit(solution)/shard_map/ppermute | solution.py:342
  59.9 5.6 %collective-permute-start.10 = (bf16[32,512]{1,0:T(8,128)(2,1)S(1)}, bf16[32,512]{1,0:T(8,128)(2,1)S(1)}, u32[]{:S(2)}, u32[]{:S(2)}) collective-permute-start(bf16[32,512]{1,0:T(8,128)(2,1)S(1)} %get-tuple-element.19), channel_id=1, source_target_pairs={{0,4},{1,5},{2,6},{3,7},{4,0},{5,1},{6,2},{7,3},{8,12},{9,13},{10,... | collective-permute-start | bytes 98312 | tf_op jit(solution)/shard_map/ppermute | solution.py:342
  61.9 5.8 %collective-permute-start.12 = (bf16[32,512]{1,0:T(8,128)(2,1)S(1)}, bf16[32,512]{1,0:T(8,128)(2,1)S(1)}, u32[]{:S(2)}, u32[]{:S(2)}) collective-permute-start(bf16[32,512]{1,0:T(8,128)(2,1)S(1)} %get-tuple-element.20), channel_id=1, source_target_pairs={{0,8},{1,9},{2,10},{3,11},{4,12},{5,13},{6,14},{7,15},{8,0},{9,1},... | collective-permute-start | bytes 98312 | tf_op jit(solution)/shard_map/ppermute | solution.py:342
  65.5 5.1 %collective-permute-start.11 = (bf16[32,512]{1,0:T(8,128)(2,1)S(1)}, bf16[32,512]{1,0:T(8,128)(2,1)S(1)}, u32[]{:S(2)}, u32[]{:S(2)}) collective-permute-start(bf16[32,512]{1,0:T(8,128)(2,1)S(1)} %get-tuple-element.21), channel_id=1, source_target_pairs={{0,12},{1,13},{2,14},{3,15},{4,8},{5,9},{6,10},{7,11},{8,4},{9,5},... | collective-permute-start | bytes 98312 | tf_op jit(solution)/shard_map/ppermute | solution.py:342

commit v4 on v3

--- a/solution.py
+++ b/solution.py
@@ -9,9 +9,9 @@
 
 EPSILON = 1e-06
 GROUP = 8
-UNROLL = 4
-FIRST = (1, 3, 2)
-SECOND = (4, 12, 8)
+UNROLL = 8
+FIRST = (2, 1, 3)
+SECOND = (8, 4, 12)
 PH = 8
 HALO = 128
 VMEM = pl.BlockSpec(memory_space=pltpu.VMEM)
@@ -28,7 +28,15 @@
     return lax.broadcasted_iota(jnp.int32, shape, 0)
 
 
-def whiten_kernel(raw_ref, taps_ref, out_ref):
+def whiten_kernel(raw_hbm, taps_hbm, out_ref, raw_ref, taps_ref, sems):
+    copies = [
+        pltpu.make_async_copy(taps_hbm, taps_ref, sems.at[0]),
+        pltpu.make_async_copy(raw_hbm, raw_ref, sems.at[1]),
+    ]
+    for copy in copies:
+        copy.start()
+    for copy in copies:
+        copy.wait()
     taps = taps_ref[...].T
     lane = lane_iota((8, 128))
     width = raw_ref.shape[1]
@@ -141,7 +149,7 @@
 def stack_kernel(place_ref, moveouts_ref, *refs):
     blocks = refs[:8]
     (tmpl_ref, mask_ref, taps_ref, b_ref, w_ref, keep_ref, *send_refs) = refs[8:17]
-    (white, edges, wide, f8, ones_ref, tail_ref, m_ref, h0, h1, a_ref, s_ref, q_ref, acc,
+    (white, edges, wide, f8, w_own, ones_ref, tail_ref, m_ref, h0, h1, a_ref, s_ref, q_ref, acc,
      high_ref, low_ref, tail_rows, sums, turned) = refs[17:]
     channels, _, rows = s_ref.shape
     count, length = tmpl_ref.shape
@@ -289,7 +297,7 @@
             lanes = slice(256 * nt, 256 * nt + 256)
             for half in range(2):
                 r = jnp.dot(
-                    w_ref[256 * half : 256 * half + 256, :], h_ref[:, lanes], preferred_element_type=F32
+                    w_own[256 * half : 256 * half + 256, :], h_ref[:, lanes], preferred_element_type=F32
                 )
                 for t in range(4):
                     for g in range(2):
@@ -300,6 +308,7 @@
                         acc[at] = acc[at] + part * (mask * s_ref[c, row : row + 1, col])
 
     acc[...] = jnp.zeros_like(acc)
+    w_own[...] = w_ref[...]
     build(0, h0)
 
     def several(i, carry):
@@ -360,8 +369,13 @@
     white = pl.pallas_call(
         whiten_kernel,
         out_shape=jax.ShapeDtypeStruct((channels, block_time + 128), BF),
-        in_specs=[VMEM] * 2,
+        in_specs=[pl.BlockSpec(memory_space=pltpu.HBM)] * 2,
         out_specs=VMEM,
+        scratch_shapes=[
+            pltpu.VMEM(raw_data.shape, F32),
+            pltpu.VMEM(whiten_taps.T.shape, F32),
+            pltpu.SemaphoreType.DMA((2,)),
+        ],
         compiler_params=pltpu.CompilerParams(vmem_limit_bytes=4 * 2**20),
     )(raw_data, whiten_taps.T)
     b, w = pl.pallas_call(
@@ -388,6 +402,7 @@
             pltpu.VMEM((8, 64, 128), F32),
             pltpu.VMEM((320, 1152), BF),
             pltpu.VMEM((64, 8, 640), F32),
+            pltpu.VMEM((512, 512), BF),
             pltpu.VMEM((384, 256), BF),
             pltpu.VMEM((7, 64, 512), BF),
             pltpu.VMEM((64, 64, 128), BF),

time: 71.7 us -> 66.3 us (0.925)
  Pallas kernels: 37.3 us -> 34.1 us
  waiting for transfers between devices: 13.4 us -> 12 us
  starting transfers between devices: 16.7 us -> 15.8 us
    pallas_call x1, Pallas kernels: 33.9 us -> 30.5 us  [shards(): pl.pallas_call(stack_kernel, out_shape=[jax.ShapeDtypeStruct((128, PH * c...]
    ppermute x6, waiting for transfers between devices: 11.7 us -> 10.3 us  [swap(): lax.ppermute(value, 'chan', [(i, i ^ flip) for i in range(lax.axis_size('...]
    ppermute x6, starting transfers between devices: 10.2 us -> 9.34 us  [swap(): lax.ppermute(value, 'chan', [(i, i ^ flip) for i in range(lax.axis_size('...]
  transfers between devices with their start and end apart: 13 -> 13, of which waited for: 8 -> 7; matrix products, arithmetic and copies ran while one was open for 0% -> 0% of each run, Pallas kernels for 2% -> 2%
where the time goes in v4:
time: 66.3 us; the launch traced here: 66 us
  Pallas kernels  34.1 us (51%)
  starting transfers between devices  15.8 us (24%)
  waiting for transfers between devices  12 us (18%)
  local copies, waits for them, and re-layouts  3.93 us (6%)
    pallas_call x1, Pallas kernels, shards(): pl.pallas_call(stack_kernel, out_shape=[jax.ShapeDtypeStruct((128, PH * c...  30.5 us
    ppermute x6, waiting for transfers between devices, swap(): lax.ppermute(value, 'chan', [(i, i ^ flip) for i in range(lax.axis_size('...  10.3 us
    ppermute x6, starting transfers between devices, swap(): lax.ppermute(value, 'chan', [(i, i ^ flip) for i in range(lax.axis_size('...  9.34 us
    ppermute x3, starting transfers between devices, gather_time(): lax.ppermute(white, 'tm', [((q + 2 * d) % 8, q) for q in range(8)])  5.81 us
    unnamed x16, local copies, waits for them, and re-layouts  3.12 us
    pallas_call x1, Pallas kernels, shards(): pl.pallas_call(whiten_kernel, out_shape=jax.ShapeDtypeStruct((channels, b...  2.21 us
    pallas_call x1, Pallas kernels, shards(): pl.pallas_call(setup_kernel, out_shape=[jax.ShapeDtypeStruct((1152, 1024)...  1.38 us
  transfers between devices with their start and end apart: 13, of which 7 were waited for; matrix products, arithmetic and copies ran while one was open for 0% of the time, Pallas kernels for 2%

profile of v4, /device:TPU:0, one launch (start us, length us, event | category | flops | bytes accessed | tf_op | source)
XLA Modules:
  0.0 66.0 jit_solution(12188991603572674395)
XLA Ops:
  0.0 0.0 copy-start
  0.0 0.9 %copy-done = f32[64,640]{1,0:T(8,128)S(1)} copy-done((f32[64,640]{1,0:T(8,128)S(1)}, f32[64,640]{1,0:T(8,128)}, u32[]{:S(2)}) %copy-start) | copy-done | bytes 163864
  0.9 0.0 copy-start.1
  0.9 0.7 %copy-done.1 = f32[64,16]{0,1:T(8,128)S(1)} copy-done((f32[64,16]{0,1:T(8,128)S(1)}, f32[64,16]{0,1:T(8,128)}, u32[]{:S(2)}) %copy-start.1) | copy-done | bytes 4120
  1.6 2.2 %shard_map.64.refs_0_ = bf16[64,768]{1,0:T(8,128)(2,1)S(1)} custom-call(f32[64,640]{1,0:T(8,128)S(1)} %copy-done, f32[16,64]{1,0:T(8,128)S(1)} %bitcast.4), custom_call_target="tpu_custom_call" | custom-call | tf_op jit(solution)/shard_map/pallas_call | solution.py:369
  3.8 0.1 collective-permute-start.3
  3.9 1.6 %collective-permute-start.2 = (bf16[64,768]{1,0:T(8,128)(2,1)S(1)}, bf16[64,768]{1,0:T(8,128)(2,1)S(1)}, u32[]{:S(2)}, u32[]{:S(2)}) collective-permute-start(bf16[64,768]{1,0:T(8,128)(2,1)S(1)} %shard_map.64.refs_0_), channel_id=1, source_target_pairs={{96,0},{112,16},{0,32},{16,48},{32,64},{48,80},{64,96},{80,112},{9... | collective-permute-start | bytes 294920 | tf_op jit(solution)/shard_map/ppermute | solution.py:345
  5.6 2.7 %collective-permute-start.1 = (bf16[64,768]{1,0:T(8,128)(2,1)S(1)}, bf16[64,768]{1,0:T(8,128)(2,1)S(1)}, u32[]{:S(2)}, u32[]{:S(2)}) collective-permute-start(bf16[64,768]{1,0:T(8,128)(2,1)S(1)} %shard_map.64.refs_0_), channel_id=1, source_target_pairs={{64,0},{80,16},{96,32},{112,48},{0,64},{16,80},{32,96},{48,112},{6... | collective-permute-start | bytes 294920 | tf_op jit(solution)/shard_map/ppermute | solution.py:345
  8.3 1.4 %collective-permute-start = (bf16[64,768]{1,0:T(8,128)(2,1)S(1)}, bf16[64,768]{1,0:T(8,128)(2,1)S(1)}, u32[]{:S(2)}, u32[]{:S(2)}) collective-permute-start(bf16[64,768]{1,0:T(8,128)(2,1)S(1)} %shard_map.64.refs_0_), channel_id=1, source_target_pairs={{32,0},{48,16},{64,32},{80,48},{96,64},{112,80},{0,96},{16,112},{3... | collective-permute-start | bytes 294920 | tf_op jit(solution)/shard_map/ppermute | solution.py:345
  9.7 0.0 copy-start.3
  9.7 0.8 %copy-done.3 = bf16[64,512]{1,0:T(8,128)(2,1)S(1)} copy-done((bf16[64,512]{1,0:T(8,128)(2,1)S(1)}, bf16[64,512]{1,0:T(8,128)(2,1)}, u32[]{:S(2)}) %copy-start.3) | copy-done | bytes 65560
  10.6 0.0 copy-start.6
  10.6 0.7 copy-done.6
  11.2 0.0 copy-start.2
  11.2 0.0 copy-start.4
  11.2 0.0 copy-start.5
  11.2 1.4 %shard_map.65 = (bf16[1152,1024]{1,0:T(8,128)(2,1)S(1)}, bf16[512,512]{1,0:T(8,128)(2,1)S(1)}) custom-call(bf16[1,113]{1,0:T(2,128)(2,1)S(1)} %bitcast.6, bf16[64,512]{1,0:T(8,128)(2,1)S(1)} %copy-done.3), custom_call_target="tpu_custom_call" | custom-call | flops 2147483648 | bytes 4194304 | tf_op jit(solution)/shard_map/pallas_call | solution.py:381
  12.6 0.0 collective-permute-done.2.refs_3_
  12.6 0.1 collective-permute-start.6
  12.7 0.8 %collective-permute-done.1.refs_2_ = bf16[64,768]{1,0:T(8,128)(2,1)S(1)} collective-permute-done((bf16[64,768]{1,0:T(8,128)(2,1)S(1)}, bf16[64,768]{1,0:T(8,128)(2,1)S(1)}, u32[]{:S(2)}, u32[]{:S(2)}) %collective-permute-start.1) | collective-permute-done | bytes 98336 | tf_op jit(solution)/shard_map/ppermute | solution.py:345
  13.5 0.0 collective-permute-start.5
  13.5 0.0 collective-permute-done.refs_1_
  13.5 0.5 collective-permute-start.4
  14.0 0.1 pad_add_fusion.place_ref
  14.1 0.0 collective-permute-done.3.refs_4_
  14.1 0.0 collective-permute-done.6.refs_7_
  14.1 0.7 %collective-permute-done.5.refs_6_ = bf16[64,768]{1,0:T(8,128)(2,1)S(1)} collective-permute-done((bf16[64,768]{1,0:T(8,128)(2,1)S(1)}, bf16[64,768]{1,0:T(8,128)(2,1)S(1)}, u32[]{:S(2)}, u32[]{:S(2)}) %collective-permute-start.5) | collective-permute-done | bytes 98336 | tf_op jit(solution)/shard_map/ppermute | solution.py:346
  14.8 0.2 collective-permute-done.4.refs_5_
  15.0 0.0 copy-done.2
  15.0 0.0 copy-done.4
  15.0 0.0 copy-done.5
  15.0 0.0 copy-done.7
  15.0 30.5 %shard_map.66 = (f32[128,512]{1,0:T(8,128)S(1)}, bf16[128,512]{1,0:T(8,128)(2,1)S(1)}, bf16[128,512]{1,0:T(8,128)(2,1)S(1)}, bf16[128,512]{1,0:T(8,128)(2,1)S(1)}) custom-call(s32[2]{0:T(128)S(1)} %pad_add_fusion.place_ref, s32[64]{0:T(128)S(1)} %copy-done.7, bf16[64,768]{1,0:T(8,128)(2,1)S(1)} %shard_map.64.refs_0_, ...), custom_call_target="tpu_custom_call" | custom-call | flops 17179869184 | bytes 8388608 | tf_op jit(solution)/shard_map/pallas_call | solution.py:394
  45.5 3.3 %collective-permute-start.7 = (bf16[128,512]{1,0:T(8,128)(2,1)S(1)}, bf16[128,512]{1,0:T(8,128)(2,1)S(1)}, u32[]{:S(2)}, u32[]{:S(2)}) collective-permute-start(bf16[128,512]{1,0:T(8,128)(2,1)S(1)} %get-tuple-element.14), channel_id=1, source_target_pairs={{0,2},{1,3},{2,0},{3,1},{4,6},{5,7},{6,4},{7,5},{8,10},{9,11},{10,... | collective-permute-start | bytes 393224 | tf_op jit(solution)/shard_map/ppermute | solution.py:351
  48.8 0.7 %collective-permute-start.8 = (bf16[128,512]{1,0:T(8,128)(2,1)S(1)}, bf16[128,512]{1,0:T(8,128)(2,1)S(1)}, u32[]{:S(2)}, u32[]{:S(2)}) collective-permute-start(bf16[128,512]{1,0:T(8,128)(2,1)S(1)} %get-tuple-element.15), channel_id=1, source_target_pairs={{0,1},{1,0},{2,3},{3,2},{4,5},{5,4},{6,7},{7,6},{8,9},{9,8},{10,11... | collective-permute-start | bytes 393224 | tf_op jit(solution)/shard_map/ppermute | solution.py:351
  49.5 0.4 collective-permute-start.9
  49.8 3.6 %collective-permute-done.7 = bf16[128,512]{1,0:T(8,128)(2,1)S(1)} collective-permute-done((bf16[128,512]{1,0:T(8,128)(2,1)S(1)}, bf16[128,512]{1,0:T(8,128)(2,1)S(1)}, u32[]{:S(2)}, u32[]{:S(2)}) %collective-permute-start.7) | collective-permute-done | bytes 131104 | tf_op jit(solution)/shard_map/ppermute | solution.py:351
  53.4 2.6 %collective-permute-done.8 = bf16[128,512]{1,0:T(8,128)(2,1)S(1)} collective-permute-done((bf16[128,512]{1,0:T(8,128)(2,1)S(1)}, bf16[128,512]{1,0:T(8,128)(2,1)S(1)}, u32[]{:S(2)}, u32[]{:S(2)}) %collective-permute-start.8) | collective-permute-done | bytes 131104 | tf_op jit(solution)/shard_map/ppermute | solution.py:351
  56.0 0.0 collective-permute-done.9
  56.0 0.1 fusion.2
  56.1 4.0 %collective-permute-start.10 = (bf16[32,512]{1,0:T(8,128)(2,1)S(1)}, bf16[32,512]{1,0:T(8,128)(2,1)S(1)}, u32[]{:S(2)}, u32[]{:S(2)}) collective-permute-start(bf16[32,512]{1,0:T(8,128)(2,1)S(1)} %get-tuple-element.19), channel_id=1, source_target_pairs={{0,8},{1,9},{2,10},{3,11},{4,12},{5,13},{6,14},{7,15},{8,0},{9,1},... | collective-permute-start | bytes 98312 | tf_op jit(solution)/shard_map/ppermute | solution.py:351
  60.1 0.7 %collective-permute-start.12 = (bf16[32,512]{1,0:T(8,128)(2,1)S(1)}, bf16[32,512]{1,0:T(8,128)(2,1)S(1)}, u32[]{:S(2)}, u32[]{:S(2)}) collective-permute-start(bf16[32,512]{1,0:T(8,128)(2,1)S(1)} %get-tuple-element.20), channel_id=1, source_target_pairs={{0,12},{1,13},{2,14},{3,15},{4,8},{5,9},{6,10},{7,11},{8,4},{9,5},... | collective-permute-start | bytes 98312 | tf_op jit(solution)/shard_map/ppermute | solution.py:351
  60.8 0.3 collective-permute-start.11
  61.1 0.9 %collective-permute-done.10 = bf16[32,512]{1,0:T(8,128)(2,1)S(1)} collective-permute-done((bf16[32,512]{1,0:T(8,128)(2,1)S(1)}, bf16[32,512]{1,0:T(8,128)(2,1)S(1)}, u32[]{:S(2)}, u32[]{:S(2)}) %collective-permute-start.10) | collective-permute-done | bytes 32800 | tf_op jit(solution)/shard_map/ppermute | solution.py:351
  62.0 3.2 %collective-permute-done.12 = bf16[32,512]{1,0:T(8,128)(2,1)S(1)} collective-permute-done((bf16[32,512]{1,0:T(8,128)(2,1)S(1)}, bf16[32,512]{1,0:T(8,128)(2,1)S(1)}, u32[]{:S(2)}, u32[]{:S(2)}) %collective-permute-start.12) | collective-permute-done | bytes 32800 | tf_op jit(solution)/shard_map/ppermute | solution.py:351
  65.2 0.0 collective-permute-done.11
  65.2 0.1 reshape.7
  65.3 0.7 %copy.8 = f32[256,64]{0,1:T(8,128)} copy(f32[256,64]{1,0:T(8,128)S(1)} %reshape.7) | data formatting | bytes 131072 | tf_op jit(solution)/shard_map/reshape | solution.py:424
  (3 shorter events, 0.0 us)
Async XLA Ops:
  0.0 0.9 %copy-start = (f32[64,640]{1,0:T(8,128)S(1)}, f32[64,640]{1,0:T(8,128)}, u32[]{:S(2)}) copy-start(f32[64,640]{1,0:T(8,128)} %raw_hbm.1) | copy-start | bytes 491524
  0.9 0.7 %copy-start.1 = (f32[64,16]{0,1:T(8,128)S(1)}, f32[64,16]{0,1:T(8,128)}, u32[]{:S(2)}) copy-start(f32[64,16]{0,1:T(8,128)} %param.7) | copy-start | bytes 12292
  3.8 10.3 %collective-permute-start.3 = (bf16[64,768]{1,0:T(8,128)(2,1)S(1)}, bf16[64,768]{1,0:T(8,128)(2,1)S(1)}, u32[]{:S(2)}, u32[]{:S(2)}) collective-permute-start(bf16[64,768]{1,0:T(8,128)(2,1)S(1)} %shard_map.64.refs_0_), channel_id=1, source_target_pairs={{16,0},{0,16},{48,32},{32,48},{80,64},{64,80},{112,96},{96,112},{1... | collective-permute-start | bytes 294920 | tf_op jit(solution)/shard_map/ppermute | solution.py:346
  3.9 8.7 %collective-permute-start.2 = (bf16[64,768]{1,0:T(8,128)(2,1)S(1)}, bf16[64,768]{1,0:T(8,128)(2,1)S(1)}, u32[]{:S(2)}, u32[]{:S(2)}) collective-permute-start(bf16[64,768]{1,0:T(8,128)(2,1)S(1)} %shard_map.64.refs_0_), channel_id=1, source_target_pairs={{96,0},{112,16},{0,32},{16,48},{32,64},{48,80},{64,96},{80,112},{9... | collective-permute-start | bytes 294920 | tf_op jit(solution)/shard_map/ppermute | solution.py:345
  5.6 8.0 %collective-permute-start.1 = (bf16[64,768]{1,0:T(8,128)(2,1)S(1)}, bf16[64,768]{1,0:T(8,128)(2,1)S(1)}, u32[]{:S(2)}, u32[]{:S(2)}) collective-permute-start(bf16[64,768]{1,0:T(8,128)(2,1)S(1)} %shard_map.64.refs_0_), channel_id=1, source_target_pairs={{64,0},{80,16},{96,32},{112,48},{0,64},{16,80},{32,96},{48,112},{6... | collective-permute-start | bytes 294920 | tf_op jit(solution)/shard_map/ppermute | solution.py:345
  8.3 5.2 %collective-permute-start = (bf16[64,768]{1,0:T(8,128)(2,1)S(1)}, bf16[64,768]{1,0:T(8,128)(2,1)S(1)}, u32[]{:S(2)}, u32[]{:S(2)}) collective-permute-start(bf16[64,768]{1,0:T(8,128)(2,1)S(1)} %shard_map.64.refs_0_), channel_id=1, source_target_pairs={{32,0},{48,16},{64,32},{80,48},{96,64},{112,80},{0,96},{16,112},{3... | collective-permute-start | bytes 294920 | tf_op jit(solution)/shard_map/ppermute | solution.py:345
  9.7 0.8 %copy-start.3 = (bf16[64,512]{1,0:T(8,128)(2,1)S(1)}, bf16[64,512]{1,0:T(8,128)(2,1)}, u32[]{:S(2)}) copy-start(bf16[64,512]{1,0:T(8,128)(2,1)} %refs_8_.1) | copy-start | bytes 196612
  10.6 0.7 copy-start.6
  11.2 3.8 %copy-start.2 = (f32[64,16]{0,1:T(8,128)S(1)}, f32[64,16]{0,1:T(8,128)}, u32[]{:S(2)}) copy-start(f32[64,16]{0,1:T(8,128)} %param.7) | copy-start | bytes 12292
  11.2 3.8 %copy-start.4 = (bf16[64,512]{1,0:T(8,128)(2,1)S(1)}, bf16[64,512]{1,0:T(8,128)(2,1)}, u32[]{:S(2)}) copy-start(bf16[64,512]{1,0:T(8,128)(2,1)} %refs_8_.1) | copy-start | bytes 196612
  11.2 3.8 %copy-start.5 = (s32[64,64]{1,0:T(8,128)S(1)}, s32[64,64]{1,0:T(8,128)}, u32[]{:S(2)}) copy-start(s32[64,64]{1,0:T(8,128)} %refs_9_.1) | copy-start | bytes 49156
  11.2 3.8 %copy-start.7 = (s32[64]{0:T(128)S(1)}, s32[64]{0:T(128)}, u32[]{:S(2)}) copy-start(s32[64]{0:T(128)} %moveouts_ref.1) | copy-start | bytes 772
  12.6 1.5 %collective-permute-start.6 = (bf16[64,768]{1,0:T(8,128)(2,1)S(1)}, bf16[64,768]{1,0:T(8,128)(2,1)S(1)}, u32[]{:S(2)}, u32[]{:S(2)}) collective-permute-start(bf16[64,768]{1,0:T(8,128)(2,1)S(1)} %collective-permute-done.2.refs_3_), channel_id=1, source_target_pairs={{16,0},{0,16},{48,32},{32,48},{80,64},{64,80},{112,96},{96,112},{1... | collective-permute-start | bytes 294920 | tf_op jit(solution)/shard_map/ppermute | solution.py:346
  13.5 1.3 %collective-permute-start.5 = (bf16[64,768]{1,0:T(8,128)(2,1)S(1)}, bf16[64,768]{1,0:T(8,128)(2,1)S(1)}, u32[]{:S(2)}, u32[]{:S(2)}) collective-permute-start(bf16[64,768]{1,0:T(8,128)(2,1)S(1)} %collective-permute-done.1.refs_2_), channel_id=1, source_target_pairs={{16,0},{0,16},{48,32},{32,48},{80,64},{64,80},{112,96},{96,112},{1... | collective-permute-start | bytes 294920 | tf_op jit(solution)/shard_map/ppermute | solution.py:346
  13.5 1.5 %collective-permute-start.4 = (bf16[64,768]{1,0:T(8,128)(2,1)S(1)}, bf16[64,768]{1,0:T(8,128)(2,1)S(1)}, u32[]{:S(2)}, u32[]{:S(2)}) collective-permute-start(bf16[64,768]{1,0:T(8,128)(2,1)S(1)} %collective-permute-done.refs_1_), channel_id=1, source_target_pairs={{16,0},{0,16},{48,32},{32,48},{80,64},{64,80},{112,96},{96,112},{1... | collective-permute-start | bytes 294920 | tf_op jit(solution)/shard_map/ppermute | solution.py:346
  45.5 7.9 %collective-permute-start.7 = (bf16[128,512]{1,0:T(8,128)(2,1)S(1)}, bf16[128,512]{1,0:T(8,128)(2,1)S(1)}, u32[]{:S(2)}, u32[]{:S(2)}) collective-permute-start(bf16[128,512]{1,0:T(8,128)(2,1)S(1)} %get-tuple-element.14), channel_id=1, source_target_pairs={{0,2},{1,3},{2,0},{3,1},{4,6},{5,7},{6,4},{7,5},{8,10},{9,11},{10,... | collective-permute-start | bytes 393224 | tf_op jit(solution)/shard_map/ppermute | solution.py:351
  48.8 7.2 %collective-permute-start.8 = (bf16[128,512]{1,0:T(8,128)(2,1)S(1)}, bf16[128,512]{1,0:T(8,128)(2,1)S(1)}, u32[]{:S(2)}, u32[]{:S(2)}) collective-permute-start(bf16[128,512]{1,0:T(8,128)(2,1)S(1)} %get-tuple-element.15), channel_id=1, source_target_pairs={{0,1},{1,0},{2,3},{3,2},{4,5},{5,4},{6,7},{7,6},{8,9},{9,8},{10,11... | collective-permute-start | bytes 393224 | tf_op jit(solution)/shard_map/ppermute | solution.py:351
  49.5 6.6 %collective-permute-start.9 = (bf16[128,512]{1,0:T(8,128)(2,1)S(1)}, bf16[128,512]{1,0:T(8,128)(2,1)S(1)}, u32[]{:S(2)}, u32[]{:S(2)}) collective-permute-start(bf16[128,512]{1,0:T(8,128)(2,1)S(1)} %get-tuple-element.16), channel_id=1, source_target_pairs={{0,3},{1,2},{2,1},{3,0},{4,7},{5,6},{6,5},{7,4},{8,11},{9,10},{10,... | collective-permute-start | bytes 393224 | tf_op jit(solution)/shard_map/ppermute | solution.py:351
  56.1 5.9 %collective-permute-start.10 = (bf16[32,512]{1,0:T(8,128)(2,1)S(1)}, bf16[32,512]{1,0:T(8,128)(2,1)S(1)}, u32[]{:S(2)}, u32[]{:S(2)}) collective-permute-start(bf16[32,512]{1,0:T(8,128)(2,1)S(1)} %get-tuple-element.19), channel_id=1, source_target_pairs={{0,8},{1,9},{2,10},{3,11},{4,12},{5,13},{6,14},{7,15},{8,0},{9,1},... | collective-permute-start | bytes 98312 | tf_op jit(solution)/shard_map/ppermute | solution.py:351
  60.1 5.1 %collective-permute-start.12 = (bf16[32,512]{1,0:T(8,128)(2,1)S(1)}, bf16[32,512]{1,0:T(8,128)(2,1)S(1)}, u32[]{:S(2)}, u32[]{:S(2)}) collective-permute-start(bf16[32,512]{1,0:T(8,128)(2,1)S(1)} %get-tuple-element.20), channel_id=1, source_target_pairs={{0,12},{1,13},{2,14},{3,15},{4,8},{5,9},{6,10},{7,11},{8,4},{9,5},... | collective-permute-start | bytes 98312 | tf_op jit(solution)/shard_map/ppermute | solution.py:351
  60.8 4.4 %collective-permute-start.11 = (bf16[32,512]{1,0:T(8,128)(2,1)S(1)}, bf16[32,512]{1,0:T(8,128)(2,1)S(1)}, u32[]{:S(2)}, u32[]{:S(2)}) collective-permute-start(bf16[32,512]{1,0:T(8,128)(2,1)S(1)} %get-tuple-element.21), channel_id=1, source_target_pairs={{0,4},{1,5},{2,6},{3,7},{4,0},{5,1},{6,2},{7,3},{8,12},{9,13},{10,... | collective-permute-start | bytes 98312 | tf_op jit(solution)/shard_map/ppermute | solution.py:351

commit v5 on v3

--- a/solution.py
+++ b/solution.py
@@ -9,9 +9,9 @@
 
 EPSILON = 1e-06
 GROUP = 8
-UNROLL = 4
-FIRST = (1, 3, 2)
-SECOND = (4, 12, 8)
+UNROLL = 8
+FIRST = (2, 1, 3)
+SECOND = (8, 4, 12)
 PH = 8
 HALO = 128
 VMEM = pl.BlockSpec(memory_space=pltpu.VMEM)
@@ -28,11 +28,11 @@
     return lax.broadcasted_iota(jnp.int32, shape, 0)
 
 
-def whiten_kernel(raw_ref, taps_ref, out_ref):
+def whiten_kernel(raw_ref, taps_ref, out_ref, first_ref):
     taps = taps_ref[...].T
     lane = lane_iota((8, 128))
-    width = raw_ref.shape[1]
-    for at in range(0, raw_ref.shape[0], 16):
+    rows_all, width = raw_ref.shape
+    for at in range(0, rows_all, 16):
         halves = []
         for row in (at, at + 8):
             rows = slice(row, row + 8)
@@ -45,14 +45,17 @@
                     acc[i] - tap * pltpu.roll(jnp.where(lane < 128 - m, pieces[i + 1], pieces[i]), m, 1)
                     for i in range(len(raw))
                 ]
-            edge = jnp.where(lane < 16, pltpu.roll(raw[-1], 16, 1), pltpu.roll(acc[0], 16, 1))
-            edge = jnp.where(lane < 32, edge, 0.0)
-            high = edge.astype(BF).astype(F32)
-            middle = (edge - high).astype(BF).astype(F32)
-            low = edge - high - middle
-            edge = high + pltpu.roll(middle, 32, 1) + pltpu.roll(low, 64, 1)
-            halves.append(jnp.concatenate(acc + [edge], axis=1))
-        out_ref[at : at + 16, :] = jnp.concatenate(halves, axis=0).astype(BF)
+            first_ref[rows, :] = acc[0]
+            halves.append(jnp.concatenate(acc, axis=1))
+        out_ref[at : at + 16, 0:width] = jnp.concatenate(halves, axis=0).astype(BF)
+    lane = lane_iota((rows_all, 128))
+    edge = pltpu.roll(jnp.where(lane < 16, first_ref[...], raw_ref[:, width - 128 :]), 16, 1)
+    edge = jnp.where(lane < 32, edge, 0.0)
+    high = edge.astype(BF).astype(F32)
+    middle = (edge - high).astype(BF).astype(F32)
+    low = edge - high - middle
+    edge = high + pltpu.roll(middle, 32, 1) + pltpu.roll(low, 64, 1)
+    out_ref[:, width:] = edge.astype(BF)
 
 
 def shift_left(pieces, amount, lane):
@@ -141,7 +144,7 @@
 def stack_kernel(place_ref, moveouts_ref, *refs):
     blocks = refs[:8]
     (tmpl_ref, mask_ref, taps_ref, b_ref, w_ref, keep_ref, *send_refs) = refs[8:17]
-    (white, edges, wide, f8, ones_ref, tail_ref, m_ref, h0, h1, a_ref, s_ref, q_ref, acc,
+    (white, edges, wide, f8, w_own, ones_ref, tail_ref, m_ref, h0, h1, a_ref, s_ref, q_ref, acc,
      high_ref, low_ref, tail_rows, sums, turned) = refs[17:]
     channels, _, rows = s_ref.shape
     count, length = tmpl_ref.shape
@@ -289,7 +292,7 @@
             lanes = slice(256 * nt, 256 * nt + 256)
             for half in range(2):
                 r = jnp.dot(
-                    w_ref[256 * half : 256 * half + 256, :], h_ref[:, lanes], preferred_element_type=F32
+                    w_own[256 * half : 256 * half + 256, :], h_ref[:, lanes], preferred_element_type=F32
                 )
                 for t in range(4):
                     for g in range(2):
@@ -300,6 +303,7 @@
                         acc[at] = acc[at] + part * (mask * s_ref[c, row : row + 1, col])
 
     acc[...] = jnp.zeros_like(acc)
+    w_own[...] = w_ref[...]
     build(0, h0)
 
     def several(i, carry):
@@ -362,6 +366,7 @@
         out_shape=jax.ShapeDtypeStruct((channels, block_time + 128), BF),
         in_specs=[VMEM] * 2,
         out_specs=VMEM,
+        scratch_shapes=[pltpu.VMEM((channels, 128), F32)],
         compiler_params=pltpu.CompilerParams(vmem_limit_bytes=4 * 2**20),
     )(raw_data, whiten_taps.T)
     b, w = pl.pallas_call(
@@ -388,6 +393,7 @@
             pltpu.VMEM((8, 64, 128), F32),
             pltpu.VMEM((320, 1152), BF),
             pltpu.VMEM((64, 8, 640), F32),
+            pltpu.VMEM((512, 512), BF),
             pltpu.VMEM((384, 256), BF),
             pltpu.VMEM((7, 64, 512), BF),
             pltpu.VMEM((64, 64, 128), BF),

time: 71.7 us -> 65.2 us (0.909)
  Pallas kernels: 37.3 us -> 33 us
  waiting for transfers between devices: 13.4 us -> 12 us
  starting transfers between devices: 16.7 us -> 15.8 us
    pallas_call x1, Pallas kernels: 33.9 us -> 30.5 us  [shards(): pl.pallas_call(stack_kernel, out_shape=[jax.ShapeDtypeStruct((128, PH * c...]
    ppermute x6, waiting for transfers between devices: 11.7 us -> 10.3 us  [swap(): lax.ppermute(value, 'chan', [(i, i ^ flip) for i in range(lax.axis_size('...]
    ppermute x6, starting transfers between devices: 10.2 us -> 9.31 us  [swap(): lax.ppermute(value, 'chan', [(i, i ^ flip) for i in range(lax.axis_size('...]
    pallas_call x1, Pallas kernels: 1.99 us -> 1.17 us  [shards(): pl.pallas_call(whiten_kernel, out_shape=jax.ShapeDtypeStruct((channels, b...]
  transfers between devices with their start and end apart: 13 -> 13, of which waited for: 8 -> 7; matrix products, arithmetic and copies ran while one was open for 0% -> 0% of each run, Pallas kernels for 2% -> 2%
where the time goes in v5:
time: 65.2 us; the launch traced here: 65 us
  Pallas kernels  33 us (51%)
  starting transfers between devices  15.8 us (24%)
  waiting for transfers between devices  12 us (18%)
  local copies, waits for them, and re-layouts  3.93 us (6%)
    pallas_call x1, Pallas kernels, shards(): pl.pallas_call(stack_kernel, out_shape=[jax.ShapeDtypeStruct((128, PH * c...  30.5 us
    ppermute x6, waiting for transfers between devices, swap(): lax.ppermute(value, 'chan', [(i, i ^ flip) for i in range(lax.axis_size('...  10.3 us
    ppermute x6, starting transfers between devices, swap(): lax.ppermute(value, 'chan', [(i, i ^ flip) for i in range(lax.axis_size('...  9.31 us
    ppermute x3, starting transfers between devices, gather_time(): lax.ppermute(white, 'tm', [((q + 2 * d) % 8, q) for q in range(8)])  5.81 us
    unnamed x16, local copies, waits for them, and re-layouts  3.12 us
    pallas_call x1, Pallas kernels, shards(): pl.pallas_call(setup_kernel, out_shape=[jax.ShapeDtypeStruct((1152, 1024)...  1.38 us
  transfers between devices with their start and end apart: 13, of which 7 were waited for; matrix products, arithmetic and copies ran while one was open for 0% of the time, Pallas kernels for 2%

profile of v5, /device:TPU:0, one launch (start us, length us, event | category | flops | bytes accessed | tf_op | source)
XLA Modules:
  0.0 65.0 jit_solution(17603495217384591539)
XLA Ops:
  0.0 0.0 copy-start
  0.0 0.9 %copy-done = f32[64,640]{1,0:T(8,128)S(1)} copy-done((f32[64,640]{1,0:T(8,128)S(1)}, f32[64,640]{1,0:T(8,128)}, u32[]{:S(2)}) %copy-start) | copy-done | bytes 163864
  0.9 0.0 copy-start.1
  0.9 0.7 %copy-done.1 = f32[64,16]{0,1:T(8,128)S(1)} copy-done((f32[64,16]{0,1:T(8,128)S(1)}, f32[64,16]{0,1:T(8,128)}, u32[]{:S(2)}) %copy-start.1) | copy-done | bytes 4120
  1.6 1.2 %shard_map.64.refs_0_ = bf16[64,768]{1,0:T(8,128)(2,1)S(1)} custom-call(f32[64,640]{1,0:T(8,128)S(1)} %copy-done, f32[16,64]{1,0:T(8,128)S(1)} %bitcast.4), custom_call_target="tpu_custom_call" | custom-call | tf_op jit(solution)/shard_map/pallas_call | solution.py:364
  2.8 0.1 collective-permute-start.3
  2.9 1.6 %collective-permute-start.2 = (bf16[64,768]{1,0:T(8,128)(2,1)S(1)}, bf16[64,768]{1,0:T(8,128)(2,1)S(1)}, u32[]{:S(2)}, u32[]{:S(2)}) collective-permute-start(bf16[64,768]{1,0:T(8,128)(2,1)S(1)} %shard_map.64.refs_0_), channel_id=1, source_target_pairs={{96,0},{112,16},{0,32},{16,48},{32,64},{48,80},{64,96},{80,112},{9... | collective-permute-start | bytes 294920 | tf_op jit(solution)/shard_map/ppermute | solution.py:340
  4.5 2.7 %collective-permute-start.1 = (bf16[64,768]{1,0:T(8,128)(2,1)S(1)}, bf16[64,768]{1,0:T(8,128)(2,1)S(1)}, u32[]{:S(2)}, u32[]{:S(2)}) collective-permute-start(bf16[64,768]{1,0:T(8,128)(2,1)S(1)} %shard_map.64.refs_0_), channel_id=1, source_target_pairs={{64,0},{80,16},{96,32},{112,48},{0,64},{16,80},{32,96},{48,112},{6... | collective-permute-start | bytes 294920 | tf_op jit(solution)/shard_map/ppermute | solution.py:340
  7.2 1.4 %collective-permute-start = (bf16[64,768]{1,0:T(8,128)(2,1)S(1)}, bf16[64,768]{1,0:T(8,128)(2,1)S(1)}, u32[]{:S(2)}, u32[]{:S(2)}) collective-permute-start(bf16[64,768]{1,0:T(8,128)(2,1)S(1)} %shard_map.64.refs_0_), channel_id=1, source_target_pairs={{32,0},{48,16},{64,32},{80,48},{96,64},{112,80},{0,96},{16,112},{3... | collective-permute-start | bytes 294920 | tf_op jit(solution)/shard_map/ppermute | solution.py:340
  8.7 0.0 copy-start.3
  8.7 0.8 %copy-done.3 = bf16[64,512]{1,0:T(8,128)(2,1)S(1)} copy-done((bf16[64,512]{1,0:T(8,128)(2,1)S(1)}, bf16[64,512]{1,0:T(8,128)(2,1)}, u32[]{:S(2)}) %copy-start.3) | copy-done | bytes 65560
  9.5 0.0 copy-start.6
  9.5 0.7 %copy-done.6 = bf16[113]{0:T(256)(128)(2,1)S(1)} copy-done((bf16[113]{0:T(256)(128)(2,1)S(1)}, bf16[113]{0:T(256)(128)(2,1)}, u32[]{:S(2)}) %copy-start.6) | copy-done | bytes 250
  10.2 0.0 copy-start.2
  10.2 0.0 copy-start.4
  10.2 0.0 copy-start.7
  10.2 1.4 %shard_map.65 = (bf16[1152,1024]{1,0:T(8,128)(2,1)S(1)}, bf16[512,512]{1,0:T(8,128)(2,1)S(1)}) custom-call(bf16[1,113]{1,0:T(2,128)(2,1)S(1)} %bitcast.6, bf16[64,512]{1,0:T(8,128)(2,1)S(1)} %copy-done.3), custom_call_target="tpu_custom_call" | custom-call | flops 2147483648 | bytes 4194304 | tf_op jit(solution)/shard_map/pallas_call | solution.py:372
  11.6 0.0 collective-permute-done.2.refs_3_
  11.6 0.1 collective-permute-start.6
  11.7 0.8 %collective-permute-done.1.refs_2_ = bf16[64,768]{1,0:T(8,128)(2,1)S(1)} collective-permute-done((bf16[64,768]{1,0:T(8,128)(2,1)S(1)}, bf16[64,768]{1,0:T(8,128)(2,1)S(1)}, u32[]{:S(2)}, u32[]{:S(2)}) %collective-permute-start.1) | collective-permute-done | bytes 98336 | tf_op jit(solution)/shard_map/ppermute | solution.py:340
  12.5 0.0 collective-permute-start.5
  12.5 0.0 collective-permute-done.refs_1_
  12.5 0.5 collective-permute-start.4
  13.0 0.1 pad_add_fusion.place_ref
  13.1 0.0 collective-permute-done.3.refs_4_
  13.1 0.0 collective-permute-done.6.refs_7_
  13.1 0.7 %collective-permute-done.5.refs_6_ = bf16[64,768]{1,0:T(8,128)(2,1)S(1)} collective-permute-done((bf16[64,768]{1,0:T(8,128)(2,1)S(1)}, bf16[64,768]{1,0:T(8,128)(2,1)S(1)}, u32[]{:S(2)}, u32[]{:S(2)}) %collective-permute-start.5) | collective-permute-done | bytes 98336 | tf_op jit(solution)/shard_map/ppermute | solution.py:341
  13.8 0.2 collective-permute-done.4.refs_5_
  13.9 0.0 copy-done.2
  13.9 0.0 copy-done.4
  13.9 0.0 copy-done.5
  13.9 0.0 copy-done.7
  13.9 30.5 %shard_map.66 = (f32[128,512]{1,0:T(8,128)S(1)}, bf16[128,512]{1,0:T(8,128)(2,1)S(1)}, bf16[128,512]{1,0:T(8,128)(2,1)S(1)}, bf16[128,512]{1,0:T(8,128)(2,1)S(1)}) custom-call(s32[2]{0:T(128)S(1)} %pad_add_fusion.place_ref, s32[64]{0:T(128)S(1)} %copy-done.7, bf16[64,768]{1,0:T(8,128)(2,1)S(1)} %shard_map.64.refs_0_, ...), custom_call_target="tpu_custom_call" | custom-call | flops 17179869184 | bytes 8388608 | tf_op jit(solution)/shard_map/pallas_call | solution.py:385
  44.4 3.3 %collective-permute-start.7 = (bf16[128,512]{1,0:T(8,128)(2,1)S(1)}, bf16[128,512]{1,0:T(8,128)(2,1)S(1)}, u32[]{:S(2)}, u32[]{:S(2)}) collective-permute-start(bf16[128,512]{1,0:T(8,128)(2,1)S(1)} %get-tuple-element.14), channel_id=1, source_target_pairs={{0,2},{1,3},{2,0},{3,1},{4,6},{5,7},{6,4},{7,5},{8,10},{9,11},{10,... | collective-permute-start | bytes 393224 | tf_op jit(solution)/shard_map/ppermute | solution.py:346
  47.7 0.7 %collective-permute-start.8 = (bf16[128,512]{1,0:T(8,128)(2,1)S(1)}, bf16[128,512]{1,0:T(8,128)(2,1)S(1)}, u32[]{:S(2)}, u32[]{:S(2)}) collective-permute-start(bf16[128,512]{1,0:T(8,128)(2,1)S(1)} %get-tuple-element.15), channel_id=1, source_target_pairs={{0,1},{1,0},{2,3},{3,2},{4,5},{5,4},{6,7},{7,6},{8,9},{9,8},{10,11... | collective-permute-start | bytes 393224 | tf_op jit(solution)/shard_map/ppermute | solution.py:346
  48.4 0.4 collective-permute-start.9
  48.8 3.6 %collective-permute-done.7 = bf16[128,512]{1,0:T(8,128)(2,1)S(1)} collective-permute-done((bf16[128,512]{1,0:T(8,128)(2,1)S(1)}, bf16[128,512]{1,0:T(8,128)(2,1)S(1)}, u32[]{:S(2)}, u32[]{:S(2)}) %collective-permute-start.7) | collective-permute-done | bytes 131104 | tf_op jit(solution)/shard_map/ppermute | solution.py:346
  52.4 2.6 %collective-permute-done.8 = bf16[128,512]{1,0:T(8,128)(2,1)S(1)} collective-permute-done((bf16[128,512]{1,0:T(8,128)(2,1)S(1)}, bf16[128,512]{1,0:T(8,128)(2,1)S(1)}, u32[]{:S(2)}, u32[]{:S(2)}) %collective-permute-start.8) | collective-permute-done | bytes 131104 | tf_op jit(solution)/shard_map/ppermute | solution.py:346
  55.0 0.0 collective-permute-done.9
  55.0 0.1 fusion.2
  55.1 4.0 %collective-permute-start.10 = (bf16[32,512]{1,0:T(8,128)(2,1)S(1)}, bf16[32,512]{1,0:T(8,128)(2,1)S(1)}, u32[]{:S(2)}, u32[]{:S(2)}) collective-permute-start(bf16[32,512]{1,0:T(8,128)(2,1)S(1)} %get-tuple-element.19), channel_id=1, source_target_pairs={{0,8},{1,9},{2,10},{3,11},{4,12},{5,13},{6,14},{7,15},{8,0},{9,1},... | collective-permute-start | bytes 98312 | tf_op jit(solution)/shard_map/ppermute | solution.py:346
  59.0 0.7 %collective-permute-start.12 = (bf16[32,512]{1,0:T(8,128)(2,1)S(1)}, bf16[32,512]{1,0:T(8,128)(2,1)S(1)}, u32[]{:S(2)}, u32[]{:S(2)}) collective-permute-start(bf16[32,512]{1,0:T(8,128)(2,1)S(1)} %get-tuple-element.20), channel_id=1, source_target_pairs={{0,12},{1,13},{2,14},{3,15},{4,8},{5,9},{6,10},{7,11},{8,4},{9,5},... | collective-permute-start | bytes 98312 | tf_op jit(solution)/shard_map/ppermute | solution.py:346
  59.8 0.3 collective-permute-start.11
  60.1 0.9 %collective-permute-done.10 = bf16[32,512]{1,0:T(8,128)(2,1)S(1)} collective-permute-done((bf16[32,512]{1,0:T(8,128)(2,1)S(1)}, bf16[32,512]{1,0:T(8,128)(2,1)S(1)}, u32[]{:S(2)}, u32[]{:S(2)}) %collective-permute-start.10) | collective-permute-done | bytes 32800 | tf_op jit(solution)/shard_map/ppermute | solution.py:346
  60.9 3.2 %collective-permute-done.12 = bf16[32,512]{1,0:T(8,128)(2,1)S(1)} collective-permute-done((bf16[32,512]{1,0:T(8,128)(2,1)S(1)}, bf16[32,512]{1,0:T(8,128)(2,1)S(1)}, u32[]{:S(2)}, u32[]{:S(2)}) %collective-permute-start.12) | collective-permute-done | bytes 32800 | tf_op jit(solution)/shard_map/ppermute | solution.py:346
  64.2 0.0 collective-permute-done.11
  64.2 0.1 reshape.7
  64.3 0.7 %copy.8 = f32[256,64]{0,1:T(8,128)} copy(f32[256,64]{1,0:T(8,128)S(1)} %reshape.7) | data formatting | bytes 131072 | tf_op jit(solution)/shard_map/reshape | solution.py:415
  (3 shorter events, 0.0 us)
Async XLA Ops:
  0.0 0.9 %copy-start = (f32[64,640]{1,0:T(8,128)S(1)}, f32[64,640]{1,0:T(8,128)}, u32[]{:S(2)}) copy-start(f32[64,640]{1,0:T(8,128)} %raw_ref.1) | copy-start | bytes 491524
  0.9 0.7 %copy-start.1 = (f32[64,16]{0,1:T(8,128)S(1)}, f32[64,16]{0,1:T(8,128)}, u32[]{:S(2)}) copy-start(f32[64,16]{0,1:T(8,128)} %param.7) | copy-start | bytes 12292
  2.8 10.3 %collective-permute-start.3 = (bf16[64,768]{1,0:T(8,128)(2,1)S(1)}, bf16[64,768]{1,0:T(8,128)(2,1)S(1)}, u32[]{:S(2)}, u32[]{:S(2)}) collective-permute-start(bf16[64,768]{1,0:T(8,128)(2,1)S(1)} %shard_map.64.refs_0_), channel_id=1, source_target_pairs={{16,0},{0,16},{48,32},{32,48},{80,64},{64,80},{112,96},{96,112},{1... | collective-permute-start | bytes 294920 | tf_op jit(solution)/shard_map/ppermute | solution.py:341
  2.9 8.7 %collective-permute-start.2 = (bf16[64,768]{1,0:T(8,128)(2,1)S(1)}, bf16[64,768]{1,0:T(8,128)(2,1)S(1)}, u32[]{:S(2)}, u32[]{:S(2)}) collective-permute-start(bf16[64,768]{1,0:T(8,128)(2,1)S(1)} %shard_map.64.refs_0_), channel_id=1, source_target_pairs={{96,0},{112,16},{0,32},{16,48},{32,64},{48,80},{64,96},{80,112},{9... | collective-permute-start | bytes 294920 | tf_op jit(solution)/shard_map/ppermute | solution.py:340
  4.5 8.0 %collective-permute-start.1 = (bf16[64,768]{1,0:T(8,128)(2,1)S(1)}, bf16[64,768]{1,0:T(8,128)(2,1)S(1)}, u32[]{:S(2)}, u32[]{:S(2)}) collective-permute-start(bf16[64,768]{1,0:T(8,128)(2,1)S(1)} %shard_map.64.refs_0_), channel_id=1, source_target_pairs={{64,0},{80,16},{96,32},{112,48},{0,64},{16,80},{32,96},{48,112},{6... | collective-permute-start | bytes 294920 | tf_op jit(solution)/shard_map/ppermute | solution.py:340
  7.2 5.2 %collective-permute-start = (bf16[64,768]{1,0:T(8,128)(2,1)S(1)}, bf16[64,768]{1,0:T(8,128)(2,1)S(1)}, u32[]{:S(2)}, u32[]{:S(2)}) collective-permute-start(bf16[64,768]{1,0:T(8,128)(2,1)S(1)} %shard_map.64.refs_0_), channel_id=1, source_target_pairs={{32,0},{48,16},{64,32},{80,48},{96,64},{112,80},{0,96},{16,112},{3... | collective-permute-start | bytes 294920 | tf_op jit(solution)/shard_map/ppermute | solution.py:340
  8.7 0.8 %copy-start.3 = (bf16[64,512]{1,0:T(8,128)(2,1)S(1)}, bf16[64,512]{1,0:T(8,128)(2,1)}, u32[]{:S(2)}) copy-start(bf16[64,512]{1,0:T(8,128)(2,1)} %refs_8_.1) | copy-start | bytes 196612
  9.5 0.7 %copy-start.6 = (bf16[113]{0:T(256)(128)(2,1)S(1)}, bf16[113]{0:T(256)(128)(2,1)}, u32[]{:S(2)}) copy-start(bf16[113]{0:T(256)(128)(2,1)} %param.8) | copy-start | bytes 682
  10.2 3.8 %copy-start.2 = (f32[64,16]{0,1:T(8,128)S(1)}, f32[64,16]{0,1:T(8,128)}, u32[]{:S(2)}) copy-start(f32[64,16]{0,1:T(8,128)} %param.7) | copy-start | bytes 12292
  10.2 3.8 %copy-start.4 = (bf16[64,512]{1,0:T(8,128)(2,1)S(1)}, bf16[64,512]{1,0:T(8,128)(2,1)}, u32[]{:S(2)}) copy-start(bf16[64,512]{1,0:T(8,128)(2,1)} %refs_8_.1) | copy-start | bytes 196612
  10.2 3.8 %copy-start.5 = (s32[64,64]{1,0:T(8,128)S(1)}, s32[64,64]{1,0:T(8,128)}, u32[]{:S(2)}) copy-start(s32[64,64]{1,0:T(8,128)} %refs_9_.1) | copy-start | bytes 49156
  10.2 3.8 %copy-start.7 = (s32[64]{0:T(128)S(1)}, s32[64]{0:T(128)}, u32[]{:S(2)}) copy-start(s32[64]{0:T(128)} %moveouts_ref.1) | copy-start | bytes 772
  11.6 1.5 %collective-permute-start.6 = (bf16[64,768]{1,0:T(8,128)(2,1)S(1)}, bf16[64,768]{1,0:T(8,128)(2,1)S(1)}, u32[]{:S(2)}, u32[]{:S(2)}) collective-permute-start(bf16[64,768]{1,0:T(8,128)(2,1)S(1)} %collective-permute-done.2.refs_3_), channel_id=1, source_target_pairs={{16,0},{0,16},{48,32},{32,48},{80,64},{64,80},{112,96},{96,112},{1... | collective-permute-start | bytes 294920 | tf_op jit(solution)/shard_map/ppermute | solution.py:341
  12.5 1.3 %collective-permute-start.5 = (bf16[64,768]{1,0:T(8,128)(2,1)S(1)}, bf16[64,768]{1,0:T(8,128)(2,1)S(1)}, u32[]{:S(2)}, u32[]{:S(2)}) collective-permute-start(bf16[64,768]{1,0:T(8,128)(2,1)S(1)} %collective-permute-done.1.refs_2_), channel_id=1, source_target_pairs={{16,0},{0,16},{48,32},{32,48},{80,64},{64,80},{112,96},{96,112},{1... | collective-permute-start | bytes 294920 | tf_op jit(solution)/shard_map/ppermute | solution.py:341
  12.5 1.5 %collective-permute-start.4 = (bf16[64,768]{1,0:T(8,128)(2,1)S(1)}, bf16[64,768]{1,0:T(8,128)(2,1)S(1)}, u32[]{:S(2)}, u32[]{:S(2)}) collective-permute-start(bf16[64,768]{1,0:T(8,128)(2,1)S(1)} %collective-permute-done.refs_1_), channel_id=1, source_target_pairs={{16,0},{0,16},{48,32},{32,48},{80,64},{64,80},{112,96},{96,112},{1... | collective-permute-start | bytes 294920 | tf_op jit(solution)/shard_map/ppermute | solution.py:341
  44.4 7.9 %collective-permute-start.7 = (bf16[128,512]{1,0:T(8,128)(2,1)S(1)}, bf16[128,512]{1,0:T(8,128)(2,1)S(1)}, u32[]{:S(2)}, u32[]{:S(2)}) collective-permute-start(bf16[128,512]{1,0:T(8,128)(2,1)S(1)} %get-tuple-element.14), channel_id=1, source_target_pairs={{0,2},{1,3},{2,0},{3,1},{4,6},{5,7},{6,4},{7,5},{8,10},{9,11},{10,... | collective-permute-start | bytes 393224 | tf_op jit(solution)/shard_map/ppermute | solution.py:346
  47.7 7.2 %collective-permute-start.8 = (bf16[128,512]{1,0:T(8,128)(2,1)S(1)}, bf16[128,512]{1,0:T(8,128)(2,1)S(1)}, u32[]{:S(2)}, u32[]{:S(2)}) collective-permute-start(bf16[128,512]{1,0:T(8,128)(2,1)S(1)} %get-tuple-element.15), channel_id=1, source_target_pairs={{0,1},{1,0},{2,3},{3,2},{4,5},{5,4},{6,7},{7,6},{8,9},{9,8},{10,11... | collective-permute-start | bytes 393224 | tf_op jit(solution)/shard_map/ppermute | solution.py:346
  48.4 6.6 %collective-permute-start.9 = (bf16[128,512]{1,0:T(8,128)(2,1)S(1)}, bf16[128,512]{1,0:T(8,128)(2,1)S(1)}, u32[]{:S(2)}, u32[]{:S(2)}) collective-permute-start(bf16[128,512]{1,0:T(8,128)(2,1)S(1)} %get-tuple-element.16), channel_id=1, source_target_pairs={{0,3},{1,2},{2,1},{3,0},{4,7},{5,6},{6,5},{7,4},{8,11},{9,10},{10,... | collective-permute-start | bytes 393224 | tf_op jit(solution)/shard_map/ppermute | solution.py:346
  55.1 5.8 %collective-permute-start.10 = (bf16[32,512]{1,0:T(8,128)(2,1)S(1)}, bf16[32,512]{1,0:T(8,128)(2,1)S(1)}, u32[]{:S(2)}, u32[]{:S(2)}) collective-permute-start(bf16[32,512]{1,0:T(8,128)(2,1)S(1)} %get-tuple-element.19), channel_id=1, source_target_pairs={{0,8},{1,9},{2,10},{3,11},{4,12},{5,13},{6,14},{7,15},{8,0},{9,1},... | collective-permute-start | bytes 98312 | tf_op jit(solution)/shard_map/ppermute | solution.py:346
  59.0 5.1 %collective-permute-start.12 = (bf16[32,512]{1,0:T(8,128)(2,1)S(1)}, bf16[32,512]{1,0:T(8,128)(2,1)S(1)}, u32[]{:S(2)}, u32[]{:S(2)}) collective-permute-start(bf16[32,512]{1,0:T(8,128)(2,1)S(1)} %get-tuple-element.20), channel_id=1, source_target_pairs={{0,12},{1,13},{2,14},{3,15},{4,8},{5,9},{6,10},{7,11},{8,4},{9,5},... | collective-permute-start | bytes 98312 | tf_op jit(solution)/shard_map/ppermute | solution.py:346
  59.8 4.4 %collective-permute-start.11 = (bf16[32,512]{1,0:T(8,128)(2,1)S(1)}, bf16[32,512]{1,0:T(8,128)(2,1)S(1)}, u32[]{:S(2)}, u32[]{:S(2)}) collective-permute-start(bf16[32,512]{1,0:T(8,128)(2,1)S(1)} %get-tuple-element.21), channel_id=1, source_target_pairs={{0,4},{1,5},{2,6},{3,7},{4,0},{5,1},{6,2},{7,3},{8,12},{9,13},{10,... | collective-permute-start | bytes 98312 | tf_op jit(solution)/shard_map/ppermute | solution.py:346

commit v6 on v5

--- a/solution.py
+++ b/solution.py
@@ -206,28 +206,38 @@
                     64 * m : 64 * m + 64, 128 * e : 128 * e + 128
                 ]
 
-    def align(c):
-        move = moveouts_ref[c]
-        move1 = jnp.right_shift(move, 3)
-        move0 = jnp.bitwise_and(move, 7)
-        turn = jnp.bitwise_and(8 - move0, 7)
-        near = sub < 8 - move0
-        whole = f8[c]
-        x = [pltpu.roll(whole[:, 128 * i : 128 * i + 128], turn, 0) for i in range(5)]
-        y0 = shift_left(x, move1, lane)
-        y1 = shift_static(y0, 1, lane)
-        y2 = shift_static(y1, 1, lane)
-        a = [jnp.where(near, p, q) for p, q in zip(y0, y1)]
-        nxt = [jnp.where(near, p, q) for p, q in zip(y1, y2)]
-        a_ref[c] = jnp.concatenate(
-            [jnp.concatenate([p, q], axis=0) for p, q in zip(a, nxt)], axis=1
-        ).astype(BF)
-        return jnp.concatenate(a, axis=1)
+    lane16 = lane_iota((16, 128))
+
+    def align(first_channel):
+        base, nears = [], []
+        for c in (first_channel, first_channel + 1):
+            move = moveouts_ref[c]
+            move1 = jnp.right_shift(move, 3)
+            move0 = jnp.bitwise_and(move, 7)
+            turn = jnp.bitwise_and(8 - move0, 7)
+            nears.append(sub < 8 - move0)
+            whole = f8[c]
+            x = [pltpu.roll(whole[:, 128 * i : 128 * i + 128], turn, 0) for i in range(5)]
+            base.append(shift_left(x, move1, lane))
+        y0 = [jnp.concatenate([p, q], axis=0) for p, q in zip(*base)]
+        y1 = shift_static([p.astype(BF) for p in y0], 1, lane16)
+        y2 = [p.astype(F32) for p in shift_static(y1, 1, lane16)]
+        y1 = [p.astype(F32) for p in y1]
+        both = []
+        for k in range(2):
+            rows8 = slice(8 * k, 8 * k + 8)
+            a = [jnp.where(nears[k], p, q[rows8]) for p, q in zip(base[k], y1)]
+            nxt = [jnp.where(nears[k], p[rows8], q[rows8]) for p, q in zip(y1, y2)]
+            a_ref[first_channel + k] = jnp.concatenate(
+                [jnp.concatenate([p, q], axis=0) for p, q in zip(a, nxt)], axis=1
+            ).astype(BF)
+            both.append(jnp.concatenate(a, axis=1))
+        return jnp.concatenate(both, axis=0)
 
     def first(i, carry):
         for e in range(0, GROUP, 2):
             c = GROUP * i + e
-            both = jnp.concatenate([align(c), align(c + 1)], axis=0)
+            both = align(c)
             square = both * both
             high = square.astype(BF)
             at = pl.ds(pl.multiple_of(8 * c, 16), 16)

time: 65.2 us -> 65.2 us (level)
  no operation moved by 1% of the time
where the time goes in v6:
time: 65.2 us; the launch traced here: 64.9 us
  Pallas kernels  33 us (51%)
  starting transfers between devices  15.8 us (24%)
  waiting for transfers between devices  12 us (18%)
  local copies, waits for them, and re-layouts  3.93 us (6%)
    pallas_call x1, Pallas kernels, shards(): pl.pallas_call(stack_kernel, out_shape=[jax.ShapeDtypeStruct((128, PH * c...  30.4 us
    ppermute x6, waiting for transfers between devices, swap(): lax.ppermute(value, 'chan', [(i, i ^ flip) for i in range(lax.axis_size('...  10.3 us
    ppermute x6, starting transfers between devices, swap(): lax.ppermute(value, 'chan', [(i, i ^ flip) for i in range(lax.axis_size('...  9.31 us
    ppermute x3, starting transfers between devices, gather_time(): lax.ppermute(white, 'tm', [((q + 2 * d) % 8, q) for q in range(8)])  5.81 us
    unnamed x16, local copies, waits for them, and re-layouts  3.12 us
    pallas_call x1, Pallas kernels, shards(): pl.pallas_call(setup_kernel, out_shape=[jax.ShapeDtypeStruct((1152, 1024)...  1.38 us
  transfers between devices with their start and end apart: 13, of which 7 were waited for; matrix products, arithmetic and copies ran while one was open for 0% of the time, Pallas kernels for 2%

profile of v6, /device:TPU:0, one launch (start us, length us, event | category | flops | bytes accessed | tf_op | source)
XLA Modules:
  0.0 64.9 jit_solution(8158806199451897671)
XLA Ops:
  0.0 0.0 copy-start
  0.0 0.9 %copy-done = f32[64,640]{1,0:T(8,128)S(1)} copy-done((f32[64,640]{1,0:T(8,128)S(1)}, f32[64,640]{1,0:T(8,128)}, u32[]{:S(2)}) %copy-start) | copy-done | bytes 163864
  0.9 0.0 copy-start.1
  0.9 0.7 %copy-done.1 = f32[64,16]{0,1:T(8,128)S(1)} copy-done((f32[64,16]{0,1:T(8,128)S(1)}, f32[64,16]{0,1:T(8,128)}, u32[]{:S(2)}) %copy-start.1) | copy-done | bytes 4120
  1.6 1.2 %shard_map.64.refs_0_ = bf16[64,768]{1,0:T(8,128)(2,1)S(1)} custom-call(f32[64,640]{1,0:T(8,128)S(1)} %copy-done, f32[16,64]{1,0:T(8,128)S(1)} %bitcast.4), custom_call_target="tpu_custom_call" | custom-call | tf_op jit(solution)/shard_map/pallas_call | solution.py:374
  2.8 0.1 collective-permute-start.3
  2.9 1.6 %collective-permute-start.2 = (bf16[64,768]{1,0:T(8,128)(2,1)S(1)}, bf16[64,768]{1,0:T(8,128)(2,1)S(1)}, u32[]{:S(2)}, u32[]{:S(2)}) collective-permute-start(bf16[64,768]{1,0:T(8,128)(2,1)S(1)} %shard_map.64.refs_0_), channel_id=1, source_target_pairs={{96,0},{112,16},{0,32},{16,48},{32,64},{48,80},{64,96},{80,112},{9... | collective-permute-start | bytes 294920 | tf_op jit(solution)/shard_map/ppermute | solution.py:350
  4.5 2.7 %collective-permute-start.1 = (bf16[64,768]{1,0:T(8,128)(2,1)S(1)}, bf16[64,768]{1,0:T(8,128)(2,1)S(1)}, u32[]{:S(2)}, u32[]{:S(2)}) collective-permute-start(bf16[64,768]{1,0:T(8,128)(2,1)S(1)} %shard_map.64.refs_0_), channel_id=1, source_target_pairs={{64,0},{80,16},{96,32},{112,48},{0,64},{16,80},{32,96},{48,112},{6... | collective-permute-start | bytes 294920 | tf_op jit(solution)/shard_map/ppermute | solution.py:350
  7.2 1.4 %collective-permute-start = (bf16[64,768]{1,0:T(8,128)(2,1)S(1)}, bf16[64,768]{1,0:T(8,128)(2,1)S(1)}, u32[]{:S(2)}, u32[]{:S(2)}) collective-permute-start(bf16[64,768]{1,0:T(8,128)(2,1)S(1)} %shard_map.64.refs_0_), channel_id=1, source_target_pairs={{32,0},{48,16},{64,32},{80,48},{96,64},{112,80},{0,96},{16,112},{3... | collective-permute-start | bytes 294920 | tf_op jit(solution)/shard_map/ppermute | solution.py:350
  8.7 0.0 copy-start.3
  8.7 0.8 %copy-done.3 = bf16[64,512]{1,0:T(8,128)(2,1)S(1)} copy-done((bf16[64,512]{1,0:T(8,128)(2,1)S(1)}, bf16[64,512]{1,0:T(8,128)(2,1)}, u32[]{:S(2)}) %copy-start.3) | copy-done | bytes 65560
  9.5 0.0 copy-start.6
  9.5 0.7 %copy-done.6 = bf16[113]{0:T(256)(128)(2,1)S(1)} copy-done((bf16[113]{0:T(256)(128)(2,1)S(1)}, bf16[113]{0:T(256)(128)(2,1)}, u32[]{:S(2)}) %copy-start.6) | copy-done | bytes 250
  10.2 0.0 copy-start.2
  10.2 0.0 copy-start.4
  10.2 0.0 copy-start.7
  10.2 1.4 %shard_map.65 = (bf16[1152,1024]{1,0:T(8,128)(2,1)S(1)}, bf16[512,512]{1,0:T(8,128)(2,1)S(1)}) custom-call(bf16[1,113]{1,0:T(2,128)(2,1)S(1)} %bitcast.6, bf16[64,512]{1,0:T(8,128)(2,1)S(1)} %copy-done.3), custom_call_target="tpu_custom_call" | custom-call | flops 2147483648 | bytes 4194304 | tf_op jit(solution)/shard_map/pallas_call | solution.py:382
  11.6 0.0 collective-permute-done.2.refs_3_
  11.6 0.1 collective-permute-start.6
  11.7 0.8 %collective-permute-done.1.refs_2_ = bf16[64,768]{1,0:T(8,128)(2,1)S(1)} collective-permute-done((bf16[64,768]{1,0:T(8,128)(2,1)S(1)}, bf16[64,768]{1,0:T(8,128)(2,1)S(1)}, u32[]{:S(2)}, u32[]{:S(2)}) %collective-permute-start.1) | collective-permute-done | bytes 98336 | tf_op jit(solution)/shard_map/ppermute | solution.py:350
  12.5 0.0 collective-permute-start.5
  12.5 0.0 collective-permute-done.refs_1_
  12.5 0.5 collective-permute-start.4
  13.0 0.1 pad_add_fusion.place_ref
  13.1 0.0 collective-permute-done.3.refs_4_
  13.1 0.0 collective-permute-done.6.refs_7_
  13.1 0.7 %collective-permute-done.5.refs_6_ = bf16[64,768]{1,0:T(8,128)(2,1)S(1)} collective-permute-done((bf16[64,768]{1,0:T(8,128)(2,1)S(1)}, bf16[64,768]{1,0:T(8,128)(2,1)S(1)}, u32[]{:S(2)}, u32[]{:S(2)}) %collective-permute-start.5) | collective-permute-done | bytes 98336 | tf_op jit(solution)/shard_map/ppermute | solution.py:351
  13.8 0.2 collective-permute-done.4.refs_5_
  13.9 0.0 copy-done.2
  13.9 0.0 copy-done.4
  13.9 0.0 copy-done.5
  13.9 0.0 copy-done.7
  13.9 30.4 %shard_map.66 = (f32[128,512]{1,0:T(8,128)S(1)}, bf16[128,512]{1,0:T(8,128)(2,1)S(1)}, bf16[128,512]{1,0:T(8,128)(2,1)S(1)}, bf16[128,512]{1,0:T(8,128)(2,1)S(1)}) custom-call(s32[2]{0:T(128)S(1)} %pad_add_fusion.place_ref, s32[64]{0:T(128)S(1)} %copy-done.7, bf16[64,768]{1,0:T(8,128)(2,1)S(1)} %shard_map.64.refs_0_, ...), custom_call_target="tpu_custom_call" | custom-call | flops 17179869184 | bytes 8388608 | tf_op jit(solution)/shard_map/pallas_call | solution.py:395
  44.4 3.3 %collective-permute-start.7 = (bf16[128,512]{1,0:T(8,128)(2,1)S(1)}, bf16[128,512]{1,0:T(8,128)(2,1)S(1)}, u32[]{:S(2)}, u32[]{:S(2)}) collective-permute-start(bf16[128,512]{1,0:T(8,128)(2,1)S(1)} %get-tuple-element.14), channel_id=1, source_target_pairs={{0,2},{1,3},{2,0},{3,1},{4,6},{5,7},{6,4},{7,5},{8,10},{9,11},{10,... | collective-permute-start | bytes 393224 | tf_op jit(solution)/shard_map/ppermute | solution.py:356
  47.7 0.7 %collective-permute-start.8 = (bf16[128,512]{1,0:T(8,128)(2,1)S(1)}, bf16[128,512]{1,0:T(8,128)(2,1)S(1)}, u32[]{:S(2)}, u32[]{:S(2)}) collective-permute-start(bf16[128,512]{1,0:T(8,128)(2,1)S(1)} %get-tuple-element.15), channel_id=1, source_target_pairs={{0,1},{1,0},{2,3},{3,2},{4,5},{5,4},{6,7},{7,6},{8,9},{9,8},{10,11... | collective-permute-start | bytes 393224 | tf_op jit(solution)/shard_map/ppermute | solution.py:356
  48.4 0.4 collective-permute-start.9
  48.7 3.6 %collective-permute-done.7 = bf16[128,512]{1,0:T(8,128)(2,1)S(1)} collective-permute-done((bf16[128,512]{1,0:T(8,128)(2,1)S(1)}, bf16[128,512]{1,0:T(8,128)(2,1)S(1)}, u32[]{:S(2)}, u32[]{:S(2)}) %collective-permute-start.7) | collective-permute-done | bytes 131104 | tf_op jit(solution)/shard_map/ppermute | solution.py:356
  52.3 2.6 %collective-permute-done.8 = bf16[128,512]{1,0:T(8,128)(2,1)S(1)} collective-permute-done((bf16[128,512]{1,0:T(8,128)(2,1)S(1)}, bf16[128,512]{1,0:T(8,128)(2,1)S(1)}, u32[]{:S(2)}, u32[]{:S(2)}) %collective-permute-start.8) | collective-permute-done | bytes 131104 | tf_op jit(solution)/shard_map/ppermute | solution.py:356
  54.9 0.0 collective-permute-done.9
  54.9 0.1 fusion.2
  55.0 4.0 %collective-permute-start.10 = (bf16[32,512]{1,0:T(8,128)(2,1)S(1)}, bf16[32,512]{1,0:T(8,128)(2,1)S(1)}, u32[]{:S(2)}, u32[]{:S(2)}) collective-permute-start(bf16[32,512]{1,0:T(8,128)(2,1)S(1)} %get-tuple-element.19), channel_id=1, source_target_pairs={{0,8},{1,9},{2,10},{3,11},{4,12},{5,13},{6,14},{7,15},{8,0},{9,1},... | collective-permute-start | bytes 98312 | tf_op jit(solution)/shard_map/ppermute | solution.py:356
  59.0 0.7 %collective-permute-start.12 = (bf16[32,512]{1,0:T(8,128)(2,1)S(1)}, bf16[32,512]{1,0:T(8,128)(2,1)S(1)}, u32[]{:S(2)}, u32[]{:S(2)}) collective-permute-start(bf16[32,512]{1,0:T(8,128)(2,1)S(1)} %get-tuple-element.20), channel_id=1, source_target_pairs={{0,12},{1,13},{2,14},{3,15},{4,8},{5,9},{6,10},{7,11},{8,4},{9,5},... | collective-permute-start | bytes 98312 | tf_op jit(solution)/shard_map/ppermute | solution.py:356
  59.7 0.3 collective-permute-start.11
  60.0 0.9 %collective-permute-done.10 = bf16[32,512]{1,0:T(8,128)(2,1)S(1)} collective-permute-done((bf16[32,512]{1,0:T(8,128)(2,1)S(1)}, bf16[32,512]{1,0:T(8,128)(2,1)S(1)}, u32[]{:S(2)}, u32[]{:S(2)}) %collective-permute-start.10) | collective-permute-done | bytes 32800 | tf_op jit(solution)/shard_map/ppermute | solution.py:356
  60.9 3.2 %collective-permute-done.12 = bf16[32,512]{1,0:T(8,128)(2,1)S(1)} collective-permute-done((bf16[32,512]{1,0:T(8,128)(2,1)S(1)}, bf16[32,512]{1,0:T(8,128)(2,1)S(1)}, u32[]{:S(2)}, u32[]{:S(2)}) %collective-permute-start.12) | collective-permute-done | bytes 32800 | tf_op jit(solution)/shard_map/ppermute | solution.py:356
  64.1 0.0 collective-permute-done.11
  64.1 0.1 reshape.7
  64.2 0.7 %copy.8 = f32[256,64]{0,1:T(8,128)} copy(f32[256,64]{1,0:T(8,128)S(1)} %reshape.7) | data formatting | bytes 131072 | tf_op jit(solution)/shard_map/reshape | solution.py:425
  (3 shorter events, 0.0 us)
Async XLA Ops:
  0.0 0.9 %copy-start = (f32[64,640]{1,0:T(8,128)S(1)}, f32[64,640]{1,0:T(8,128)}, u32[]{:S(2)}) copy-start(f32[64,640]{1,0:T(8,128)} %raw_ref.1) | copy-start | bytes 491524
  0.9 0.7 %copy-start.1 = (f32[64,16]{0,1:T(8,128)S(1)}, f32[64,16]{0,1:T(8,128)}, u32[]{:S(2)}) copy-start(f32[64,16]{0,1:T(8,128)} %param.7) | copy-start | bytes 12292
  2.8 10.3 %collective-permute-start.3 = (bf16[64,768]{1,0:T(8,128)(2,1)S(1)}, bf16[64,768]{1,0:T(8,128)(2,1)S(1)}, u32[]{:S(2)}, u32[]{:S(2)}) collective-permute-start(bf16[64,768]{1,0:T(8,128)(2,1)S(1)} %shard_map.64.refs_0_), channel_id=1, source_target_pairs={{16,0},{0,16},{48,32},{32,48},{80,64},{64,80},{112,96},{96,112},{1... | collective-permute-start | bytes 294920 | tf_op jit(solution)/shard_map/ppermute | solution.py:351
  2.9 8.7 %collective-permute-start.2 = (bf16[64,768]{1,0:T(8,128)(2,1)S(1)}, bf16[64,768]{1,0:T(8,128)(2,1)S(1)}, u32[]{:S(2)}, u32[]{:S(2)}) collective-permute-start(bf16[64,768]{1,0:T(8,128)(2,1)S(1)} %shard_map.64.refs_0_), channel_id=1, source_target_pairs={{96,0},{112,16},{0,32},{16,48},{32,64},{48,80},{64,96},{80,112},{9... | collective-permute-start | bytes 294920 | tf_op jit(solution)/shard_map/ppermute | solution.py:350
  4.5 8.0 %collective-permute-start.1 = (bf16[64,768]{1,0:T(8,128)(2,1)S(1)}, bf16[64,768]{1,0:T(8,128)(2,1)S(1)}, u32[]{:S(2)}, u32[]{:S(2)}) collective-permute-start(bf16[64,768]{1,0:T(8,128)(2,1)S(1)} %shard_map.64.refs_0_), channel_id=1, source_target_pairs={{64,0},{80,16},{96,32},{112,48},{0,64},{16,80},{32,96},{48,112},{6... | collective-permute-start | bytes 294920 | tf_op jit(solution)/shard_map/ppermute | solution.py:350
  7.2 5.2 %collective-permute-start = (bf16[64,768]{1,0:T(8,128)(2,1)S(1)}, bf16[64,768]{1,0:T(8,128)(2,1)S(1)}, u32[]{:S(2)}, u32[]{:S(2)}) collective-permute-start(bf16[64,768]{1,0:T(8,128)(2,1)S(1)} %shard_map.64.refs_0_), channel_id=1, source_target_pairs={{32,0},{48,16},{64,32},{80,48},{96,64},{112,80},{0,96},{16,112},{3... | collective-permute-start | bytes 294920 | tf_op jit(solution)/shard_map/ppermute | solution.py:350
  8.7 0.8 %copy-start.3 = (bf16[64,512]{1,0:T(8,128)(2,1)S(1)}, bf16[64,512]{1,0:T(8,128)(2,1)}, u32[]{:S(2)}) copy-start(bf16[64,512]{1,0:T(8,128)(2,1)} %refs_8_.1) | copy-start | bytes 196612
  9.5 0.7 %copy-start.6 = (bf16[113]{0:T(256)(128)(2,1)S(1)}, bf16[113]{0:T(256)(128)(2,1)}, u32[]{:S(2)}) copy-start(bf16[113]{0:T(256)(128)(2,1)} %param.8) | copy-start | bytes 682
  10.2 3.8 %copy-start.2 = (f32[64,16]{0,1:T(8,128)S(1)}, f32[64,16]{0,1:T(8,128)}, u32[]{:S(2)}) copy-start(f32[64,16]{0,1:T(8,128)} %param.7) | copy-start | bytes 12292
  10.2 3.8 %copy-start.4 = (bf16[64,512]{1,0:T(8,128)(2,1)S(1)}, bf16[64,512]{1,0:T(8,128)(2,1)}, u32[]{:S(2)}) copy-start(bf16[64,512]{1,0:T(8,128)(2,1)} %refs_8_.1) | copy-start | bytes 196612
  10.2 3.8 %copy-start.5 = (s32[64,64]{1,0:T(8,128)S(1)}, s32[64,64]{1,0:T(8,128)}, u32[]{:S(2)}) copy-start(s32[64,64]{1,0:T(8,128)} %refs_9_.1) | copy-start | bytes 49156
  10.2 3.8 %copy-start.7 = (s32[64]{0:T(128)S(1)}, s32[64]{0:T(128)}, u32[]{:S(2)}) copy-start(s32[64]{0:T(128)} %moveouts_ref.1) | copy-start | bytes 772
  11.6 1.5 %collective-permute-start.6 = (bf16[64,768]{1,0:T(8,128)(2,1)S(1)}, bf16[64,768]{1,0:T(8,128)(2,1)S(1)}, u32[]{:S(2)}, u32[]{:S(2)}) collective-permute-start(bf16[64,768]{1,0:T(8,128)(2,1)S(1)} %collective-permute-done.2.refs_3_), channel_id=1, source_target_pairs={{16,0},{0,16},{48,32},{32,48},{80,64},{64,80},{112,96},{96,112},{1... | collective-permute-start | bytes 294920 | tf_op jit(solution)/shard_map/ppermute | solution.py:351
  12.5 1.3 %collective-permute-start.5 = (bf16[64,768]{1,0:T(8,128)(2,1)S(1)}, bf16[64,768]{1,0:T(8,128)(2,1)S(1)}, u32[]{:S(2)}, u32[]{:S(2)}) collective-permute-start(bf16[64,768]{1,0:T(8,128)(2,1)S(1)} %collective-permute-done.1.refs_2_), channel_id=1, source_target_pairs={{16,0},{0,16},{48,32},{32,48},{80,64},{64,80},{112,96},{96,112},{1... | collective-permute-start | bytes 294920 | tf_op jit(solution)/shard_map/ppermute | solution.py:351
  12.5 1.5 %collective-permute-start.4 = (bf16[64,768]{1,0:T(8,128)(2,1)S(1)}, bf16[64,768]{1,0:T(8,128)(2,1)S(1)}, u32[]{:S(2)}, u32[]{:S(2)}) collective-permute-start(bf16[64,768]{1,0:T(8,128)(2,1)S(1)} %collective-permute-done.refs_1_), channel_id=1, source_target_pairs={{16,0},{0,16},{48,32},{32,48},{80,64},{64,80},{112,96},{96,112},{1... | collective-permute-start | bytes 294920 | tf_op jit(solution)/shard_map/ppermute | solution.py:351
  44.4 7.9 %collective-permute-start.7 = (bf16[128,512]{1,0:T(8,128)(2,1)S(1)}, bf16[128,512]{1,0:T(8,128)(2,1)S(1)}, u32[]{:S(2)}, u32[]{:S(2)}) collective-permute-start(bf16[128,512]{1,0:T(8,128)(2,1)S(1)} %get-tuple-element.14), channel_id=1, source_target_pairs={{0,2},{1,3},{2,0},{3,1},{4,6},{5,7},{6,4},{7,5},{8,10},{9,11},{10,... | collective-permute-start | bytes 393224 | tf_op jit(solution)/shard_map/ppermute | solution.py:356
  47.7 7.2 %collective-permute-start.8 = (bf16[128,512]{1,0:T(8,128)(2,1)S(1)}, bf16[128,512]{1,0:T(8,128)(2,1)S(1)}, u32[]{:S(2)}, u32[]{:S(2)}) collective-permute-start(bf16[128,512]{1,0:T(8,128)(2,1)S(1)} %get-tuple-element.15), channel_id=1, source_target_pairs={{0,1},{1,0},{2,3},{3,2},{4,5},{5,4},{6,7},{7,6},{8,9},{9,8},{10,11... | collective-permute-start | bytes 393224 | tf_op jit(solution)/shard_map/ppermute | solution.py:356
  48.4 6.6 %collective-permute-start.9 = (bf16[128,512]{1,0:T(8,128)(2,1)S(1)}, bf16[128,512]{1,0:T(8,128)(2,1)S(1)}, u32[]{:S(2)}, u32[]{:S(2)}) collective-permute-start(bf16[128,512]{1,0:T(8,128)(2,1)S(1)} %get-tuple-element.16), channel_id=1, source_target_pairs={{0,3},{1,2},{2,1},{3,0},{4,7},{5,6},{6,5},{7,4},{8,11},{9,10},{10,... | collective-permute-start | bytes 393224 | tf_op jit(solution)/shard_map/ppermute | solution.py:356
  55.0 5.8 %collective-permute-start.10 = (bf16[32,512]{1,0:T(8,128)(2,1)S(1)}, bf16[32,512]{1,0:T(8,128)(2,1)S(1)}, u32[]{:S(2)}, u32[]{:S(2)}) collective-permute-start(bf16[32,512]{1,0:T(8,128)(2,1)S(1)} %get-tuple-element.19), channel_id=1, source_target_pairs={{0,8},{1,9},{2,10},{3,11},{4,12},{5,13},{6,14},{7,15},{8,0},{9,1},... | collective-permute-start | bytes 98312 | tf_op jit(solution)/shard_map/ppermute | solution.py:356
  59.0 5.1 %collective-permute-start.12 = (bf16[32,512]{1,0:T(8,128)(2,1)S(1)}, bf16[32,512]{1,0:T(8,128)(2,1)S(1)}, u32[]{:S(2)}, u32[]{:S(2)}) collective-permute-start(bf16[32,512]{1,0:T(8,128)(2,1)S(1)} %get-tuple-element.20), channel_id=1, source_target_pairs={{0,12},{1,13},{2,14},{3,15},{4,8},{5,9},{6,10},{7,11},{8,4},{9,5},... | collective-permute-start | bytes 98312 | tf_op jit(solution)/shard_map/ppermute | solution.py:356
  59.7 4.4 %collective-permute-start.11 = (bf16[32,512]{1,0:T(8,128)(2,1)S(1)}, bf16[32,512]{1,0:T(8,128)(2,1)S(1)}, u32[]{:S(2)}, u32[]{:S(2)}) collective-permute-start(bf16[32,512]{1,0:T(8,128)(2,1)S(1)} %get-tuple-element.21), channel_id=1, source_target_pairs={{0,4},{1,5},{2,6},{3,7},{4,0},{5,1},{6,2},{7,3},{8,12},{9,13},{10,... | collective-permute-start | bytes 98312 | tf_op jit(solution)/shard_map/ppermute | solution.py:356

commit v7 on v5

--- a/solution.py
+++ b/solution.py
@@ -10,7 +10,7 @@
 EPSILON = 1e-06
 GROUP = 8
 UNROLL = 8
-FIRST = (2, 1, 3)
+FIRST = (1, 3, 2)
 SECOND = (8, 4, 12)
 PH = 8
 HALO = 128

time: 65.2 us -> 65.8 us (level)
  transfers between devices with their start and end apart: 13 -> 13, of which waited for: 7 -> 8; matrix products, arithmetic and copies ran while one was open for 0% -> 0% of each run, Pallas kernels for 2% -> 2%
where the time goes in v7:
time: 65.8 us; the launch traced here: 65.6 us
  Pallas kernels  33 us (50%)
  starting transfers between devices  16 us (24%)
  waiting for transfers between devices  12.3 us (19%)
  local copies, waits for them, and re-layouts  3.93 us (6%)
    pallas_call x1, Pallas kernels, shards(): pl.pallas_call(stack_kernel, out_shape=[jax.ShapeDtypeStruct((128, PH * c...  30.5 us
    ppermute x6, waiting for transfers between devices, swap(): lax.ppermute(value, 'chan', [(i, i ^ flip) for i in range(lax.axis_size('...  10.7 us
    ppermute x6, starting transfers between devices, swap(): lax.ppermute(value, 'chan', [(i, i ^ flip) for i in range(lax.axis_size('...  9.56 us
    ppermute x3, starting transfers between devices, gather_time(): lax.ppermute(white, 'tm', [((q + 2 * d) % 8, q) for q in range(8)])  5.81 us
    unnamed x16, local copies, waits for them, and re-layouts  3.12 us
    pallas_call x1, Pallas kernels, shards(): pl.pallas_call(setup_kernel, out_shape=[jax.ShapeDtypeStruct((1152, 1024)...  1.38 us
  transfers between devices with their start and end apart: 13, of which 8 were waited for; matrix products, arithmetic and copies ran while one was open for 0% of the time, Pallas kernels for 2%

profile of v7, /device:TPU:0, one launch (start us, length us, event | category | flops | bytes accessed | tf_op | source)
XLA Modules:
  0.0 65.6 jit_solution(11579429392567025366)
XLA Ops:
  0.0 0.0 copy-start
  0.0 0.9 %copy-done = f32[64,640]{1,0:T(8,128)S(1)} copy-done((f32[64,640]{1,0:T(8,128)S(1)}, f32[64,640]{1,0:T(8,128)}, u32[]{:S(2)}) %copy-start) | copy-done | bytes 163864
  0.9 0.0 copy-start.1
  0.9 0.7 %copy-done.1 = f32[64,16]{0,1:T(8,128)S(1)} copy-done((f32[64,16]{0,1:T(8,128)S(1)}, f32[64,16]{0,1:T(8,128)}, u32[]{:S(2)}) %copy-start.1) | copy-done | bytes 4120
  1.6 1.2 %shard_map.64.refs_0_ = bf16[64,768]{1,0:T(8,128)(2,1)S(1)} custom-call(f32[64,640]{1,0:T(8,128)S(1)} %copy-done, f32[16,64]{1,0:T(8,128)S(1)} %bitcast.4), custom_call_target="tpu_custom_call" | custom-call | tf_op jit(solution)/shard_map/pallas_call | solution.py:364
  2.8 0.1 collective-permute-start.3
  2.9 1.6 %collective-permute-start.2 = (bf16[64,768]{1,0:T(8,128)(2,1)S(1)}, bf16[64,768]{1,0:T(8,128)(2,1)S(1)}, u32[]{:S(2)}, u32[]{:S(2)}) collective-permute-start(bf16[64,768]{1,0:T(8,128)(2,1)S(1)} %shard_map.64.refs_0_), channel_id=1, source_target_pairs={{96,0},{112,16},{0,32},{16,48},{32,64},{48,80},{64,96},{80,112},{9... | collective-permute-start | bytes 294920 | tf_op jit(solution)/shard_map/ppermute | solution.py:340
  4.5 2.7 %collective-permute-start.1 = (bf16[64,768]{1,0:T(8,128)(2,1)S(1)}, bf16[64,768]{1,0:T(8,128)(2,1)S(1)}, u32[]{:S(2)}, u32[]{:S(2)}) collective-permute-start(bf16[64,768]{1,0:T(8,128)(2,1)S(1)} %shard_map.64.refs_0_), channel_id=1, source_target_pairs={{64,0},{80,16},{96,32},{112,48},{0,64},{16,80},{32,96},{48,112},{6... | collective-permute-start | bytes 294920 | tf_op jit(solution)/shard_map/ppermute | solution.py:340
  7.2 1.4 %collective-permute-start = (bf16[64,768]{1,0:T(8,128)(2,1)S(1)}, bf16[64,768]{1,0:T(8,128)(2,1)S(1)}, u32[]{:S(2)}, u32[]{:S(2)}) collective-permute-start(bf16[64,768]{1,0:T(8,128)(2,1)S(1)} %shard_map.64.refs_0_), channel_id=1, source_target_pairs={{32,0},{48,16},{64,32},{80,48},{96,64},{112,80},{0,96},{16,112},{3... | collective-permute-start | bytes 294920 | tf_op jit(solution)/shard_map/ppermute | solution.py:340
  8.7 0.0 copy-start.3
  8.7 0.8 %copy-done.3 = bf16[64,512]{1,0:T(8,128)(2,1)S(1)} copy-done((bf16[64,512]{1,0:T(8,128)(2,1)S(1)}, bf16[64,512]{1,0:T(8,128)(2,1)}, u32[]{:S(2)}) %copy-start.3) | copy-done | bytes 65560
  9.5 0.0 copy-start.6
  9.5 0.7 copy-done.6
  10.2 0.0 copy-start.2
  10.2 0.0 copy-start.4
  10.2 0.0 copy-start.5
  10.2 1.4 %shard_map.65 = (bf16[1152,1024]{1,0:T(8,128)(2,1)S(1)}, bf16[512,512]{1,0:T(8,128)(2,1)S(1)}) custom-call(bf16[1,113]{1,0:T(2,128)(2,1)S(1)} %bitcast.6, bf16[64,512]{1,0:T(8,128)(2,1)S(1)} %copy-done.3), custom_call_target="tpu_custom_call" | custom-call | flops 2147483648 | bytes 4194304 | tf_op jit(solution)/shard_map/pallas_call | solution.py:372
  11.6 0.0 collective-permute-done.2.refs_3_
  11.6 0.1 collective-permute-start.6
  11.7 0.8 %collective-permute-done.1.refs_2_ = bf16[64,768]{1,0:T(8,128)(2,1)S(1)} collective-permute-done((bf16[64,768]{1,0:T(8,128)(2,1)S(1)}, bf16[64,768]{1,0:T(8,128)(2,1)S(1)}, u32[]{:S(2)}, u32[]{:S(2)}) %collective-permute-start.1) | collective-permute-done | bytes 98336 | tf_op jit(solution)/shard_map/ppermute | solution.py:340
  12.5 0.0 collective-permute-start.5
  12.5 0.0 collective-permute-done.refs_1_
  12.5 0.5 collective-permute-start.4
  13.0 0.1 pad_add_fusion.place_ref
  13.1 0.0 collective-permute-done.3.refs_4_
  13.1 0.0 collective-permute-done.6.refs_7_
  13.1 0.7 %collective-permute-done.5.refs_6_ = bf16[64,768]{1,0:T(8,128)(2,1)S(1)} collective-permute-done((bf16[64,768]{1,0:T(8,128)(2,1)S(1)}, bf16[64,768]{1,0:T(8,128)(2,1)S(1)}, u32[]{:S(2)}, u32[]{:S(2)}) %collective-permute-start.5) | collective-permute-done | bytes 98336 | tf_op jit(solution)/shard_map/ppermute | solution.py:341
  13.8 0.2 collective-permute-done.4.refs_5_
  13.9 0.0 copy-done.2
  13.9 0.0 copy-done.4
  13.9 0.0 copy-done.5
  13.9 0.0 copy-done.7
  13.9 30.5 %shard_map.66 = (f32[128,512]{1,0:T(8,128)S(1)}, bf16[128,512]{1,0:T(8,128)(2,1)S(1)}, bf16[128,512]{1,0:T(8,128)(2,1)S(1)}, bf16[128,512]{1,0:T(8,128)(2,1)S(1)}) custom-call(s32[2]{0:T(128)S(1)} %pad_add_fusion.place_ref, s32[64]{0:T(128)S(1)} %copy-done.7, bf16[64,768]{1,0:T(8,128)(2,1)S(1)} %shard_map.64.refs_0_, ...), custom_call_target="tpu_custom_call" | custom-call | flops 17179869184 | bytes 8388608 | tf_op jit(solution)/shard_map/pallas_call | solution.py:385
  44.4 1.7 %collective-permute-start.7 = (bf16[128,512]{1,0:T(8,128)(2,1)S(1)}, bf16[128,512]{1,0:T(8,128)(2,1)S(1)}, u32[]{:S(2)}, u32[]{:S(2)}) collective-permute-start(bf16[128,512]{1,0:T(8,128)(2,1)S(1)} %get-tuple-element.14), channel_id=1, source_target_pairs={{0,1},{1,0},{2,3},{3,2},{4,5},{5,4},{6,7},{7,6},{8,9},{9,8},{10,11... | collective-permute-start | bytes 393224 | tf_op jit(solution)/shard_map/ppermute | solution.py:346
  46.1 2.2 %collective-permute-start.8 = (bf16[128,512]{1,0:T(8,128)(2,1)S(1)}, bf16[128,512]{1,0:T(8,128)(2,1)S(1)}, u32[]{:S(2)}, u32[]{:S(2)}) collective-permute-start(bf16[128,512]{1,0:T(8,128)(2,1)S(1)} %get-tuple-element.15), channel_id=1, source_target_pairs={{0,3},{1,2},{2,1},{3,0},{4,7},{5,6},{6,5},{7,4},{8,11},{9,10},{10,... | collective-permute-start | bytes 393224 | tf_op jit(solution)/shard_map/ppermute | solution.py:346
  48.3 0.7 %collective-permute-start.9 = (bf16[128,512]{1,0:T(8,128)(2,1)S(1)}, bf16[128,512]{1,0:T(8,128)(2,1)S(1)}, u32[]{:S(2)}, u32[]{:S(2)}) collective-permute-start(bf16[128,512]{1,0:T(8,128)(2,1)S(1)} %get-tuple-element.16), channel_id=1, source_target_pairs={{0,2},{1,3},{2,0},{3,1},{4,6},{5,7},{6,4},{7,5},{8,10},{9,11},{10,... | collective-permute-start | bytes 393224 | tf_op jit(solution)/shard_map/ppermute | solution.py:346
  49.0 1.3 %collective-permute-done.7 = bf16[128,512]{1,0:T(8,128)(2,1)S(1)} collective-permute-done((bf16[128,512]{1,0:T(8,128)(2,1)S(1)}, bf16[128,512]{1,0:T(8,128)(2,1)S(1)}, u32[]{:S(2)}, u32[]{:S(2)}) %collective-permute-start.7) | collective-permute-done | bytes 131104 | tf_op jit(solution)/shard_map/ppermute | solution.py:346
  50.3 3.8 %collective-permute-done.8 = bf16[128,512]{1,0:T(8,128)(2,1)S(1)} collective-permute-done((bf16[128,512]{1,0:T(8,128)(2,1)S(1)}, bf16[128,512]{1,0:T(8,128)(2,1)S(1)}, u32[]{:S(2)}, u32[]{:S(2)}) %collective-permute-start.8) | collective-permute-done | bytes 131104 | tf_op jit(solution)/shard_map/ppermute | solution.py:346
  54.1 1.5 %collective-permute-done.9 = bf16[128,512]{1,0:T(8,128)(2,1)S(1)} collective-permute-done((bf16[128,512]{1,0:T(8,128)(2,1)S(1)}, bf16[128,512]{1,0:T(8,128)(2,1)S(1)}, u32[]{:S(2)}, u32[]{:S(2)}) %collective-permute-start.9) | collective-permute-done | bytes 131104 | tf_op jit(solution)/shard_map/ppermute | solution.py:346
  55.6 0.1 fusion.2
  55.7 4.0 %collective-permute-start.10 = (bf16[32,512]{1,0:T(8,128)(2,1)S(1)}, bf16[32,512]{1,0:T(8,128)(2,1)S(1)}, u32[]{:S(2)}, u32[]{:S(2)}) collective-permute-start(bf16[32,512]{1,0:T(8,128)(2,1)S(1)} %get-tuple-element.19), channel_id=1, source_target_pairs={{0,8},{1,9},{2,10},{3,11},{4,12},{5,13},{6,14},{7,15},{8,0},{9,1},... | collective-permute-start | bytes 98312 | tf_op jit(solution)/shard_map/ppermute | solution.py:346
  59.7 0.7 %collective-permute-start.12 = (bf16[32,512]{1,0:T(8,128)(2,1)S(1)}, bf16[32,512]{1,0:T(8,128)(2,1)S(1)}, u32[]{:S(2)}, u32[]{:S(2)}) collective-permute-start(bf16[32,512]{1,0:T(8,128)(2,1)S(1)} %get-tuple-element.20), channel_id=1, source_target_pairs={{0,12},{1,13},{2,14},{3,15},{4,8},{5,9},{6,10},{7,11},{8,4},{9,5},... | collective-permute-start | bytes 98312 | tf_op jit(solution)/shard_map/ppermute | solution.py:346
  60.4 0.3 collective-permute-start.11
  60.7 0.9 %collective-permute-done.10 = bf16[32,512]{1,0:T(8,128)(2,1)S(1)} collective-permute-done((bf16[32,512]{1,0:T(8,128)(2,1)S(1)}, bf16[32,512]{1,0:T(8,128)(2,1)S(1)}, u32[]{:S(2)}, u32[]{:S(2)}) %collective-permute-start.10) | collective-permute-done | bytes 32800 | tf_op jit(solution)/shard_map/ppermute | solution.py:346
  61.5 3.2 %collective-permute-done.12 = bf16[32,512]{1,0:T(8,128)(2,1)S(1)} collective-permute-done((bf16[32,512]{1,0:T(8,128)(2,1)S(1)}, bf16[32,512]{1,0:T(8,128)(2,1)S(1)}, u32[]{:S(2)}, u32[]{:S(2)}) %collective-permute-start.12) | collective-permute-done | bytes 32800 | tf_op jit(solution)/shard_map/ppermute | solution.py:346
  64.8 0.0 collective-permute-done.11
  64.8 0.1 reshape.7
  64.9 0.7 %copy.8 = f32[256,64]{0,1:T(8,128)} copy(f32[256,64]{1,0:T(8,128)S(1)} %reshape.7) | data formatting | bytes 131072 | tf_op jit(solution)/shard_map/reshape | solution.py:415
  (3 shorter events, 0.0 us)
Async XLA Ops:
  0.0 0.9 %copy-start = (f32[64,640]{1,0:T(8,128)S(1)}, f32[64,640]{1,0:T(8,128)}, u32[]{:S(2)}) copy-start(f32[64,640]{1,0:T(8,128)} %raw_ref.1) | copy-start | bytes 491524
  0.9 0.7 %copy-start.1 = (f32[64,16]{0,1:T(8,128)S(1)}, f32[64,16]{0,1:T(8,128)}, u32[]{:S(2)}) copy-start(f32[64,16]{0,1:T(8,128)} %param.7) | copy-start | bytes 12292
  2.8 10.3 %collective-permute-start.3 = (bf16[64,768]{1,0:T(8,128)(2,1)S(1)}, bf16[64,768]{1,0:T(8,128)(2,1)S(1)}, u32[]{:S(2)}, u32[]{:S(2)}) collective-permute-start(bf16[64,768]{1,0:T(8,128)(2,1)S(1)} %shard_map.64.refs_0_), channel_id=1, source_target_pairs={{16,0},{0,16},{48,32},{32,48},{80,64},{64,80},{112,96},{96,112},{1... | collective-permute-start | bytes 294920 | tf_op jit(solution)/shard_map/ppermute | solution.py:341
  2.9 8.7 %collective-permute-start.2 = (bf16[64,768]{1,0:T(8,128)(2,1)S(1)}, bf16[64,768]{1,0:T(8,128)(2,1)S(1)}, u32[]{:S(2)}, u32[]{:S(2)}) collective-permute-start(bf16[64,768]{1,0:T(8,128)(2,1)S(1)} %shard_map.64.refs_0_), channel_id=1, source_target_pairs={{96,0},{112,16},{0,32},{16,48},{32,64},{48,80},{64,96},{80,112},{9... | collective-permute-start | bytes 294920 | tf_op jit(solution)/shard_map/ppermute | solution.py:340
  4.5 8.0 %collective-permute-start.1 = (bf16[64,768]{1,0:T(8,128)(2,1)S(1)}, bf16[64,768]{1,0:T(8,128)(2,1)S(1)}, u32[]{:S(2)}, u32[]{:S(2)}) collective-permute-start(bf16[64,768]{1,0:T(8,128)(2,1)S(1)} %shard_map.64.refs_0_), channel_id=1, source_target_pairs={{64,0},{80,16},{96,32},{112,48},{0,64},{16,80},{32,96},{48,112},{6... | collective-permute-start | bytes 294920 | tf_op jit(solution)/shard_map/ppermute | solution.py:340
  7.2 5.2 %collective-permute-start = (bf16[64,768]{1,0:T(8,128)(2,1)S(1)}, bf16[64,768]{1,0:T(8,128)(2,1)S(1)}, u32[]{:S(2)}, u32[]{:S(2)}) collective-permute-start(bf16[64,768]{1,0:T(8,128)(2,1)S(1)} %shard_map.64.refs_0_), channel_id=1, source_target_pairs={{32,0},{48,16},{64,32},{80,48},{96,64},{112,80},{0,96},{16,112},{3... | collective-permute-start | bytes 294920 | tf_op jit(solution)/shard_map/ppermute | solution.py:340
  8.7 0.8 %copy-start.3 = (bf16[64,512]{1,0:T(8,128)(2,1)S(1)}, bf16[64,512]{1,0:T(8,128)(2,1)}, u32[]{:S(2)}) copy-start(bf16[64,512]{1,0:T(8,128)(2,1)} %refs_8_.1) | copy-start | bytes 196612
  9.5 0.7 copy-start.6
  10.2 3.8 %copy-start.2 = (f32[64,16]{0,1:T(8,128)S(1)}, f32[64,16]{0,1:T(8,128)}, u32[]{:S(2)}) copy-start(f32[64,16]{0,1:T(8,128)} %param.7) | copy-start | bytes 12292
  10.2 3.8 %copy-start.4 = (bf16[64,512]{1,0:T(8,128)(2,1)S(1)}, bf16[64,512]{1,0:T(8,128)(2,1)}, u32[]{:S(2)}) copy-start(bf16[64,512]{1,0:T(8,128)(2,1)} %refs_8_.1) | copy-start | bytes 196612
  10.2 3.8 %copy-start.5 = (s32[64,64]{1,0:T(8,128)S(1)}, s32[64,64]{1,0:T(8,128)}, u32[]{:S(2)}) copy-start(s32[64,64]{1,0:T(8,128)} %refs_9_.1) | copy-start | bytes 49156
  10.2 3.8 %copy-start.7 = (s32[64]{0:T(128)S(1)}, s32[64]{0:T(128)}, u32[]{:S(2)}) copy-start(s32[64]{0:T(128)} %moveouts_ref.1) | copy-start | bytes 772
  11.6 1.5 %collective-permute-start.6 = (bf16[64,768]{1,0:T(8,128)(2,1)S(1)}, bf16[64,768]{1,0:T(8,128)(2,1)S(1)}, u32[]{:S(2)}, u32[]{:S(2)}) collective-permute-start(bf16[64,768]{1,0:T(8,128)(2,1)S(1)} %collective-permute-done.2.refs_3_), channel_id=1, source_target_pairs={{16,0},{0,16},{48,32},{32,48},{80,64},{64,80},{112,96},{96,112},{1... | collective-permute-start | bytes 294920 | tf_op jit(solution)/shard_map/ppermute | solution.py:341
  12.5 1.3 %collective-permute-start.5 = (bf16[64,768]{1,0:T(8,128)(2,1)S(1)}, bf16[64,768]{1,0:T(8,128)(2,1)S(1)}, u32[]{:S(2)}, u32[]{:S(2)}) collective-permute-start(bf16[64,768]{1,0:T(8,128)(2,1)S(1)} %collective-permute-done.1.refs_2_), channel_id=1, source_target_pairs={{16,0},{0,16},{48,32},{32,48},{80,64},{64,80},{112,96},{96,112},{1... | collective-permute-start | bytes 294920 | tf_op jit(solution)/shard_map/ppermute | solution.py:341
  12.5 1.5 %collective-permute-start.4 = (bf16[64,768]{1,0:T(8,128)(2,1)S(1)}, bf16[64,768]{1,0:T(8,128)(2,1)S(1)}, u32[]{:S(2)}, u32[]{:S(2)}) collective-permute-start(bf16[64,768]{1,0:T(8,128)(2,1)S(1)} %collective-permute-done.refs_1_), channel_id=1, source_target_pairs={{16,0},{0,16},{48,32},{32,48},{80,64},{64,80},{112,96},{96,112},{1... | collective-permute-start | bytes 294920 | tf_op jit(solution)/shard_map/ppermute | solution.py:341
  44.4 5.8 %collective-permute-start.7 = (bf16[128,512]{1,0:T(8,128)(2,1)S(1)}, bf16[128,512]{1,0:T(8,128)(2,1)S(1)}, u32[]{:S(2)}, u32[]{:S(2)}) collective-permute-start(bf16[128,512]{1,0:T(8,128)(2,1)S(1)} %get-tuple-element.14), channel_id=1, source_target_pairs={{0,1},{1,0},{2,3},{3,2},{4,5},{5,4},{6,7},{7,6},{8,9},{9,8},{10,11... | collective-permute-start | bytes 393224 | tf_op jit(solution)/shard_map/ppermute | solution.py:346
  46.1 8.0 %collective-permute-start.8 = (bf16[128,512]{1,0:T(8,128)(2,1)S(1)}, bf16[128,512]{1,0:T(8,128)(2,1)S(1)}, u32[]{:S(2)}, u32[]{:S(2)}) collective-permute-start(bf16[128,512]{1,0:T(8,128)(2,1)S(1)} %get-tuple-element.15), channel_id=1, source_target_pairs={{0,3},{1,2},{2,1},{3,0},{4,7},{5,6},{6,5},{7,4},{8,11},{9,10},{10,... | collective-permute-start | bytes 393224 | tf_op jit(solution)/shard_map/ppermute | solution.py:346
  48.3 7.3 %collective-permute-start.9 = (bf16[128,512]{1,0:T(8,128)(2,1)S(1)}, bf16[128,512]{1,0:T(8,128)(2,1)S(1)}, u32[]{:S(2)}, u32[]{:S(2)}) collective-permute-start(bf16[128,512]{1,0:T(8,128)(2,1)S(1)} %get-tuple-element.16), channel_id=1, source_target_pairs={{0,2},{1,3},{2,0},{3,1},{4,6},{5,7},{6,4},{7,5},{8,10},{9,11},{10,... | collective-permute-start | bytes 393224 | tf_op jit(solution)/shard_map/ppermute | solution.py:346
  55.7 5.9 %collective-permute-start.10 = (bf16[32,512]{1,0:T(8,128)(2,1)S(1)}, bf16[32,512]{1,0:T(8,128)(2,1)S(1)}, u32[]{:S(2)}, u32[]{:S(2)}) collective-permute-start(bf16[32,512]{1,0:T(8,128)(2,1)S(1)} %get-tuple-element.19), channel_id=1, source_target_pairs={{0,8},{1,9},{2,10},{3,11},{4,12},{5,13},{6,14},{7,15},{8,0},{9,1},... | collective-permute-start | bytes 98312 | tf_op jit(solution)/shard_map/ppermute | solution.py:346
  59.7 5.1 %collective-permute-start.12 = (bf16[32,512]{1,0:T(8,128)(2,1)S(1)}, bf16[32,512]{1,0:T(8,128)(2,1)S(1)}, u32[]{:S(2)}, u32[]{:S(2)}) collective-permute-start(bf16[32,512]{1,0:T(8,128)(2,1)S(1)} %get-tuple-element.20), channel_id=1, source_target_pairs={{0,12},{1,13},{2,14},{3,15},{4,8},{5,9},{6,10},{7,11},{8,4},{9,5},... | collective-permute-start | bytes 98312 | tf_op jit(solution)/shard_map/ppermute | solution.py:346
  60.4 4.4 %collective-permute-start.11 = (bf16[32,512]{1,0:T(8,128)(2,1)S(1)}, bf16[32,512]{1,0:T(8,128)(2,1)S(1)}, u32[]{:S(2)}, u32[]{:S(2)}) collective-permute-start(bf16[32,512]{1,0:T(8,128)(2,1)S(1)} %get-tuple-element.21), channel_id=1, source_target_pairs={{0,4},{1,5},{2,6},{3,7},{4,0},{5,1},{6,2},{7,3},{8,12},{9,13},{10,... | collective-permute-start | bytes 98312 | tf_op jit(solution)/shard_map/ppermute | solution.py:346
